TPU v7x, 128 devices: a whole 4x4x4 slice. The times are simulated.
128 devices in a mesh: cache: 32 (over x, y, core), tp: 4 (over z).
Axes of the slice: x: 4, y: 4, z: 4, core: 2. Of those that a mesh axis runs over, the one named last changes fastest.
Arguments:
- queries: bfloat16 [65536, 2048], P('cache', 'tp'), may hold values from -6 to 6
- key_vecs: bfloat16 [65536, 2048], P('cache', 'tp'), may hold values from -6 to 6
- values: bfloat16 [65536, 2048], P('cache', 'tp'), may hold values from -6 to 6
- log_decay: bfloat16 [65536, 2048], P('cache', 'tp'), may hold values from -2 to 0
- write_strength: float32 [65536, 16], P('cache', 'tp'), may hold values from 0.2 to 0.9
- inverses: float32 [1024, 64, 1024], P('cache', None, 'tp'), may hold values from -1 to 1
- suffix_stretches: int32 [512], P('cache'), may hold values from 1 to 2, 768 in all
- ckpt_store: float32 [64, 16, 128, 128], P('cache', 'tp'), may hold values from -4 to 4
- hit_owner: int32 [512], P('cache'), may hold values from 0 to 31, as said below
- hit_slot: int32 [512], P('cache'), may hold values from 0 to 1
- ret_owner: int32 [512], P('cache'), may hold values from 0 to 31, as said below
- out_gate: bfloat16 [65536, 2048], P('cache', 'tp'), may hold values from -6 to 6
- norm_gain: float32 [128], replicated, may hold values from 0.1 to 1.9
- out_weight: bfloat16 [2048, 2304], P('tp'), may hold values from -0.125 to 0.125
Outputs:
- mixed: bfloat16 [65536, 2304], P(('cache', 'tp'))
- new_ckpts: float32 [512, 16, 128, 128], P('cache', 'tp')
Inputs may be any that keep to these rules, and one draw needn't show every extreme that they name: `hit_owner`: within each index of cache's block of 16 requests, no owner is named more than 1 times, and in every block some owner is named exactly 1 times; for each position r within the blocks, every owner is named at position r by exactly one block. `ret_owner`: within each index of cache's block of 16 requests, no owner is named more than 1 times, and in every block some owner is named exactly 1 times; for each position r within the blocks, every owner is named at position r by exactly one block.
All inputs are finite; a program needn't handle non-finite values. No bound on the sum of `suffix_stretches` on one device may be relied on, other than what follows from the above.
Results may differ from a plain program's by a relative error of at most 0.018.
Values may be sent and summed in bfloat16 or wider, within the bound.
No kernel may reach another device: no remote copies, remote signals or barrier semaphores. Data moves between devices by JAX's collectives and lax.ppermute only.
A program may use at most 192 MiB of HBM per device.

v0:
```python
import jax
import jax.numpy as jnp
from jax import lax
from jax.experimental import pallas as pl
from jax.experimental.pallas import tpu as pltpu
from jax.sharding import PartitionSpec as P

DK = 128
DV = 128
CH = 64
MAXCH = 2
R_DEV = 16
HEADS = 4
PAIRS = HEADS // 2
CACHE = 32
N_TP = 4
D = 2304
HALF = D // 2
WIDTH = HEADS * DK
ROWS = MAXCH * CH
TAG_ROWS = 16
QUARTER_SHIFTS = (2, 1, 3, 0)

f32 = jnp.float32
bf16 = jnp.bfloat16


def block_diagonal(left, right):
    zeros = jnp.zeros_like(left)
    return jnp.concatenate(
        [jnp.concatenate([left, zeros], axis=1), jnp.concatenate([zeros, right], axis=1)],
        axis=0,
    )


def pair_diagonal(pair):
    return block_diagonal(pair[:, :DK], pair[:, DK:])


def side_by_side(left, right):
    return jnp.concatenate([left, right], axis=1)


def prepare_kernel(
    counts_ref, q_ref, k_ref, v_ref, g_ref, b_ref, m_ref, wq_ref, u_ref, lk_ref, d_ref
):
    lower = lax.broadcasted_iota(jnp.int32, (CH, CH), 0) >= lax.broadcasted_iota(
        jnp.int32, (CH, CH), 1
    )
    summing = jnp.where(lower, 1.0, 0.0).astype(bf16)
    row = lax.broadcasted_iota(jnp.int32, (CH, 2 * CH), 0)
    column = lax.broadcasted_iota(jnp.int32, (CH, 2 * CH), 1)
    causal = row >= lax.rem(column, CH)
    decays = []
    for c in range(MAXCH):
        rows = pl.ds(c * CH, CH)
        cumulative = jnp.dot(summing, g_ref[rows, :], preferred_element_type=f32)
        for p in range(PAIRS):
            query_fwd, key_fwd, key_back, key_end, strong_values = [], [], [], [], []
            for h in (2 * p, 2 * p + 1):
                lanes = pl.ds(h * DK, DK)
                q = q_ref[rows, lanes].astype(f32)
                k = k_ref[rows, lanes].astype(f32)
                v = v_ref[rows, lanes].astype(f32)
                strength = b_ref[rows, h : h + 1]
                cum = cumulative[:, h * DK : (h + 1) * DK]
                last = cum[CH - 1 : CH, :]
                forward = jnp.exp(cum)
                q_unit = q * lax.rsqrt(jnp.sum(q * q, axis=1, keepdims=True) + 1e-06)
                k_unit = k * lax.rsqrt(jnp.sum(k * k, axis=1, keepdims=True) + 1e-06)
                query_fwd.append((q_unit * forward).astype(bf16))
                key_fwd.append((strength * (k_unit * forward)).astype(bf16))
                key_back.append((k_unit * jnp.exp(-cum)).astype(bf16))
                key_end.append(k_unit * jnp.exp(last - cum))
                strong_values.append((strength * v).astype(bf16))
                decays.append(jnp.exp(last))
            wide = pl.ds(p * 2 * DK, 2 * DK)
            narrow = pl.ds(p * 2 * CH, 2 * CH)
            inverse = m_ref[c, :, narrow].astype(bf16)
            w = jnp.dot(inverse, block_diagonal(*key_fwd), preferred_element_type=f32)
            u = jnp.dot(inverse, block_diagonal(*strong_values), preferred_element_type=f32)
            queries = side_by_side(*query_fwd)
            scores = lax.dot_general(
                queries,
                block_diagonal(*key_back),
                (((1,), (1,)), ((), ())),
                preferred_element_type=f32,
            )
            wq_ref[0, c, pl.ds(0, CH), wide] = w.astype(bf16)
            wq_ref[0, c, pl.ds(CH, CH), wide] = queries
            u_ref[0, c, :, wide] = u.astype(bf16)
            lk_ref[0, c, pl.ds(0, CH), narrow] = jnp.where(causal, scores, 0.0).astype(bf16)
            lk_ref[0, c, pl.ds(CH, DK), narrow] = jnp.concatenate(key_end, axis=0).T.astype(bf16)
    d_ref[0] = jnp.concatenate(decays, axis=0).T


def advance_kernel(
    order_ref,
    hit_ref,
    ret_ref,
    counts_ref,
    s_ref,
    wq_ref,
    u_ref,
    lk_ref,
    d_ref,
    gate_ref,
    gain_ref,
    far_ref,
    next_ref,
    back_ref,
    own_ref,
    send_ref,
    gated_ref,
):
    step = pl.program_id(0)
    live = counts_ref[order_ref[step]] > 1
    gain = gain_ref[...]

    def put_gated(c, p, out):
        for side in range(2):
            h = 2 * p + side
            rows, lanes = pl.ds(c * CH, CH), pl.ds(h * DV, DV)
            head_out = out[:, side * DV : (side + 1) * DV]
            mean_square = jnp.mean(head_out * head_out, axis=1, keepdims=True)
            normed = head_out * lax.rsqrt(mean_square + 1e-05) * gain
            gate = gate_ref[rows, lanes].astype(f32)
            gated_ref[rows, lanes] = (normed * jax.nn.sigmoid(gate)).astype(bf16)

    def stretch(c, p, state_pair, diagonal):
        wide = pl.ds(p * 2 * DK, 2 * DK)
        narrow = pl.ds(p * 2 * CH, 2 * CH)
        read = jnp.dot(wq_ref[0, c, :, wide], diagonal, preferred_element_type=f32)
        new_values = (u_ref[0, c, :, wide].astype(f32) - read[:CH]).astype(bf16)
        written = jnp.dot(
            lk_ref[0, c, :, narrow], pair_diagonal(new_values), preferred_element_type=f32
        )
        out = read[CH:] + written[:CH]
        states = []
        for side in range(2):
            at = c * HEADS + 2 * p + side
            decay = d_ref[0, :, at : at + 1]
            states.append(decay * state_pair[side] + written[CH:, side * DV : (side + 1) * DV])
        return out, states

    finals = []
    for p in range(PAIRS):
        left, right = s_ref[0, pl.ds(2 * p * DK, DK), :], s_ref[0, pl.ds((2 * p + 1) * DK, DK), :]
        out, states = stretch(
            0, p, (left.astype(f32), right.astype(f32)), block_diagonal(left, right)
        )
        put_gated(0, p, out)
        finals.append(states)

    @pl.when(live)
    def _():
        for p in range(PAIRS):
            states = finals[p]
            diagonal = block_diagonal(*[s.astype(bf16) for s in states])
            out, states = stretch(1, p, states, diagonal)
            put_gated(1, p, out)
            for side in range(2):
                send_ref[0, pl.ds((2 * p + side) * DK, DK), :] = states[side].astype(bf16)

    @pl.when(jnp.logical_not(live))
    def _():
        for p in range(PAIRS):
            for side in range(2):
                send_ref[0, pl.ds((2 * p + side) * DK, DK), :] = finals[p][side].astype(bf16)
        gated_ref[pl.ds(CH, CH), :] = jnp.zeros((CH, WIDTH), bf16)

    quarter = step // (R_DEV // N_TP)
    for index, out_ref in enumerate((far_ref, next_ref, back_ref, own_ref)):

        @pl.when(quarter == index)
        def _(out_ref=out_ref):
            out_ref[...] = gated_ref[...]


def project_kernel(core_ref, *refs):
    gated, own_ref, direct, swapped = refs[:4], refs[4], refs[5:8], refs[8:11]
    out_ref = refs[11]

    def total(others):
        acc = jnp.dot(gated[3][...], own_ref[...], preferred_element_type=f32)
        for rows_ref, weight_ref in zip(gated[:3], others):
            acc = acc + jnp.dot(rows_ref[...], weight_ref[...], preferred_element_type=f32)
        return acc.astype(bf16)

    @pl.when(pl.program_id(0) == 0)
    def _():
        out_ref[...] = total(direct)

    @pl.when(pl.program_id(0) == 1)
    def _():
        out_ref[...] = total(swapped)


def unpack_kernel(source_ref, in_ref, out_ref):
    out_ref[...] = in_ref[...].astype(f32)


def prepare(counts, queries, key_vecs, values, log_decay, write_strength, inverses):
    token_rows = pl.BlockSpec((ROWS, WIDTH), lambda i, n: (i, 0))
    return pl.pallas_call(
        prepare_kernel,
        grid_spec=pltpu.PrefetchScalarGridSpec(
            num_scalar_prefetch=1,
            grid=(R_DEV,),
            in_specs=[token_rows] * 4
            + [
                pl.BlockSpec((ROWS, HEADS), lambda i, n: (i, 0)),
                pl.BlockSpec((MAXCH, CH, HEADS * CH), lambda i, n: (i, 0, 0)),
            ],
            out_specs=[
                pl.BlockSpec((1, MAXCH, 2 * CH, WIDTH), lambda i, n: (i, 0, 0, 0)),
                pl.BlockSpec((1, MAXCH, CH, WIDTH), lambda i, n: (i, 0, 0, 0)),
                pl.BlockSpec((1, MAXCH, CH + DK, HEADS * CH), lambda i, n: (i, 0, 0, 0)),
                pl.BlockSpec((1, DK, MAXCH * HEADS), lambda i, n: (i, 0, 0)),
            ],
        ),
        out_shape=[
            jax.ShapeDtypeStruct((R_DEV, MAXCH, 2 * CH, WIDTH), bf16),
            jax.ShapeDtypeStruct((R_DEV, MAXCH, CH, WIDTH), bf16),
            jax.ShapeDtypeStruct((R_DEV, MAXCH, CH + DK, HEADS * CH), bf16),
            jax.ShapeDtypeStruct((R_DEV, DK, MAXCH * HEADS), f32),
        ],
        compiler_params=pltpu.CompilerParams(vmem_limit_bytes=24 << 20),
        cost_estimate=pl.CostEstimate(
            flops=800_000_000, bytes_accessed=20_000_000, transcendentals=3_000_000
        ),
        name="prepare",
    )(counts, queries, key_vecs, values, log_decay, write_strength, inverses)


def advance(order, hit_rows, ret_owner, counts, stored, wq, u, lk, d, out_gate, gain):
    per = R_DEV // N_TP

    def quarter_rows(index):
        return pl.BlockSpec(
            (ROWS, WIDTH),
            lambda i, o, s, r, n: (jnp.clip(i - per * index, 0, per - 1), 0),
        )

    return pl.pallas_call(
        advance_kernel,
        grid_spec=pltpu.PrefetchScalarGridSpec(
            num_scalar_prefetch=4,
            grid=(R_DEV,),
            in_specs=[
                pl.BlockSpec((1, HEADS * DK, DV), lambda i, o, s, r, n: (s[o[i]], 0, 0)),
                pl.BlockSpec((1, MAXCH, 2 * CH, WIDTH), lambda i, o, s, r, n: (o[i], 0, 0, 0)),
                pl.BlockSpec((1, MAXCH, CH, WIDTH), lambda i, o, s, r, n: (o[i], 0, 0, 0)),
                pl.BlockSpec(
                    (1, MAXCH, CH + DK, HEADS * CH), lambda i, o, s, r, n: (o[i], 0, 0, 0)
                ),
                pl.BlockSpec((1, DK, MAXCH * HEADS), lambda i, o, s, r, n: (o[i], 0, 0)),
                pl.BlockSpec((ROWS, WIDTH), lambda i, o, s, r, n: (o[i], 0)),
                pl.BlockSpec((1, DV), lambda i, o, s, r, n: (0, 0)),
            ],
            out_specs=[quarter_rows(index) for index in range(N_TP)]
            + [pl.BlockSpec((1, HEADS * DK, DV), lambda i, o, s, r, n: (r[o[i]], 0, 0))],
            scratch_shapes=[pltpu.VMEM((ROWS, WIDTH), bf16)],
        ),
        out_shape=[jax.ShapeDtypeStruct((per * ROWS, WIDTH), bf16)] * N_TP
        + [jax.ShapeDtypeStruct((CACHE, HEADS * DK, DV), bf16)],
        compiler_params=pltpu.CompilerParams(vmem_limit_bytes=24 << 20),
        cost_estimate=pl.CostEstimate(
            flops=1_000_000_000, bytes_accessed=18_000_000, transcendentals=2_000_000
        ),
        name="advance",
    )(order, hit_rows, ret_owner, counts, stored, wq, u, lk, d, out_gate, gain)


def project(core, gated, own_weight, direct, swapped):
    tiles = 3
    tile = HALF // tiles
    rows = gated[0].shape[0]
    whole = pl.BlockSpec((rows, WIDTH), lambda j, t, c: (0, 0))
    chosen = lambda j, c: jnp.where(j == 0, c[0], 1 - c[0])
    return pl.pallas_call(
        project_kernel,
        grid_spec=pltpu.PrefetchScalarGridSpec(
            num_scalar_prefetch=1,
            grid=(2, tiles),
            in_specs=[whole] * 4
            + [pl.BlockSpec((WIDTH, tile), lambda j, t, c: (0, chosen(j, c) * tiles + t))]
            + [pl.BlockSpec((WIDTH, tile), lambda j, t, c: (0, jnp.where(j == 0, t, tiles - 1)))]
            * 3
            + [pl.BlockSpec((WIDTH, tile), lambda j, t, c: (0, jnp.where(j == 0, 0, t)))] * 3,
            out_specs=pl.BlockSpec((rows, tile), lambda j, t, c: (0, chosen(j, c) * tiles + t)),
        ),
        out_shape=jax.ShapeDtypeStruct((rows, D), bf16),
        compiler_params=pltpu.CompilerParams(vmem_limit_bytes=24 << 20),
        cost_estimate=pl.CostEstimate(
            flops=4_800_000_000, bytes_accessed=14_000_000, transcendentals=0
        ),
        name="project",
    )(core, *gated, own_weight, *direct, *swapped)


def unpack(source, received):
    return pl.pallas_call(
        unpack_kernel,
        grid_spec=pltpu.PrefetchScalarGridSpec(
            num_scalar_prefetch=1,
            grid=(R_DEV,),
            in_specs=[pl.BlockSpec((1, HEADS * DK, DV), lambda i, s: (s[i], 0, 0))],
            out_specs=pl.BlockSpec((1, HEADS * DK, DV), lambda i, s: (i, 0, 0)),
        ),
        out_shape=jax.ShapeDtypeStruct((R_DEV, HEADS * DK, DV), f32),
        compiler_params=pltpu.CompilerParams(vmem_limit_bytes=16 << 20),
        cost_estimate=pl.CostEstimate(flops=0, bytes_accessed=6_300_000, transcendentals=0),
        name="unpack",
    )(source, received)


def along_tp(x, shift):
    return lax.ppermute(x, "tp", [(z, (z + shift) % N_TP) for z in range(N_TP)])


def to_sibling(x):
    return lax.ppermute(x, "cache", [(i, i ^ 1) for i in range(CACHE)])


def body(
    queries,
    key_vecs,
    values,
    log_decay,
    write_strength,
    inverses,
    suffix_stretches,
    ckpt_store,
    hit_owner,
    hit_slot,
    ret_owner,
    out_gate,
    norm_gain,
    out_weight,
):
    self_index = lax.axis_index("cache")
    z = lax.axis_index("tp")
    core = lax.rem(self_index, 2)
    stored_here = ckpt_store.shape[0]

    tags = jnp.zeros((stored_here, TAG_ROWS, DV), bf16)
    tags = tags.at[:, 0, :R_DEV].set(ret_owner.astype(bf16)[None])
    stored = jnp.concatenate(
        [ckpt_store.astype(bf16).reshape(stored_here, HEADS * DK, DV), tags], axis=1
    )
    stored = lax.all_gather(stored, "cache", axis=0, tiled=True)

    half_weight = lax.dynamic_slice(out_weight, (0, core * HALF), (WIDTH, HALF))
    shifts = QUARTER_SHIFTS[:3]
    direct = [along_tp(half_weight, shift) for shift in shifts]

    wq, u, lk, d = prepare(
        suffix_stretches, queries, key_vecs, values, log_decay, write_strength, inverses
    )

    place = jnp.arange(R_DEV, dtype=jnp.int32)
    per = R_DEV // N_TP
    turn = jnp.repeat(jnp.asarray(QUARTER_SHIFTS, jnp.int32), per)
    order = lax.rem(z + turn, N_TP) * per + lax.rem(place, per)
    hit_rows = hit_owner * stored_here + hit_slot
    *gated, sending = advance(
        order,
        hit_rows,
        ret_owner,
        suffix_stretches,
        stored,
        wq,
        u,
        lk,
        d,
        out_gate,
        norm_gain.reshape(1, DV),
    )
    received = lax.all_to_all(sending, "cache", split_axis=0, concat_axis=0, tiled=True)

    others = [along_tp(rows, shift) for rows, shift in zip(gated[:3], shifts)]
    swapped = [to_sibling(weight) for weight in direct]
    mixed = project(core.reshape(1), others + [gated[3]], out_weight, direct, swapped)

    owners = stored[::stored_here, HEADS * DK, :R_DEV].astype(jnp.int32)
    source = jnp.sum(
        jnp.where(owners == self_index, jnp.arange(CACHE, dtype=jnp.int32)[:, None], 0), axis=0
    )
    new_ckpts = unpack(source, received).reshape(R_DEV, HEADS, DK, DV)
    return (mixed, new_ckpts)


def solution(mesh):
    placed = (
        P("cache", "tp"),
        P("cache", "tp"),
        P("cache", "tp"),
        P("cache", "tp"),
        P("cache", "tp"),
        P("cache", None, "tp"),
        P("cache"),
        P("cache", "tp", None, None),
        P("cache"),
        P("cache"),
        P("cache"),
        P("cache", "tp"),
        P(),
        P("tp", None),
    )
    return jax.shard_map(
        body,
        mesh=mesh,
        in_specs=placed,
        out_specs=(P(("cache", "tp"), None), P("cache", "tp", None, None)),
        check_vma=False,
    )
```

profile of v0, /device:TPU:1, one launch (start us, length us, event | category | flops | bytes accessed | tf_op | source)
XLA Modules:
  0.0 214.4 jit_solution(1496995427940382142)
XLA Ops:
  13.3 1.6 copy-done.10
  14.9 1.6 copy-done.11
  16.5 1.6 copy-done.12
  19.7 11.3 %prepare.1 = (bf16[16,2,128,512]{3,2,1,0:T(8,128)(2,1)S(1)}, bf16[16,2,64,512]{3,2,1,0:T(8,128)(2,1)S(1)}, bf16[16,2,192,256]{3,2,1,0:T(8,128)(2,1)S(1)}, f32[16,128,8]{2,1,0:T(8,128)S(1)}) custom-call(s32[16]{0:T(128)S(1)} %copy-done.17, bf16[2048,512]{1,0:T(8,128)(2,1)S(1)} %copy-done.9, bf16[2048,512]{1,0:T(8,128)(2,1)S(1)} %copy-done.10, ...), custom_call_target="tpu_custom_call" | custom-call | flops 800000000 | bytes 20000000 | tf_op jit(solution)/shard_map/prepare/pallas_call | solution.py:205
  31.0 2.0 copy-done.1
  33.0 1.6 copy-done.4
  37.0 30.4 %all-gather.2.cloned.1.call-done.s_ref = bf16[64,528,128]{2,1,0:T(8,128)(2,1)} async-done(((bf16[2,528,128]{2,1,0:T(8,128)(2,1)}), bf16[64,528,128]{2,1,0:T(8,128)(2,1)}) %all-gather.2.cloned.1.call-update) | async-done | bytes 8650768 | tf_op jit(solution)/shard_map/all_gather | solution.py:352
  67.4 3.5 %copy-done = bf16[64,528,128]{2,1,0:T(8,128)(2,1)S(1)} copy-done((bf16[64,528,128]{2,1,0:T(8,128)(2,1)S(1)}, bf16[64,528,128]{2,1,0:T(8,128)(2,1)}, u32[]{:S(2)}) %copy-start) | copy-done | bytes 8650776
  70.8 2.2 %copy-done.2 = bf16[16,2,128,512]{3,2,1,0:T(8,128)(2,1)S(1)} copy-done((bf16[16,2,128,512]{3,2,1,0:T(8,128)(2,1)S(1)}, bf16[16,2,128,512]{3,2,1,0:T(8,128)(2,1)}, u32[]{:S(2)}) %copy-start.2) | copy-done | bytes 4194328
  73.0 1.9 copy-done.5
  74.9 1.6 copy-done.8
  77.7 13.5 %advance.1 = (bf16[512,512]{1,0:T(8,128)(2,1)S(1)}, bf16[512,512]{1,0:T(8,128)(2,1)S(1)}, bf16[512,512]{1,0:T(8,128)(2,1)S(1)}, bf16[512,512]{1,0:T(8,128)(2,1)S(1)}, bf16[32,512,128]{2,1,0:T(8,128)(2,1)S(1)}) custom-call(s32[16]{0:T(128)S(1)} %get-tuple-element.32.order_ref, s32[16]{0:T(128)S(1)} %get-tuple-element.33.hit_ref, s32[16]{0:T(128)S(1)} %copy-done.18, ...), custom_call_target="tpu_custom_call" | custom-call | flops 1000000000 | bytes 18000000 | tf_op jit(solution)/shard_map/advance/pallas_call | solution.py:245
  91.2 2.0 copy-done.3
  96.4 4.8 %all-to-all-start = ((bf16[32,512,128]{2,1,0:T(8,128)(2,1)}), bf16[32,512,128]{2,1,0:T(8,128)(2,1)}, u32[]{:S(2)}, u32[]{:S(2)}) async-start(bf16[32,512,128]{2,1,0:T(8,128)(2,1)} %copy-done.3), calls=%async_computation | async-start | bytes 8388608 | tf_op jit(solution)/shard_map/all_to_all | solution.py:380
  101.4 2.9 %collective-permute-start.3 = (bf16[512,1152]{1,0:T(8,128)(2,1)S(1)}, bf16[512,1152]{1,0:T(8,128)(2,1)S(1)}, u32[]{:S(2)}, u32[]{:S(2)}) collective-permute-start(bf16[512,1152]{1,0:T(8,128)(2,1)S(1)} %constant_dynamic-slice_fusion), channel_id=1, source_target_pairs={{0,2},{1,3},{2,0},{3,1},{4,6},{5,7},{6,4},{7,5},{8,10},{9,11},{10,... | collective-permute-start | bytes 3538952 | tf_op jit(solution)/shard_map/ppermute | solution.py:319
  104.7 2.3 %collective-permute-start.5 = (bf16[512,1152]{1,0:T(8,128)(2,1)S(1)}, bf16[512,1152]{1,0:T(8,128)(2,1)}, u32[]{:S(2)}, u32[]{:S(2)}) collective-permute-start(bf16[512,1152]{1,0:T(8,128)(2,1)S(1)} %constant_dynamic-slice_fusion), channel_id=1, source_target_pairs={{0,3},{1,0},{2,1},{3,2},{4,7},{5,4},{6,5},{7,6},{8,11},{9,8},{10,9... | collective-permute-start | bytes 3538952 | tf_op jit(solution)/shard_map/ppermute | solution.py:319
  107.0 23.4 %collective-permute-done.3.refs_5_ = bf16[512,1152]{1,0:T(8,128)(2,1)S(1)} collective-permute-done((bf16[512,1152]{1,0:T(8,128)(2,1)S(1)}, bf16[512,1152]{1,0:T(8,128)(2,1)S(1)}, u32[]{:S(2)}, u32[]{:S(2)}) %collective-permute-start.3) | collective-permute-done | bytes 1179680 | tf_op jit(solution)/shard_map/ppermute | solution.py:319
  130.4 1.8 collective-permute-start.6
  132.1 24.1 %collective-permute-done.4.refs_6_ = bf16[512,1152]{1,0:T(8,128)(2,1)} collective-permute-done((bf16[512,1152]{1,0:T(8,128)(2,1)S(1)}, bf16[512,1152]{1,0:T(8,128)(2,1)}, u32[]{:S(2)}, u32[]{:S(2)}) %collective-permute-start.4) | collective-permute-done | bytes 1179680 | tf_op jit(solution)/shard_map/ppermute | solution.py:319
  157.0 1.8 collective-permute-start
  164.8 7.4 %collective-permute-done.refs_0_ = bf16[512,512]{1,0:T(8,128)(2,1)} collective-permute-done((bf16[512,512]{1,0:T(8,128)(2,1)}, bf16[512,512]{1,0:T(8,128)(2,1)}, u32[]{:S(2)}, u32[]{:S(2)}) %collective-permute-start) | collective-permute-done | bytes 524320 | tf_op jit(solution)/shard_map/ppermute | solution.py:319
  172.2 11.7 %collective-permute-done.1.refs_1_ = bf16[512,512]{1,0:T(8,128)(2,1)} collective-permute-done((bf16[512,512]{1,0:T(8,128)(2,1)}, bf16[512,512]{1,0:T(8,128)(2,1)}, u32[]{:S(2)}, u32[]{:S(2)}) %collective-permute-start.1) | collective-permute-done | bytes 524320 | tf_op jit(solution)/shard_map/ppermute | solution.py:319
  186.3 11.0 %project.1 = bf16[512,2304]{1,0:T(8,128)(2,1)} custom-call(s32[1]{0:T(128)} %bitcast.core_ref, bf16[512,512]{1,0:T(8,128)(2,1)} %collective-permute-done.refs_0_, bf16[512,512]{1,0:T(8,128)(2,1)} %collective-permute-done.1.refs_1_, bf16[512,512]{1,0:T(8,128)(2,1)} %collective-permute-done.2.refs_2_, bf16[512,512]{1,0:T(8,128)(2,1)S(1)} %copy-done.23, ...), custom_call_target="tpu_custom_call" | custom-call | flops 4800000000 | bytes 14000000 | tf_op jit(solution)/shard_map/project/pallas_call | solution.py:281
  197.2 10.4 %unpack.1 = f32[16,512,128]{2,1,0:T(8,128)} custom-call(s32[16]{0:T(128)S(1)} %select_reduce_fusion.source_ref, bf16[32,512,128]{2,1,0:T(8,128)(2,1)} %all-to-all-done.in_ref), custom_call_target="tpu_custom_call" | custom-call | bytes 6300000 | tf_op jit(solution)/shard_map/unpack/pallas_call | solution.py:303
  (75 shorter events, 24.1 us)
Async XLA Ops:
  7.2 4.5 %copy-start.17 = (s32[16]{0:T(128)S(1)}, s32[16]{0:T(128)}, u32[]{:S(2)}) copy-start(s32[16]{0:T(128)} %counts_ref.3) | copy-start | bytes 196
  7.2 60.2 %all-gather.2.cloned.1.call-start = ((), (), s32[]{:S(2)}) async-start(), calls=%async_computation.1 | async-start | bytes 8921088 | tf_op jit(solution)/shard_map/all_gather | solution.py:352
  19.7 17.3 %copy-start.27 = (s32[16]{0:T(128)S(1)}, s32[16]{0:T(128)}, u32[]{:S(2)}) copy-start(s32[16]{0:T(128)} %param.26) | copy-start | bytes 196
  19.7 17.3 %copy-start.28 = (s32[16]{0:T(128)S(1)}, s32[16]{0:T(128)}, u32[]{:S(2)}) copy-start(s32[16]{0:T(128)} %param.25) | copy-start | bytes 196
  19.7 47.7 %copy-start.6 = (bf16[2048,512]{1,0:T(8,128)(2,1)S(1)}, bf16[2048,512]{1,0:T(8,128)(2,1)}, u32[]{:S(2)}) copy-start(bf16[2048,512]{1,0:T(8,128)(2,1)} %gate_ref.1) | copy-start | bytes 6291460
  19.7 47.7 %copy-start.18 = (s32[16]{0:T(128)S(1)}, s32[16]{0:T(128)}, u32[]{:S(2)}) copy-start(s32[16]{0:T(128)} %ret_ref.1) | copy-start | bytes 196
  19.7 47.7 %copy-start.19 = (f32[128]{0:T(128)S(1)}, f32[128]{0:T(128)}, u32[]{:S(2)}) copy-start(f32[128]{0:T(128)} %param.29) | copy-start | bytes 1540
  31.0 2.0 copy-start.1
  33.0 1.6 copy-start.4
  67.4 3.5 %copy-start = (bf16[64,528,128]{2,1,0:T(8,128)(2,1)S(1)}, bf16[64,528,128]{2,1,0:T(8,128)(2,1)}, u32[]{:S(2)}) copy-start(bf16[64,528,128]{2,1,0:T(8,128)(2,1)} %all-gather.2.cloned.1.call-done.s_ref) | copy-start | bytes 25952260
  70.8 2.2 %copy-start.2 = (bf16[16,2,128,512]{3,2,1,0:T(8,128)(2,1)S(1)}, bf16[16,2,128,512]{3,2,1,0:T(8,128)(2,1)}, u32[]{:S(2)}) copy-start(bf16[16,2,128,512]{3,2,1,0:T(8,128)(2,1)} %copy-done.1) | copy-start | bytes 12582916
  73.0 1.9 copy-start.5
  91.2 2.0 copy-start.3
  96.4 4.8 %copy-start.16 = (bf16[512,2304]{1,0:T(8,128)(2,1)S(1)}, bf16[512,2304]{1,0:T(8,128)(2,1)}, u32[]{:S(2)}) copy-start(bf16[512,2304]{1,0:T(8,128)(2,1)} %refs_4_.1) | copy-start | bytes 7077892
  96.4 100.8 %all-to-all-start = ((bf16[32,512,128]{2,1,0:T(8,128)(2,1)}), bf16[32,512,128]{2,1,0:T(8,128)(2,1)}, u32[]{:S(2)}, u32[]{:S(2)}) async-start(bf16[32,512,128]{2,1,0:T(8,128)(2,1)} %copy-done.3), calls=%async_computation | async-start | bytes 8388608 | tf_op jit(solution)/shard_map/all_to_all | solution.py:380
  101.4 29.0 %collective-permute-start.3 = (bf16[512,1152]{1,0:T(8,128)(2,1)S(1)}, bf16[512,1152]{1,0:T(8,128)(2,1)S(1)}, u32[]{:S(2)}, u32[]{:S(2)}) collective-permute-start(bf16[512,1152]{1,0:T(8,128)(2,1)S(1)} %constant_dynamic-slice_fusion), channel_id=1, source_target_pairs={{0,2},{1,3},{2,0},{3,1},{4,6},{5,7},{6,4},{7,5},{8,10},{9,11},{10,... | collective-permute-start | bytes 3538952 | tf_op jit(solution)/shard_map/ppermute | solution.py:319
  104.3 51.9 %collective-permute-start.4 = (bf16[512,1152]{1,0:T(8,128)(2,1)S(1)}, bf16[512,1152]{1,0:T(8,128)(2,1)}, u32[]{:S(2)}, u32[]{:S(2)}) collective-permute-start(bf16[512,1152]{1,0:T(8,128)(2,1)S(1)} %constant_dynamic-slice_fusion), channel_id=1, source_target_pairs={{0,1},{1,2},{2,3},{3,0},{4,5},{5,6},{6,7},{7,4},{8,9},{9,10},{10,1... | collective-permute-start | bytes 3538952 | tf_op jit(solution)/shard_map/ppermute | solution.py:319
  104.7 52.0 %collective-permute-start.5 = (bf16[512,1152]{1,0:T(8,128)(2,1)S(1)}, bf16[512,1152]{1,0:T(8,128)(2,1)}, u32[]{:S(2)}, u32[]{:S(2)}) collective-permute-start(bf16[512,1152]{1,0:T(8,128)(2,1)S(1)} %constant_dynamic-slice_fusion), channel_id=1, source_target_pairs={{0,3},{1,0},{2,1},{3,2},{4,7},{5,4},{6,5},{7,6},{8,11},{9,8},{10,9... | collective-permute-start | bytes 3538952 | tf_op jit(solution)/shard_map/ppermute | solution.py:319
  130.4 29.6 %collective-permute-start.6 = (bf16[512,1152]{1,0:T(8,128)(2,1)S(1)}, bf16[512,1152]{1,0:T(8,128)(2,1)S(1)}, u32[]{:S(2)}, u32[]{:S(2)}) collective-permute-start(bf16[512,1152]{1,0:T(8,128)(2,1)S(1)} %collective-permute-done.3.refs_5_), channel_id=1, source_target_pairs={{0,4},{4,0},{8,12},{12,8},{16,20},{20,16},{24,28},{28,24},{32,36},... | collective-permute-start | bytes 3538952 | tf_op jit(solution)/shard_map/ppermute | solution.py:323
  156.2 8.6 %collective-permute-start.7 = (bf16[512,1152]{1,0:T(8,128)(2,1)}, bf16[512,1152]{1,0:T(8,128)(2,1)}, u32[]{:S(2)}, u32[]{:S(2)}) collective-permute-start(bf16[512,1152]{1,0:T(8,128)(2,1)} %collective-permute-done.4.refs_6_), channel_id=1, source_target_pairs={{0,4},{4,0},{8,12},{12,8},{16,20},{20,16},{24,28},{28,24},{32,36},... | collective-permute-start | bytes 3538952 | tf_op jit(solution)/shard_map/ppermute | solution.py:323
  156.7 8.1 %collective-permute-start.8 = (bf16[512,1152]{1,0:T(8,128)(2,1)}, bf16[512,1152]{1,0:T(8,128)(2,1)}, u32[]{:S(2)}, u32[]{:S(2)}) collective-permute-start(bf16[512,1152]{1,0:T(8,128)(2,1)} %collective-permute-done.5.refs_7_), channel_id=1, source_target_pairs={{0,4},{4,0},{8,12},{12,8},{16,20},{20,16},{24,28},{28,24},{32,36},... | collective-permute-start | bytes 3538952 | tf_op jit(solution)/shard_map/ppermute | solution.py:323
  157.0 15.2 %collective-permute-start = (bf16[512,512]{1,0:T(8,128)(2,1)}, bf16[512,512]{1,0:T(8,128)(2,1)}, u32[]{:S(2)}, u32[]{:S(2)}) collective-permute-start(bf16[512,512]{1,0:T(8,128)(2,1)} %copy-done.26), channel_id=1, source_target_pairs={{0,2},{1,3},{2,0},{3,1},{4,6},{5,7},{6,4},{7,5},{8,10},{9,11},{10,... | collective-permute-start | bytes 1572872 | tf_op jit(solution)/shard_map/ppermute | solution.py:319
  158.8 25.1 %collective-permute-start.1 = (bf16[512,512]{1,0:T(8,128)(2,1)}, bf16[512,512]{1,0:T(8,128)(2,1)}, u32[]{:S(2)}, u32[]{:S(2)}) collective-permute-start(bf16[512,512]{1,0:T(8,128)(2,1)} %copy-done.25), channel_id=1, source_target_pairs={{0,1},{1,2},{2,3},{3,0},{4,5},{5,6},{6,7},{7,4},{8,9},{9,10},{10,1... | collective-permute-start | bytes 1572872 | tf_op jit(solution)/shard_map/ppermute | solution.py:319
  161.0 23.0 %collective-permute-start.2 = (bf16[512,512]{1,0:T(8,128)(2,1)}, bf16[512,512]{1,0:T(8,128)(2,1)}, u32[]{:S(2)}, u32[]{:S(2)}) collective-permute-start(bf16[512,512]{1,0:T(8,128)(2,1)} %copy-done.24), channel_id=1, source_target_pairs={{0,3},{1,0},{2,1},{3,2},{4,7},{5,4},{6,5},{7,6},{8,11},{9,8},{10,9... | collective-permute-start | bytes 1572872 | tf_op jit(solution)/shard_map/ppermute | solution.py:319
  (16 other events, 19.6 us)
Sparse Core Ops, SparseCore 0:
  10.3 57.0 all-gather.1
where the time goes:
time: 216 us; the launch traced here: 214 us
  waiting for transfers between devices  97 us (45%)
  Pallas kernels  46.1 us (21%)
  local copies, waits for them, and re-layouts  35.7 us (17%)
  starting transfers between devices  17.5 us (8%)
  between operations  14.2 us (7%)
  other arithmetic  3.92 us (2%)
    ppermute x6, waiting for transfers between devices, along_tp(): return lax.ppermute(x, 'tp', [(z, (z + shift) % N_TP) for z in range(N_TP)])  66.6 us
    unnamed x60, local copies, waits for them, and re-layouts  34.6 us
    all_gather x1, waiting for transfers between devices, body(): stored = lax.all_gather(stored, 'cache', axis=0, tiled=True)  30.4 us
    pallas_call x1, Pallas kernels, advance(): pl.pallas_call(advance_kernel, grid_spec=pltpu.PrefetchScalarGridSpec(num...  13.5 us
    pallas_call x1, Pallas kernels, prepare(): pl.pallas_call(prepare_kernel, grid_spec=pltpu.PrefetchScalarGridSpec(num...  11.3 us
    pallas_call x1, Pallas kernels, project(): pl.pallas_call(project_kernel, grid_spec=pltpu.PrefetchScalarGridSpec(num...  11 us
    pallas_call x1, Pallas kernels, unpack(): pl.pallas_call(unpack_kernel, grid_spec=pltpu.PrefetchScalarGridSpec(num_...  10.4 us
    ppermute x6, starting transfers between devices, along_tp(): return lax.ppermute(x, 'tp', [(z, (z + shift) % N_TP) for z in range(N_TP)])  10 us
  transfers between devices with their start and end apart: 11, of which 5 were waited for; matrix products, arithmetic and copies ran while one was open for 2% of the time, Pallas kernels for 10%

commit v1 on v0

v1 whole, which is shorter than its diff:
```python
import functools

import jax
import jax.numpy as jnp
from jax import lax
from jax.experimental import pallas as pl
from jax.experimental.pallas import tpu as pltpu
from jax.sharding import PartitionSpec as P

DK = 128
DV = 128
CH = 64
MAXCH = 2
R_DEV = 16
HEADS = 4
PAIRS = HEADS // 2
CACHE = 32
N_TP = 4
CHIP_SHIFTS = (2, 1, 3)
D = 2304
HALF = D // 2
PAIR = 2 * DK
ROWS = MAXCH * CH
TAG_ROWS = 16
READY = 2
GROUP = 4
UNPACKED = 4
VMEM_BYTES = 60 << 20
QUARTER_SHIFTS = (2, 1, 3, 0)

f32 = jnp.float32
bf16 = jnp.bfloat16


def block_diagonal(left, right):
    zeros = jnp.zeros_like(left)
    return jnp.concatenate(
        [jnp.concatenate([left, zeros], axis=1), jnp.concatenate([zeros, right], axis=1)],
        axis=0,
    )


def pair_diagonal(pair):
    return block_diagonal(pair[:, :DK], pair[:, DK:])


def side_by_side(left, right):
    return jnp.concatenate([left, right], axis=1)


def prepare_kernel(
    pair,
    q_ref,
    k_ref,
    v_ref,
    g_ref,
    b_ref,
    m_ref,
    gate_ref,
    gain_ref,
    wq_ref,
    u_ref,
    lk_ref,
    d_ref,
    gain_out_ref,
    decay_ref,
):
    step = pl.program_id(0)
    lower = lax.broadcasted_iota(jnp.int32, (CH, CH), 0) >= lax.broadcasted_iota(
        jnp.int32, (CH, CH), 1
    )
    summing = jnp.where(lower, 1.0, 0.0).astype(bf16)
    row = lax.broadcasted_iota(jnp.int32, (CH, 2 * CH), 0)
    column = lax.broadcasted_iota(jnp.int32, (CH, 2 * CH), 1)
    causal = row >= lax.rem(column, CH)
    first_half = column[:1] < CH
    gain = gain_ref[...]
    decays = []
    for r in range(READY):
        strengths = [
            b_ref[2 * pair + side : 2 * pair + side + 1, pl.ds(r * ROWS, ROWS)]
            for side in range(2)
        ]
        turned = [pltpu.roll(strength, CH, 1) for strength in strengths]
        for c in range(MAXCH):
            rows = pl.ds(r * ROWS + c * CH, CH)
            cumulative = jnp.dot(summing, g_ref[rows, :], preferred_element_type=f32)
            query_fwd, key_fwd, key_back, key_end, plain_values = [], [], [], [], []
            for side in range(2):
                lanes = pl.ds(side * DK, DK)
                q = q_ref[rows, lanes].astype(f32)
                k = k_ref[rows, lanes].astype(f32)
                cum = cumulative[:, side * DK : (side + 1) * DK]
                last = cum[CH - 1 : CH, :]
                forward = jnp.exp(cum)
                q_scale = lax.rsqrt(jnp.sum(q * q, axis=1, keepdims=True) + 1e-06)
                k_unit = k * lax.rsqrt(jnp.sum(k * k, axis=1, keepdims=True) + 1e-06)
                query_fwd.append((q * q_scale * forward).astype(bf16))
                key_fwd.append((k_unit * forward).astype(bf16))
                key_back.append((k_unit * jnp.exp(-cum)).astype(bf16))
                key_end.append(k_unit * jnp.exp(last - cum))
                plain_values.append(v_ref[rows, lanes])
                decays.append(jnp.exp(last))
                gate = jax.nn.sigmoid(gate_ref[rows, lanes].astype(f32))
                gain_out_ref[rows, lanes] = (gain * gate).astype(bf16)
            if c == 0:
                strength = jnp.where(first_half, strengths[0], turned[1])
            else:
                strength = jnp.where(first_half, turned[0], strengths[1])
            inverse = (m_ref[r * MAXCH + c] * strength).astype(bf16)
            w = jnp.dot(inverse, block_diagonal(*key_fwd), preferred_element_type=f32)
            u = jnp.dot(inverse, block_diagonal(*plain_values), preferred_element_type=f32)
            queries = side_by_side(*query_fwd)
            scores = lax.dot_general(
                queries,
                block_diagonal(*key_back),
                (((1,), (1,)), ((), ())),
                preferred_element_type=f32,
            )
            wq_ref[r, c, pl.ds(0, CH), :] = w.astype(bf16)
            wq_ref[r, c, pl.ds(CH, CH), :] = queries
            u_ref[r, c] = u.astype(bf16)
            lk_ref[r, c, pl.ds(0, CH), :] = jnp.where(causal, scores, 0.0).astype(bf16)
            lk_ref[r, c, pl.ds(CH, DK), :] = jnp.concatenate(key_end, axis=0).T.astype(bf16)
    decay_ref[pl.ds(pl.multiple_of(step * READY * 4, 8), READY * 4), :] = jnp.concatenate(
        decays, axis=0
    )

    @pl.when(step == R_DEV // READY - 1)
    def _():
        d_ref[...] = decay_ref[...].T


def advance_kernel(
    order_ref,
    place_ref,
    row_ref,
    ret_ref,
    counts_ref,
    *refs,
):
    sources, refs = refs[:-22], refs[-22:]
    ready, gated_outs, send_ref = refs[:5], refs[5:9], refs[9]
    wq_ref, u_ref, lk_ref, d_ref, gain_ref, initial_ref, gated_ref, final_ref = refs[10:18]
    ready_sems, in_sems, gated_sems, out_sems = refs[18:]

    def request_of(place):
        return order_ref[place // GROUP] * GROUP + place % GROUP

    def ready_copies(quarter):
        at = pl.ds(order_ref[quarter] * GROUP, GROUP)
        tokens = pl.ds(order_ref[quarter] * GROUP * ROWS, GROUP * ROWS)
        where = (at, at, at, tokens)
        sources = (ready[0], ready[1], ready[2], ready[4])
        return [
            pltpu.make_async_copy(
                source.at[where[n]], target.at[quarter], ready_sems.at[quarter * 4 + n]
            )
            for n, (source, target) in enumerate(zip(sources, (wq_ref, u_ref, lk_ref, gain_ref)))
        ]

    def decay_copy():
        return pltpu.make_async_copy(ready[3], d_ref, ready_sems.at[N_TP * 4])

    def copy_in(place, side, source):
        row = row_ref[request_of(place) * 2 + side]
        first = 0 if len(sources) > 1 else side * DK
        return pltpu.make_async_copy(
            source.at[row, pl.ds(first, DK)],
            initial_ref.at[place, pl.ds(side * DK, DK)],
            in_sems.at[place * 2 + side],
        )

    def copy_out(place):
        return pltpu.make_async_copy(
            final_ref.at[place], send_ref.at[ret_ref[request_of(place)]], out_sems.at[place]
        )

    def start_states(quarter):
        for place in range(quarter * GROUP, (quarter + 1) * GROUP):
            for side in range(2):
                chosen = place_ref[request_of(place) * 2 + side]
                for index, source in enumerate(sources):

                    @pl.when(chosen == index)
                    def _(place=place, side=side, source=source):
                        copy_in(place, side, source).start()

    def stretch(quarter, c, states, diagonals, decays):
        reads = [
            jnp.dot(wq_ref[quarter, r, c], diagonals[r], preferred_element_type=f32)
            for r in range(GROUP)
        ]
        news = [
            (u_ref[quarter, r, c].astype(f32) - reads[r][:CH]).astype(bf16) for r in range(GROUP)
        ]
        writes = [
            jnp.dot(lk_ref[quarter, r, c], pair_diagonal(news[r]), preferred_element_type=f32)
            for r in range(GROUP)
        ]
        after = []
        for r in range(GROUP):
            sides = []
            for side in range(2):
                at = r * 4 + 2 * c + side
                lanes = slice(side * DV, (side + 1) * DV)
                decay = decays[:, at : at + 1]
                sides.append(decay * states[r][side] + writes[r][CH:, lanes])
            after.append(sides)
        return [reads[r][CH:] + writes[r][:CH] for r in range(GROUP)], after

    def put_gated(quarter, c, outs, lives):
        for r in range(GROUP):
            for side in range(2):
                rows, lanes = pl.ds(r * ROWS + c * CH, CH), pl.ds(side * DV, DV)
                head_out = outs[r][:, side * DV : (side + 1) * DV]
                mean_square = jnp.mean(head_out * head_out, axis=1, keepdims=True)
                gated = head_out * lax.rsqrt(mean_square + 1e-05)
                gated = gated * gain_ref[quarter, rows, lanes].astype(f32)
                if c > 0:
                    gated = jnp.where(lives[r], gated, 0.0)
                gated_ref[quarter, rows, lanes] = gated.astype(bf16)

    decay_copy().start()
    for quarter in range(N_TP):
        start_states(quarter)
        for copy in ready_copies(quarter):
            copy.start()
    decay_copy().wait()

    for quarter in range(N_TP):
        places = [quarter * GROUP + r for r in range(GROUP)]
        lives = [counts_ref[request_of(place)] > 1 for place in places]
        for copy in ready_copies(quarter):
            copy.wait()
        for place in places:
            for side in range(2):
                copy_in(place, side, sources[0]).wait()
        stored = [
            [initial_ref[place, pl.ds(side * DK, DK), :] for side in range(2)] for place in places
        ]
        states = [[side.astype(f32) for side in sides] for sides in stored]
        decays = pltpu.roll(d_ref[...], DK - order_ref[quarter] * GROUP * 4, 1)
        outs, states = stretch(
            quarter, 0, states, [block_diagonal(*sides) for sides in stored], decays
        )
        put_gated(quarter, 0, outs, lives)
        diagonals = [block_diagonal(*[side.astype(bf16) for side in sides]) for sides in states]
        outs, after = stretch(quarter, 1, states, diagonals, decays)
        for r, place in enumerate(places):
            for side in range(2):
                final = jnp.where(lives[r], after[r][side], states[r][side])
                final_ref[place, pl.ds(side * DK, DK), :] = final.astype(bf16)
            copy_out(place).start()
        put_gated(quarter, 1, outs, lives)
        pltpu.make_async_copy(
            gated_ref.at[quarter], gated_outs[quarter], gated_sems.at[quarter]
        ).start()

    for quarter in range(N_TP):
        pltpu.make_async_copy(
            gated_ref.at[quarter], gated_outs[quarter], gated_sems.at[quarter]
        ).wait()
    for place in range(R_DEV):
        copy_out(place).wait()


def pack_kernel(core_ref, owner_ref, store_ref, keep_ref, give_ref, later_ref):
    core = core_ref[0]
    lane = lax.broadcasted_iota(jnp.int32, (TAG_ROWS, DV), 1)
    tag = jnp.zeros((TAG_ROWS, DV), jnp.int32)
    for r in range(R_DEV):
        tag = jnp.where(lane == r, owner_ref[r], tag)
    tag = tag.astype(f32).astype(bf16)
    for row in range(later_ref.shape[0]):
        keep_ref[row] = store_ref[row, core].astype(bf16)
        give_ref[row] = store_ref[row, 1 - core].astype(bf16)
        for side in range(2):
            later_ref[row, pl.ds(side * DK, DK), :] = store_ref[row, 2 + side].astype(bf16)
        later_ref[row, pl.ds(PAIR, TAG_ROWS), :] = tag


def locate_kernel(self_ref, tag_ref, source_ref):
    self_owner = self_ref[0].astype(f32)
    source = jnp.zeros((1, DV), f32)
    for block in range(CACHE):
        named = tag_ref[block].astype(f32)[:1, :] == self_owner
        source = source + jnp.where(named, float(block), 0.0)
    source_ref[...] = source.astype(jnp.int32)


def project_kernel(core_ref, *refs):
    gated, own_ref, direct, swapped = refs[:8], refs[8], refs[9:13], refs[13:17]
    out_ref = refs[17]

    def total(weights):
        acc = None
        for p in range(PAIRS):
            rows = pl.ds(p * PAIR, PAIR)
            sides = [weights[p][...]] + [ref[rows, :] for ref in (*weights[2:], own_ref)]
            for rows_ref, side in zip(gated[p * N_TP : (p + 1) * N_TP], sides):
                part = jnp.dot(rows_ref[...], side, preferred_element_type=f32)
                acc = part if acc is None else acc + part
        return acc.astype(bf16)

    @pl.when(pl.program_id(0) == 0)
    def _():
        out_ref[...] = total(direct)

    @pl.when(pl.program_id(0) == 1)
    def _():
        out_ref[...] = total(swapped)


def unpack_kernel(source_ref, *refs):
    for place in range(UNPACKED):
        refs[-1][place] = refs[place][0].astype(f32)


def pack(core, owners, ckpt_store):
    stored_here = ckpt_store.shape[0]
    whole = pl.BlockSpec(memory_space=pltpu.VMEM)
    scalars = pl.BlockSpec(memory_space=pltpu.SMEM)
    return pl.pallas_call(
        pack_kernel,
        in_specs=[scalars, scalars, whole],
        out_shape=[
            jax.ShapeDtypeStruct((stored_here, DK, DV), bf16),
            jax.ShapeDtypeStruct((stored_here, DK, DV), bf16),
            jax.ShapeDtypeStruct((stored_here, PAIR + TAG_ROWS, DV), bf16),
        ],
        compiler_params=pltpu.CompilerParams(vmem_limit_bytes=VMEM_BYTES),
        cost_estimate=pl.CostEstimate(flops=0, bytes_accessed=800_000, transcendentals=0),
        name="pack",
    )(core, owners, ckpt_store)


def locate(self_index, gathered):
    return pl.pallas_call(
        locate_kernel,
        grid=(1,),
        in_specs=[
            pl.BlockSpec(memory_space=pltpu.SMEM),
            pl.BlockSpec((CACHE, TAG_ROWS, DV), lambda i: (0, PAIR // TAG_ROWS, 0)),
        ],
        out_specs=pl.BlockSpec((1, DV), lambda i: (0, 0)),
        out_shape=jax.ShapeDtypeStruct((1, DV), jnp.int32),
        compiler_params=pltpu.CompilerParams(vmem_limit_bytes=VMEM_BYTES),
        cost_estimate=pl.CostEstimate(flops=0, bytes_accessed=200_000, transcendentals=0),
        name="locate",
    )(self_index, gathered.reshape(CACHE, -1, DV)).reshape(DV)


def prepare(pair, queries, key_vecs, values, log_decay, write_strength, inverses, out_gate, gain):
    token_rows = pl.BlockSpec((READY * ROWS, PAIR), lambda i: (i, pair))
    return pl.pallas_call(
        functools.partial(prepare_kernel, pair),
        grid=(R_DEV // READY,),
        in_specs=[token_rows] * 4
        + [
            pl.BlockSpec((HEADS, READY * ROWS), lambda i: (0, i)),
            pl.BlockSpec((READY * MAXCH, CH, 2 * CH), lambda i: (i, 0, pair)),
            token_rows,
            pl.BlockSpec((1, DV), lambda i: (0, 0)),
        ],
        out_specs=[
            pl.BlockSpec((READY, MAXCH, 2 * CH, PAIR), lambda i: (i, 0, 0, 0)),
            pl.BlockSpec((READY, MAXCH, CH, PAIR), lambda i: (i, 0, 0, 0)),
            pl.BlockSpec((READY, MAXCH, CH + DK, 2 * CH), lambda i: (i, 0, 0, 0)),
            pl.BlockSpec((DK, DK), lambda i: (0, 0)),
            pl.BlockSpec((READY * ROWS, PAIR), lambda i: (i, 0)),
        ],
        out_shape=[
            jax.ShapeDtypeStruct((R_DEV, MAXCH, 2 * CH, PAIR), bf16),
            jax.ShapeDtypeStruct((R_DEV, MAXCH, CH, PAIR), bf16),
            jax.ShapeDtypeStruct((R_DEV, MAXCH, CH + DK, 2 * CH), bf16),
            jax.ShapeDtypeStruct((DK, DK), f32),
            jax.ShapeDtypeStruct((R_DEV * ROWS, PAIR), bf16),
        ],
        scratch_shapes=[pltpu.VMEM((DK, DK), f32)],
        compiler_params=pltpu.CompilerParams(vmem_limit_bytes=VMEM_BYTES),
        cost_estimate=pl.CostEstimate(
            flops=400_000_000, bytes_accessed=14_000_000, transcendentals=2_000_000
        ),
        name="prepare",
    )(queries, key_vecs, values, log_decay, write_strength.T, inverses, out_gate, gain)


def advance(order, place, row, ret_owner, counts, sources, ready):
    anywhere = pl.BlockSpec(memory_space=pl.ANY)
    return pl.pallas_call(
        advance_kernel,
        grid_spec=pltpu.PrefetchScalarGridSpec(
            num_scalar_prefetch=5,
            grid=(1,),
            in_specs=[anywhere] * (len(sources) + len(ready)),
            out_specs=[anywhere] * (N_TP + 1),
            scratch_shapes=[
                pltpu.VMEM((N_TP, GROUP, MAXCH, 2 * CH, PAIR), bf16),
                pltpu.VMEM((N_TP, GROUP, MAXCH, CH, PAIR), bf16),
                pltpu.VMEM((N_TP, GROUP, MAXCH, CH + DK, 2 * CH), bf16),
                pltpu.VMEM((DK, DK), f32),
                pltpu.VMEM((N_TP, GROUP * ROWS, PAIR), bf16),
                pltpu.VMEM((R_DEV, PAIR, DV), bf16),
                pltpu.VMEM((N_TP, GROUP * ROWS, PAIR), bf16),
                pltpu.VMEM((R_DEV, PAIR, DV), bf16),
                pltpu.SemaphoreType.DMA((N_TP * 4 + 1,)),
                pltpu.SemaphoreType.DMA((R_DEV * 2,)),
                pltpu.SemaphoreType.DMA((N_TP,)),
                pltpu.SemaphoreType.DMA((R_DEV,)),
            ],
        ),
        out_shape=[jax.ShapeDtypeStruct((GROUP * ROWS, PAIR), bf16)] * N_TP
        + [jax.ShapeDtypeStruct((CACHE, PAIR, DV), bf16)],
        compiler_params=pltpu.CompilerParams(vmem_limit_bytes=VMEM_BYTES),
        cost_estimate=pl.CostEstimate(
            flops=500_000_000, bytes_accessed=10_000_000, transcendentals=100_000
        ),
        name="advance",
    )(order, place, row, ret_owner, counts, *sources, *ready)


def project(core, gated, own_weight, direct, swapped):
    tiles = 3
    tile = HALF // tiles
    rows = gated[0].shape[0]
    whole = pl.BlockSpec((rows, PAIR), lambda j, t, c: (0, 0))
    chosen = lambda j, c: jnp.where(j == 0, c[0], 1 - c[0])
    heights = [weight.shape[0] for weight in direct]
    return pl.pallas_call(
        project_kernel,
        grid_spec=pltpu.PrefetchScalarGridSpec(
            num_scalar_prefetch=1,
            grid=(2, tiles),
            in_specs=[whole] * (PAIRS * N_TP)
            + [pl.BlockSpec((HEADS * DK, tile), lambda j, t, c: (0, chosen(j, c) * tiles + t))]
            + [
                pl.BlockSpec((height, tile), lambda j, t, c: (0, jnp.where(j == 0, t, tiles - 1)))
                for height in heights
            ]
            + [
                pl.BlockSpec((height, tile), lambda j, t, c: (0, jnp.where(j == 0, 0, t)))
                for height in heights
            ],
            out_specs=pl.BlockSpec((rows, tile), lambda j, t, c: (0, chosen(j, c) * tiles + t)),
        ),
        out_shape=jax.ShapeDtypeStruct((rows, D), bf16),
        compiler_params=pltpu.CompilerParams(vmem_limit_bytes=VMEM_BYTES),
        cost_estimate=pl.CostEstimate(
            flops=4_800_000_000, bytes_accessed=14_000_000, transcendentals=0
        ),
        name="project",
    )(core, *gated, own_weight, *direct, *swapped)


def unpack(pair, source, received, before=None):
    def slot_of(place):
        return pl.BlockSpec((1, PAIR, DV), lambda i, s: (s[i * UNPACKED + place], 0, 0))

    kept = [] if before is None else [before]
    return pl.pallas_call(
        unpack_kernel,
        grid_spec=pltpu.PrefetchScalarGridSpec(
            num_scalar_prefetch=1,
            grid=(R_DEV // UNPACKED,),
            in_specs=[slot_of(place) for place in range(UNPACKED)]
            + [pl.BlockSpec(memory_space=pl.ANY)] * len(kept),
            out_specs=pl.BlockSpec((UNPACKED, PAIR, DV), lambda i, s: (i, pair, 0)),
        ),
        out_shape=jax.ShapeDtypeStruct((R_DEV, HEADS * DK, DV), f32),
        input_output_aliases={1 + UNPACKED: 0} if kept else {},
        compiler_params=pltpu.CompilerParams(vmem_limit_bytes=VMEM_BYTES),
        cost_estimate=pl.CostEstimate(flops=0, bytes_accessed=3_200_000, transcendentals=0),
        name="unpack",
    )(source, *[received] * UNPACKED, *kept)


def along_tp(x, shift):
    return lax.ppermute(x, "tp", [(z, (z + shift) % N_TP) for z in range(N_TP)])


def chip_and_core(index):
    return index // 8, index // 2 % 4, index % 2


def to_sibling(x):
    return lax.ppermute(x, "cache", [(i, i ^ 1) for i in range(CACHE)])


def along_chips(x, turned, shift):
    pairs = []
    for index in range(CACHE):
        chip_x, chip_y, core = chip_and_core(index)
        if (core == 0) != turned:
            chip_x = (chip_x + shift) % 4
        else:
            chip_y = (chip_y + shift) % 4
        pairs.append((index, (chip_x * 4 + chip_y) * 2 + core))
    return lax.ppermute(x, "cache", pairs)


def gather_by_chips(keep, give, beside, work):
    mine = jnp.concatenate([keep, to_sibling(give)], axis=0)
    line = jnp.concatenate(
        [mine] + [along_chips(mine, False, shift) for shift in CHIP_SHIFTS], axis=0
    )
    line, tokens = lax.optimization_barrier((line, beside[0]))
    beside = (tokens, beside[1])
    plane = [line] + [along_chips(line, True, shift) for shift in CHIP_SHIFTS]
    plane, done = lax.optimization_barrier((plane, work(beside)))
    return plane + [to_sibling(part) for part in plane], done


def places_by_chips(self_index, owner, slot):
    here_x, here_y, here_core = chip_and_core(self_index)
    chip_x, chip_y, core = chip_and_core(owner)
    ordinal = jnp.asarray([0, 2, 1, 3], jnp.int32)
    away_x = ordinal[lax.rem(here_x - chip_x + 4, 4)]
    away_y = ordinal[lax.rem(here_y - chip_y + 4, 4)]
    places, rows = [], []
    for head in range(2):
        first, second = (away_x, away_y) if head == 0 else (away_y, away_x)
        places.append(second + jnp.where(here_core == head, 0, 4))
        rows.append(first * 4 + jnp.where(core == head, 0, 2) + slot)
    return jnp.stack(places, axis=1).reshape(-1), jnp.stack(rows, axis=1).reshape(-1)


def body(
    queries,
    key_vecs,
    values,
    log_decay,
    write_strength,
    inverses,
    suffix_stretches,
    ckpt_store,
    hit_owner,
    hit_slot,
    ret_owner,
    out_gate,
    norm_gain,
    out_weight,
):
    self_index = lax.axis_index("cache").astype(jnp.int32)
    z = lax.axis_index("tp").astype(jnp.int32)
    core = lax.rem(self_index, 2)
    stored_here = ckpt_store.shape[0]

    keep, give, later = pack(core.reshape(1), ret_owner, ckpt_store)
    later = lax.all_gather(later, "cache", axis=0, tiled=True)

    half_weight = lax.dynamic_slice(out_weight, (0, core * HALF), (HEADS * DK, HALF))
    shifts = QUARTER_SHIFTS[:3]
    near_weights = [along_tp(half_weight, shift) for shift in shifts[1:]]

    tokens = (
        queries,
        key_vecs,
        values,
        log_decay,
        write_strength,
        inverses,
        out_gate,
        norm_gain.reshape(1, DV),
    )
    earlier, (ready, near_weights) = gather_by_chips(
        keep,
        give,
        (tokens, near_weights),
        lambda beside: (prepare(0, *beside[0]), beside[1]),
    )

    far_weight = [
        along_tp(weight[p * PAIR : (p + 1) * PAIR], shift)
        for p, (weight, shift) in enumerate(zip(near_weights, shifts[1:]))
    ]

    order = lax.rem(z + jnp.asarray(QUARTER_SHIFTS, jnp.int32), N_TP)
    place, row = places_by_chips(self_index, hit_owner, hit_slot)
    *gated, sending = advance(order, place, row, ret_owner, suffix_stretches, earlier, ready)
    received = [lax.all_to_all(sending, "cache", split_axis=0, concat_axis=0, tiled=True)]
    others = [along_tp(rows, shift) for rows, shift in zip(gated[:3], shifts)]
    gated_parts = others + [gated[3]]

    tokens, _ = lax.optimization_barrier((tokens, sending))
    ready = prepare(1, *tokens)
    later, far_weight, _ = lax.optimization_barrier((later, far_weight, others))
    place = jnp.zeros_like(place)
    row = jnp.repeat(hit_owner * stored_here + hit_slot, 2)
    *gated, sending = advance(order, place, row, ret_owner, suffix_stretches, [later], ready)
    received.append(lax.all_to_all(sending, "cache", split_axis=0, concat_axis=0, tiled=True))
    gated_parts += [along_tp(rows, shift) for rows, shift in zip(gated[:3], shifts)] + [gated[3]]

    direct = [*far_weight, *near_weights]
    swapped = [to_sibling(weight) for weight in direct]
    mixed = project(core.reshape(1), gated_parts, out_weight, direct, swapped)

    source = locate(self_index.reshape(1), later)
    new_ckpts = None
    for p in range(PAIRS):
        new_ckpts = unpack(p, source, received[p], new_ckpts)
    new_ckpts = new_ckpts.reshape(R_DEV, HEADS, DK, DV)
    return (mixed, new_ckpts)


def solution(mesh):
    placed = (
        P("cache", "tp"),
        P("cache", "tp"),
        P("cache", "tp"),
        P("cache", "tp"),
        P("cache", "tp"),
        P("cache", None, "tp"),
        P("cache"),
        P("cache", "tp", None, None),
        P("cache"),
        P("cache"),
        P("cache"),
        P("cache", "tp"),
        P(),
        P("tp", None),
    )
    return jax.shard_map(
        body,
        mesh=mesh,
        in_specs=placed,
        out_specs=(P(("cache", "tp"), None), P("cache", "tp", None, None)),
        check_vma=False,
    )
```

time: 216 us -> 152 us (0.70)
  waiting for transfers between devices: 97 us -> 17.6 us
  starting transfers between devices: 17.5 us -> 49.5 us
  local copies, waits for them, and re-layouts: 35.7 us -> 10.2 us
  Pallas kernels: 46.1 us -> 58.6 us
  other arithmetic: 3.92 us -> 0.61 us
    ppermute x6 -> x10, waiting for transfers between devices: 66.6 us -> 12.6 us  [along_tp(): return lax.ppermute(x, 'tp', [(z, (z + shift) % N_TP) for z in range(N_TP)])]
    unnamed x60 -> x43, local copies, waits for them, and re-layouts: 34.6 us -> 2.47 us
    all_gather x1, waiting for transfers between devices: 30.4 us -> 0.01 us  [body(): later = lax.all_gather(later, 'cache', axis=0, tiled=True)]
    pallas_call x1 -> x4, Pallas kernels: 11.3 us -> 23.1 us  [the longest x2 19.9 us: prepare(): pl.pallas_call(functools.partial(prepare_kernel, pair), grid=(R_DEV // RE...]
    ppermute x0 -> x6, starting transfers between devices: none -> 11.2 us  [along_chips(): return lax.ppermute(x, 'cache', pairs)]
    all_to_all x1 -> x2, starting transfers between devices: 4.81 us -> 14.9 us  [body(): lax.all_to_all(sending, 'cache', split_axis=0, concat_axis=0, tiled=True)]
    ppermute x6 -> x10, starting transfers between devices: 10 us -> 18.4 us  [along_tp(): return lax.ppermute(x, 'tp', [(z, (z + shift) % N_TP) for z in range(N_TP)])]
    ppermute x0 -> x6, waiting for transfers between devices: none -> 2.82 us  [along_chips(): return lax.ppermute(x, 'cache', pairs)]
  transfers between devices with their start and end apart: 11 -> 28, of which waited for: 5 -> 11; matrix products, arithmetic and copies ran while one was open for 2% -> 6% of each run, Pallas kernels for 10% -> 35%
where the time goes in v1:
time: 152 us; the launch traced here: 151 us
  Pallas kernels  58.6 us (39%)
  starting transfers between devices  49.5 us (33%)
  waiting for transfers between devices  17.6 us (12%)
  between operations  14.3 us (9%)
  local copies, waits for them, and re-layouts  10.2 us (7%)
    pallas_call x2, Pallas kernels, prepare(): pl.pallas_call(functools.partial(prepare_kernel, pair), grid=(R_DEV // RE...  19.9 us
    ppermute x10, starting transfers between devices, along_tp(): return lax.ppermute(x, 'tp', [(z, (z + shift) % N_TP) for z in range(N_TP)])  18.4 us
    pallas_call x2, Pallas kernels, advance(): pl.pallas_call(advance_kernel, grid_spec=pltpu.PrefetchScalarGridSpec(num...  15.3 us
    all_to_all x2, starting transfers between devices, body(): lax.all_to_all(sending, 'cache', split_axis=0, concat_axis=0, tiled=True)  14.9 us
    ppermute x10, waiting for transfers between devices, along_tp(): return lax.ppermute(x, 'tp', [(z, (z + shift) % N_TP) for z in range(N_TP)])  12.6 us
    pallas_call x1, Pallas kernels, project(): pl.pallas_call(project_kernel, grid_spec=pltpu.PrefetchScalarGridSpec(num...  11.7 us
    ppermute x6, starting transfers between devices, along_chips(): return lax.ppermute(x, 'cache', pairs)  11.2 us
    pallas_call x2, Pallas kernels, unpack(): pl.pallas_call(unpack_kernel, grid_spec=pltpu.PrefetchScalarGridSpec(num_...  8.51 us
  transfers between devices with their start and end apart: 28, of which 11 were waited for; matrix products, arithmetic and copies ran while one was open for 6% of the time, Pallas kernels for 35%

profile of v1, /device:TPU:1, one launch (start us, length us, event | category | flops | bytes accessed | tf_op | source)
XLA Modules:
  0.0 150.8 jit_solution(16151832474359613221)
XLA Ops:
  10.5 2.5 %collective-permute-start.7 = (bf16[512,1152]{1,0:T(8,128)(2,1)S(1)}, bf16[512,1152]{1,0:T(8,128)(2,1)}, u32[]{:S(2)}, u32[]{:S(2)}) collective-permute-start(bf16[512,1152]{1,0:T(8,128)(2,1)S(1)} %constant_dynamic-slice_fusion), channel_id=1, source_target_pairs={{0,1},{1,2},{2,3},{3,0},{4,5},{5,6},{6,7},{7,4},{8,9},{9,10},{10,1... | collective-permute-start | bytes 3538952 | tf_op jit(solution)/shard_map/ppermute | solution.py:479
  13.0 2.2 %collective-permute-start.8 = (bf16[512,1152]{1,0:T(8,128)(2,1)S(1)}, bf16[512,1152]{1,0:T(8,128)(2,1)}, u32[]{:S(2)}, u32[]{:S(2)}) collective-permute-start(bf16[512,1152]{1,0:T(8,128)(2,1)S(1)} %constant_dynamic-slice_fusion), channel_id=1, source_target_pairs={{0,3},{1,0},{2,1},{3,2},{4,7},{5,4},{6,5},{7,6},{8,11},{9,8},{10,9... | collective-permute-start | bytes 3538952 | tf_op jit(solution)/shard_map/ppermute | solution.py:479
  17.1 3.0 %collective-permute-start.1 = (bf16[4,128,128]{2,1,0:T(8,128)(2,1)S(1)}, bf16[4,128,128]{2,1,0:T(8,128)(2,1)S(1)}, u32[]{:S(2)}, u32[]{:S(2)}) collective-permute-start(bf16[4,128,128]{2,1,0:T(8,128)(2,1)S(1)} %get-tuple-element.110), channel_id=1, source_target_pairs={{0,64},{4,20},{8,72},{12,28},{16,80},{20,4},{24,88},{28,12},{32,96... | collective-permute-start | bytes 393224 | tf_op jit(solution)/shard_map/ppermute | solution.py:499
  20.5 2.3 %collective-permute-start.3 = (bf16[4,128,128]{2,1,0:T(8,128)(2,1)S(1)}, bf16[4,128,128]{2,1,0:T(8,128)(2,1)S(1)}, u32[]{:S(2)}, u32[]{:S(2)}) collective-permute-start(bf16[4,128,128]{2,1,0:T(8,128)(2,1)S(1)} %get-tuple-element.110), channel_id=1, source_target_pairs={{0,96},{4,28},{8,104},{12,4},{16,112},{20,12},{24,120},{28,20},{32... | collective-permute-start | bytes 393224 | tf_op jit(solution)/shard_map/ppermute | solution.py:499
  22.8 2.7 %collective-permute-done.2 = bf16[4,128,128]{2,1,0:T(8,128)(2,1)S(1)} collective-permute-done((bf16[4,128,128]{2,1,0:T(8,128)(2,1)S(1)}, bf16[4,128,128]{2,1,0:T(8,128)(2,1)S(1)}, u32[]{:S(2)}, u32[]{:S(2)}) %collective-permute-start.2) | collective-permute-done | bytes 131104 | tf_op jit(solution)/shard_map/ppermute | solution.py:499
  25.6 2.8 %collective-permute-start.4 = (bf16[16,128,128]{2,1,0:T(8,128)(2,1)S(1)}, bf16[16,128,128]{2,1,0:T(8,128)(2,1)S(1)}, u32[]{:S(2)}, u32[]{:S(2)}) collective-permute-start(bf16[16,128,128]{2,1,0:T(8,128)(2,1)S(1)} %constant_dynamic-update-slice_fusion.2.refs_0_), channel_id=1, source_target_pairs={{0,16},{4,68},{8,24},{12,76},{16,0},{20,84},{24,8},{28,92},{32,48}... | collective-permute-start | bytes 1572872 | tf_op jit(solution)/shard_map/ppermute | solution.py:499
  28.7 2.4 %collective-permute-start.6 = (bf16[16,128,128]{2,1,0:T(8,128)(2,1)S(1)}, bf16[16,128,128]{2,1,0:T(8,128)(2,1)S(1)}, u32[]{:S(2)}, u32[]{:S(2)}) collective-permute-start(bf16[16,128,128]{2,1,0:T(8,128)(2,1)S(1)} %constant_dynamic-update-slice_fusion.2.refs_0_), channel_id=1, source_target_pairs={{0,24},{4,100},{8,0},{12,108},{16,8},{20,116},{24,16},{28,124},{32... | collective-permute-start | bytes 1572872 | tf_op jit(solution)/shard_map/ppermute | solution.py:499
  32.5 10.0 %prepare.2 = (bf16[16,2,128,256]{3,2,1,0:T(8,128)(2,1)}, bf16[16,2,64,256]{3,2,1,0:T(8,128)(2,1)}, bf16[16,2,192,128]{3,2,1,0:T(8,128)(2,1)}, f32[128,128]{1,0:T(8,128)}, bf16[2048,256]{1,0:T(8,128)(2,1)}) custom-call(bf16[2048,512]{1,0:T(8,128)(2,1)} %q_ref.1, bf16[2048,512]{1,0:T(8,128)(2,1)} %k_ref.1, bf16[2048,512]{1,0:T(8,128)(2,1)} %v_ref.1, ...), custom_call_target="tpu_custom_call" | custom-call | flops 400000000 | bytes 14000000 | tf_op jit(solution)/shard_map/prepare/pallas_call | solution.py:356
  42.6 2.3 %collective-permute-start.9 = (bf16[16,128,128]{2,1,0:T(8,128)(2,1)S(1)}, bf16[16,128,128]{2,1,0:T(8,128)(2,1)S(1)}, u32[]{:S(2)}, u32[]{:S(2)}) collective-permute-start(bf16[16,128,128]{2,1,0:T(8,128)(2,1)S(1)} %constant_dynamic-update-slice_fusion.2.refs_0_), channel_id=1, source_target_pairs={{0,4},{4,0},{8,12},{12,8},{16,20},{20,16},{24,28},{28,24},{32,36},... | collective-permute-start | bytes 1572872 | tf_op jit(solution)/shard_map/ppermute | solution.py:487
  48.8 7.9 %advance.2 = (bf16[512,256]{1,0:T(8,128)(2,1)}, bf16[512,256]{1,0:T(8,128)(2,1)}, bf16[512,256]{1,0:T(8,128)(2,1)}, bf16[512,256]{1,0:T(8,128)(2,1)}, bf16[32,256,128]{2,1,0:T(8,128)(2,1)}) custom-call(s32[4]{0:T(128)} %compare_select_fusion.8.order_ref, s32[32]{0:T(128)} %reshape.51.place_ref, s32[32]{0:T(128)} %reshape.52.row_ref, s32[16]{0:T(128)} %ret_ref.3, ...), custom_call_target="tpu_custom_call" | custom-call | flops 500000000 | bytes 10000000 | tf_op jit(solution)/shard_map/advance/pallas_call | solution.py:391
  56.7 6.7 %all-to-all-start.1 = ((bf16[32,256,128]{2,1,0:T(8,128)(2,1)}), bf16[32,256,128]{2,1,0:T(8,128)(2,1)S(1)}, u32[]{:S(2)}, u32[]{:S(2)}) async-start(bf16[32,256,128]{2,1,0:T(8,128)(2,1)} %get-tuple-element.89), calls=%async_computation.1 | async-start | bytes 4194304 | tf_op jit(solution)/shard_map/all_to_all | solution.py:581
  65.8 2.7 %collective-permute-start.17 = (bf16[256,1152]{1,0:T(8,128)(2,1)S(1)}, bf16[256,1152]{1,0:T(8,128)(2,1)}, u32[]{:S(2)}, u32[]{:S(2)}) collective-permute-start(bf16[256,1152]{1,0:T(8,128)(2,1)S(1)} %slice.7), channel_id=1, source_target_pairs={{0,3},{1,0},{2,1},{3,2},{4,7},{5,4},{6,5},{7,6},{8,11},{9,8},{10,9... | collective-permute-start | bytes 1769480 | tf_op jit(solution)/shard_map/ppermute | solution.py:479
  70.4 1.9 %collective-permute-start.15 = (bf16[512,256]{1,0:T(8,128)(2,1)}, bf16[512,256]{1,0:T(8,128)(2,1)}, u32[]{:S(2)}, u32[]{:S(2)}) collective-permute-start(bf16[512,256]{1,0:T(8,128)(2,1)} %get-tuple-element.83), channel_id=1, source_target_pairs={{0,3},{1,0},{2,1},{3,2},{4,7},{5,4},{6,5},{7,6},{8,11},{9,8},{10,9... | collective-permute-start | bytes 786440 | tf_op jit(solution)/shard_map/ppermute | solution.py:479
  73.0 10.0 %prepare.3 = (bf16[16,2,128,256]{3,2,1,0:T(8,128)(2,1)}, bf16[16,2,64,256]{3,2,1,0:T(8,128)(2,1)}, bf16[16,2,192,128]{3,2,1,0:T(8,128)(2,1)}, f32[128,128]{1,0:T(8,128)}, bf16[2048,256]{1,0:T(8,128)(2,1)}) custom-call(bf16[2048,512]{1,0:T(8,128)(2,1)} %q_ref.1, bf16[2048,512]{1,0:T(8,128)(2,1)} %k_ref.1, bf16[2048,512]{1,0:T(8,128)(2,1)} %v_ref.1, ...), custom_call_target="tpu_custom_call" | custom-call | flops 400000000 | bytes 14000000 | tf_op jit(solution)/shard_map/prepare/pallas_call | solution.py:356
  82.9 4.2 %collective-permute-done.13.refs_0_ = bf16[512,256]{1,0:T(8,128)(2,1)S(1)} collective-permute-done((bf16[512,256]{1,0:T(8,128)(2,1)}, bf16[512,256]{1,0:T(8,128)(2,1)S(1)}, u32[]{:S(2)}, u32[]{:S(2)}) %collective-permute-start.13) | collective-permute-done | bytes 262176 | tf_op jit(solution)/shard_map/ppermute | solution.py:479
  87.2 4.8 %collective-permute-done.14.refs_1_ = bf16[512,256]{1,0:T(8,128)(2,1)} collective-permute-done((bf16[512,256]{1,0:T(8,128)(2,1)}, bf16[512,256]{1,0:T(8,128)(2,1)}, u32[]{:S(2)}, u32[]{:S(2)}) %collective-permute-start.14) | collective-permute-done | bytes 262176 | tf_op jit(solution)/shard_map/ppermute | solution.py:479
  92.8 7.4 %advance.3 = (bf16[512,256]{1,0:T(8,128)(2,1)}, bf16[512,256]{1,0:T(8,128)(2,1)}, bf16[512,256]{1,0:T(8,128)(2,1)}, bf16[512,256]{1,0:T(8,128)(2,1)}, bf16[32,256,128]{2,1,0:T(8,128)(2,1)}) custom-call(s32[4]{0:T(128)} %compare_select_fusion.8.order_ref, s32[32]{0:T(128)} %broadcast_in_dim.20.place_ref, s32[32]{0:T(128)} %reshape.54.row_ref, s32[16]{0:T(128)} %ret_ref.3, ...), custom_call_target="tpu_custom_call" | custom-call | flops 500000000 | bytes 10000000 | tf_op jit(solution)/shard_map/advance/pallas_call | solution.py:391
  101.6 8.2 %all-to-all-start = ((bf16[32,256,128]{2,1,0:T(8,128)(2,1)}), bf16[32,256,128]{2,1,0:T(8,128)(2,1)}, u32[]{:S(2)}, u32[]{:S(2)}) async-start(bf16[32,256,128]{2,1,0:T(8,128)(2,1)} %get-tuple-element.109), calls=%async_computation | async-start | bytes 4194304 | tf_op jit(solution)/shard_map/all_to_all | solution.py:591
  110.9 3.2 %collective-permute-start.18 = (bf16[512,256]{1,0:T(8,128)(2,1)}, bf16[512,256]{1,0:T(8,128)(2,1)}, u32[]{:S(2)}, u32[]{:S(2)}) collective-permute-start(bf16[512,256]{1,0:T(8,128)(2,1)} %get-tuple-element.103), channel_id=1, source_target_pairs={{0,2},{1,3},{2,0},{3,1},{4,6},{5,7},{6,4},{7,5},{8,10},{9,11},{10,... | collective-permute-start | bytes 786440 | tf_op jit(solution)/shard_map/ppermute | solution.py:479
  114.9 3.1 %collective-permute-start.20 = (bf16[512,256]{1,0:T(8,128)(2,1)S(1)}, bf16[512,256]{1,0:T(8,128)(2,1)}, u32[]{:S(2)}, u32[]{:S(2)}) collective-permute-start(bf16[512,256]{1,0:T(8,128)(2,1)S(1)} %copy-done.16), channel_id=1, source_target_pairs={{0,3},{1,0},{2,1},{3,2},{4,7},{5,4},{6,5},{7,6},{8,11},{9,8},{10,9... | collective-permute-start | bytes 786440 | tf_op jit(solution)/shard_map/ppermute | solution.py:479
  119.4 4.3 %unpack.2.refs_4_ = f32[16,512,128]{2,1,0:T(8,128)} custom-call(s32[128]{0:T(128)} %bitcast.20, bf16[32,256,128]{2,1,0:T(8,128)(2,1)} %copy-done.1, bf16[32,256,128]{2,1,0:T(8,128)(2,1)} %copy-done.1, bf16[32,256,128]{2,1,0:T(8,128)(2,1)} %copy-done.1, bf16[32,256,128]{2,1,0:T(8,128)(2,1)} %copy-done.1), custom_call_target="tpu_custom_call" | custom-call | bytes 3200000 | tf_op jit(solution)/shard_map/unpack/pallas_call | solution.py:461
  123.7 3.1 %collective-permute-done.19.refs_5_ = bf16[512,256]{1,0:T(8,128)(2,1)} collective-permute-done((bf16[512,256]{1,0:T(8,128)(2,1)S(1)}, bf16[512,256]{1,0:T(8,128)(2,1)}, u32[]{:S(2)}, u32[]{:S(2)}) %collective-permute-start.19) | collective-permute-done | bytes 262176 | tf_op jit(solution)/shard_map/ppermute | solution.py:479
  128.0 11.7 %project.1 = bf16[512,2304]{1,0:T(8,128)(2,1)} custom-call(s32[1]{0:T(128)} %bitcast.core_ref, bf16[512,256]{1,0:T(8,128)(2,1)} %copy-done.15, bf16[512,256]{1,0:T(8,128)(2,1)} %collective-permute-done.14.refs_1_, bf16[512,256]{1,0:T(8,128)(2,1)} %collective-permute-done.15.refs_2_, bf16[512,256]{1,0:T(8,128)(2,1)} %get-tuple-element.84.refs_3_, ...), custom_call_target="tpu_custom_call" | custom-call | flops 4800000000 | bytes 14000000 | tf_op jit(solution)/shard_map/project/pallas_call | solution.py:430
  139.7 4.3 %unpack.3 = f32[16,512,128]{2,1,0:T(8,128)} custom-call(s32[128]{0:T(128)} %bitcast.21, bf16[32,256,128]{2,1,0:T(8,128)(2,1)} %all-to-all-done.refs_0_.refs_1_.refs_2_.refs_3_, bf16[32,256,128]{2,1,0:T(8,128)(2,1)} %all-to-all-done.refs_0_.refs_1_.refs_2_.refs_3_, ...), custom_call_target="tpu_custom_call", output_to_operand_aliasing={{}: (5, {})} | custom-call | bytes 3200000 | tf_op jit(solution)/shard_map/unpack/pallas_call | solution.py:461
  (105 shorter events, 22.9 us)
Async XLA Ops:
  7.2 85.1 %all-gather.2.cloned.1.call-start = ((), (), s32[]{:S(2)}) async-start(), calls=%async_computation.2 | async-start | bytes 4595712 | tf_op jit(solution)/shard_map/all_gather | solution.py:550
  10.5 32.1 %collective-permute-start.7 = (bf16[512,1152]{1,0:T(8,128)(2,1)S(1)}, bf16[512,1152]{1,0:T(8,128)(2,1)}, u32[]{:S(2)}, u32[]{:S(2)}) collective-permute-start(bf16[512,1152]{1,0:T(8,128)(2,1)S(1)} %constant_dynamic-slice_fusion), channel_id=1, source_target_pairs={{0,1},{1,2},{2,3},{3,0},{4,5},{5,6},{6,7},{7,4},{8,9},{9,10},{10,1... | collective-permute-start | bytes 3538952 | tf_op jit(solution)/shard_map/ppermute | solution.py:479
  13.0 29.6 %collective-permute-start.8 = (bf16[512,1152]{1,0:T(8,128)(2,1)S(1)}, bf16[512,1152]{1,0:T(8,128)(2,1)}, u32[]{:S(2)}, u32[]{:S(2)}) collective-permute-start(bf16[512,1152]{1,0:T(8,128)(2,1)S(1)} %constant_dynamic-slice_fusion), channel_id=1, source_target_pairs={{0,3},{1,0},{2,1},{3,2},{4,7},{5,4},{6,5},{7,6},{8,11},{9,8},{10,9... | collective-permute-start | bytes 3538952 | tf_op jit(solution)/shard_map/ppermute | solution.py:479
  17.1 5.7 %collective-permute-start.1 = (bf16[4,128,128]{2,1,0:T(8,128)(2,1)S(1)}, bf16[4,128,128]{2,1,0:T(8,128)(2,1)S(1)}, u32[]{:S(2)}, u32[]{:S(2)}) collective-permute-start(bf16[4,128,128]{2,1,0:T(8,128)(2,1)S(1)} %get-tuple-element.110), channel_id=1, source_target_pairs={{0,64},{4,20},{8,72},{12,28},{16,80},{20,4},{24,88},{28,12},{32,96... | collective-permute-start | bytes 393224 | tf_op jit(solution)/shard_map/ppermute | solution.py:499
  20.1 5.4 %collective-permute-start.2 = (bf16[4,128,128]{2,1,0:T(8,128)(2,1)S(1)}, bf16[4,128,128]{2,1,0:T(8,128)(2,1)S(1)}, u32[]{:S(2)}, u32[]{:S(2)}) collective-permute-start(bf16[4,128,128]{2,1,0:T(8,128)(2,1)S(1)} %get-tuple-element.110), channel_id=1, source_target_pairs={{0,32},{4,12},{8,40},{12,20},{16,48},{20,28},{24,56},{28,4},{32,64... | collective-permute-start | bytes 393224 | tf_op jit(solution)/shard_map/ppermute | solution.py:499
  20.5 5.1 %collective-permute-start.3 = (bf16[4,128,128]{2,1,0:T(8,128)(2,1)S(1)}, bf16[4,128,128]{2,1,0:T(8,128)(2,1)S(1)}, u32[]{:S(2)}, u32[]{:S(2)}) collective-permute-start(bf16[4,128,128]{2,1,0:T(8,128)(2,1)S(1)} %get-tuple-element.110), channel_id=1, source_target_pairs={{0,96},{4,28},{8,104},{12,4},{16,112},{20,12},{24,120},{28,20},{32... | collective-permute-start | bytes 393224 | tf_op jit(solution)/shard_map/ppermute | solution.py:499
  25.6 16.9 %collective-permute-start.4 = (bf16[16,128,128]{2,1,0:T(8,128)(2,1)S(1)}, bf16[16,128,128]{2,1,0:T(8,128)(2,1)S(1)}, u32[]{:S(2)}, u32[]{:S(2)}) collective-permute-start(bf16[16,128,128]{2,1,0:T(8,128)(2,1)S(1)} %constant_dynamic-update-slice_fusion.2.refs_0_), channel_id=1, source_target_pairs={{0,16},{4,68},{8,24},{12,76},{16,0},{20,84},{24,8},{28,92},{32,48}... | collective-permute-start | bytes 1572872 | tf_op jit(solution)/shard_map/ppermute | solution.py:499
  28.4 14.1 %collective-permute-start.5 = (bf16[16,128,128]{2,1,0:T(8,128)(2,1)S(1)}, bf16[16,128,128]{2,1,0:T(8,128)(2,1)S(1)}, u32[]{:S(2)}, u32[]{:S(2)}) collective-permute-start(bf16[16,128,128]{2,1,0:T(8,128)(2,1)S(1)} %constant_dynamic-update-slice_fusion.2.refs_0_), channel_id=1, source_target_pairs={{0,8},{4,36},{8,16},{12,44},{16,24},{20,52},{24,0},{28,60},{32,40}... | collective-permute-start | bytes 1572872 | tf_op jit(solution)/shard_map/ppermute | solution.py:499
  28.7 13.9 %collective-permute-start.6 = (bf16[16,128,128]{2,1,0:T(8,128)(2,1)S(1)}, bf16[16,128,128]{2,1,0:T(8,128)(2,1)S(1)}, u32[]{:S(2)}, u32[]{:S(2)}) collective-permute-start(bf16[16,128,128]{2,1,0:T(8,128)(2,1)S(1)} %constant_dynamic-update-slice_fusion.2.refs_0_), channel_id=1, source_target_pairs={{0,24},{4,100},{8,0},{12,108},{16,8},{20,116},{24,16},{28,124},{32... | collective-permute-start | bytes 1572872 | tf_op jit(solution)/shard_map/ppermute | solution.py:499
  42.6 5.0 %collective-permute-start.9 = (bf16[16,128,128]{2,1,0:T(8,128)(2,1)S(1)}, bf16[16,128,128]{2,1,0:T(8,128)(2,1)S(1)}, u32[]{:S(2)}, u32[]{:S(2)}) collective-permute-start(bf16[16,128,128]{2,1,0:T(8,128)(2,1)S(1)} %constant_dynamic-update-slice_fusion.2.refs_0_), channel_id=1, source_target_pairs={{0,4},{4,0},{8,12},{12,8},{16,20},{20,16},{24,28},{28,24},{32,36},... | collective-permute-start | bytes 1572872 | tf_op jit(solution)/shard_map/ppermute | solution.py:487
  56.7 43.5 %all-to-all-start.1 = ((bf16[32,256,128]{2,1,0:T(8,128)(2,1)}), bf16[32,256,128]{2,1,0:T(8,128)(2,1)S(1)}, u32[]{:S(2)}, u32[]{:S(2)}) async-start(bf16[32,256,128]{2,1,0:T(8,128)(2,1)} %get-tuple-element.89), calls=%async_computation.1 | async-start | bytes 4194304 | tf_op jit(solution)/shard_map/all_to_all | solution.py:581
  64.6 18.3 %collective-permute-start.16 = (bf16[256,1152]{1,0:T(8,128)(2,1)S(1)}, bf16[256,1152]{1,0:T(8,128)(2,1)}, u32[]{:S(2)}, u32[]{:S(2)}) collective-permute-start(bf16[256,1152]{1,0:T(8,128)(2,1)S(1)} %slice.6), channel_id=1, source_target_pairs={{0,1},{1,2},{2,3},{3,0},{4,5},{5,6},{6,7},{7,4},{8,9},{9,10},{10,1... | collective-permute-start | bytes 1769480 | tf_op jit(solution)/shard_map/ppermute | solution.py:479
  65.8 17.1 %collective-permute-start.17 = (bf16[256,1152]{1,0:T(8,128)(2,1)S(1)}, bf16[256,1152]{1,0:T(8,128)(2,1)}, u32[]{:S(2)}, u32[]{:S(2)}) collective-permute-start(bf16[256,1152]{1,0:T(8,128)(2,1)S(1)} %slice.7), channel_id=1, source_target_pairs={{0,3},{1,0},{2,1},{3,2},{4,7},{5,4},{6,5},{7,6},{8,11},{9,8},{10,9... | collective-permute-start | bytes 1769480 | tf_op jit(solution)/shard_map/ppermute | solution.py:479
  68.5 18.6 %collective-permute-start.13 = (bf16[512,256]{1,0:T(8,128)(2,1)}, bf16[512,256]{1,0:T(8,128)(2,1)S(1)}, u32[]{:S(2)}, u32[]{:S(2)}) collective-permute-start(bf16[512,256]{1,0:T(8,128)(2,1)} %get-tuple-element.81), channel_id=1, source_target_pairs={{0,2},{1,3},{2,0},{3,1},{4,6},{5,7},{6,4},{7,5},{8,10},{9,11},{10,... | collective-permute-start | bytes 786440 | tf_op jit(solution)/shard_map/ppermute | solution.py:479
  69.6 22.3 %collective-permute-start.14 = (bf16[512,256]{1,0:T(8,128)(2,1)}, bf16[512,256]{1,0:T(8,128)(2,1)}, u32[]{:S(2)}, u32[]{:S(2)}) collective-permute-start(bf16[512,256]{1,0:T(8,128)(2,1)} %get-tuple-element.82), channel_id=1, source_target_pairs={{0,1},{1,2},{2,3},{3,0},{4,5},{5,6},{6,7},{7,4},{8,9},{9,10},{10,1... | collective-permute-start | bytes 786440 | tf_op jit(solution)/shard_map/ppermute | solution.py:479
  70.4 21.9 %collective-permute-start.15 = (bf16[512,256]{1,0:T(8,128)(2,1)}, bf16[512,256]{1,0:T(8,128)(2,1)}, u32[]{:S(2)}, u32[]{:S(2)}) collective-permute-start(bf16[512,256]{1,0:T(8,128)(2,1)} %get-tuple-element.83), channel_id=1, source_target_pairs={{0,3},{1,0},{2,1},{3,2},{4,7},{5,4},{6,5},{7,6},{8,11},{9,8},{10,9... | collective-permute-start | bytes 786440 | tf_op jit(solution)/shard_map/ppermute | solution.py:479
  101.6 38.1 %all-to-all-start = ((bf16[32,256,128]{2,1,0:T(8,128)(2,1)}), bf16[32,256,128]{2,1,0:T(8,128)(2,1)}, u32[]{:S(2)}, u32[]{:S(2)}) async-start(bf16[32,256,128]{2,1,0:T(8,128)(2,1)} %get-tuple-element.109), calls=%async_computation | async-start | bytes 4194304 | tf_op jit(solution)/shard_map/all_to_all | solution.py:591
  109.8 4.3 %collective-permute-start.23 = (bf16[512,1152]{1,0:T(8,128)(2,1)}, bf16[512,1152]{1,0:T(8,128)(2,1)S(1)}, u32[]{:S(2)}, u32[]{:S(2)}) collective-permute-start(bf16[512,1152]{1,0:T(8,128)(2,1)} %collective-permute-done.7.refs_11_), channel_id=1, source_target_pairs={{0,4},{4,0},{8,12},{12,8},{16,20},{20,16},{24,28},{28,24},{32,36},... | collective-permute-start | bytes 3538952 | tf_op jit(solution)/shard_map/ppermute | solution.py:487
  110.1 4.8 %collective-permute-start.24 = (bf16[512,1152]{1,0:T(8,128)(2,1)}, bf16[512,1152]{1,0:T(8,128)(2,1)S(1)}, u32[]{:S(2)}, u32[]{:S(2)}) collective-permute-start(bf16[512,1152]{1,0:T(8,128)(2,1)} %collective-permute-done.8.refs_12_), channel_id=1, source_target_pairs={{0,4},{4,0},{8,12},{12,8},{16,20},{20,16},{24,28},{28,24},{32,36},... | collective-permute-start | bytes 3538952 | tf_op jit(solution)/shard_map/ppermute | solution.py:487
  110.3 16.6 %collective-permute-start.21 = (bf16[256,1152]{1,0:T(8,128)(2,1)}, bf16[256,1152]{1,0:T(8,128)(2,1)S(1)}, u32[]{:S(2)}, u32[]{:S(2)}) collective-permute-start(bf16[256,1152]{1,0:T(8,128)(2,1)} %collective-permute-done.16.refs_9_), channel_id=1, source_target_pairs={{0,4},{4,0},{8,12},{12,8},{16,20},{20,16},{24,28},{28,24},{32,36},... | collective-permute-start | bytes 1769480 | tf_op jit(solution)/shard_map/ppermute | solution.py:487
  110.7 16.3 %collective-permute-start.22 = (bf16[256,1152]{1,0:T(8,128)(2,1)}, bf16[256,1152]{1,0:T(8,128)(2,1)S(1)}, u32[]{:S(2)}, u32[]{:S(2)}) collective-permute-start(bf16[256,1152]{1,0:T(8,128)(2,1)} %collective-permute-done.17.refs_10_), channel_id=1, source_target_pairs={{0,4},{4,0},{8,12},{12,8},{16,20},{20,16},{24,28},{28,24},{32,36},... | collective-permute-start | bytes 1769480 | tf_op jit(solution)/shard_map/ppermute | solution.py:487
  110.9 12.8 %collective-permute-start.18 = (bf16[512,256]{1,0:T(8,128)(2,1)}, bf16[512,256]{1,0:T(8,128)(2,1)}, u32[]{:S(2)}, u32[]{:S(2)}) collective-permute-start(bf16[512,256]{1,0:T(8,128)(2,1)} %get-tuple-element.103), channel_id=1, source_target_pairs={{0,2},{1,3},{2,0},{3,1},{4,6},{5,7},{6,4},{7,5},{8,10},{9,11},{10,... | collective-permute-start | bytes 786440 | tf_op jit(solution)/shard_map/ppermute | solution.py:479
  114.1 12.7 %collective-permute-start.19 = (bf16[512,256]{1,0:T(8,128)(2,1)S(1)}, bf16[512,256]{1,0:T(8,128)(2,1)}, u32[]{:S(2)}, u32[]{:S(2)}) collective-permute-start(bf16[512,256]{1,0:T(8,128)(2,1)S(1)} %copy-done.17), channel_id=1, source_target_pairs={{0,1},{1,2},{2,3},{3,0},{4,5},{5,6},{6,7},{7,4},{8,9},{9,10},{10,1... | collective-permute-start | bytes 786440 | tf_op jit(solution)/shard_map/ppermute | solution.py:479
  114.9 12.0 %collective-permute-start.20 = (bf16[512,256]{1,0:T(8,128)(2,1)S(1)}, bf16[512,256]{1,0:T(8,128)(2,1)}, u32[]{:S(2)}, u32[]{:S(2)}) collective-permute-start(bf16[512,256]{1,0:T(8,128)(2,1)S(1)} %copy-done.16), channel_id=1, source_target_pairs={{0,3},{1,0},{2,1},{3,2},{4,7},{5,4},{6,5},{7,6},{8,11},{9,8},{10,9... | collective-permute-start | bytes 786440 | tf_op jit(solution)/shard_map/ppermute | solution.py:479
  (24 other events, 192.7 us)
Sparse Core Ops, SparseCore 0:
  10.3 55.0 all-gather.1

commit v2 on v1

--- a/solution.py
+++ b/solution.py
@@ -16,20 +16,29 @@
 PAIRS = HEADS // 2
 CACHE = 32
 N_TP = 4
+CK_DEV = 2
 CHIP_SHIFTS = (2, 1, 3)
 D = 2304
-HALF = D // 2
+TILES = 3
 PAIR = 2 * DK
 ROWS = MAXCH * CH
 TAG_ROWS = 16
-READY = 2
+READY = 4
 GROUP = 4
-UNPACKED = 4
 VMEM_BYTES = 60 << 20
+UNPACK_BYTES = 8 << 20
 QUARTER_SHIFTS = (2, 1, 3, 0)
 
 f32 = jnp.float32
 bf16 = jnp.bfloat16
+
+
+def chip_and_core(index):
+    return index // 8, index // 2 % 4, index % 2
+
+
+def chip_ordinal(shift):
+    return jnp.where(shift == 1, 2, jnp.where(shift == 2, 1, shift))
 
 
 def block_diagonal(left, right):
@@ -132,9 +141,8 @@
 
 
 def advance_kernel(
-    order_ref,
-    place_ref,
-    row_ref,
+    owner_ref,
+    slot_ref,
     ret_ref,
     counts_ref,
     *refs,
@@ -144,12 +152,27 @@
     wq_ref, u_ref, lk_ref, d_ref, gain_ref, initial_ref, gated_ref, final_ref = refs[10:18]
     ready_sems, in_sems, gated_sems, out_sems = refs[18:]
 
+    here_x, here_y, here_core = chip_and_core(lax.axis_index("cache"))
+    z = lax.axis_index("tp")
+    order = [lax.rem(z + shift, N_TP) for shift in QUARTER_SHIFTS]
+
     def request_of(place):
-        return order_ref[place // GROUP] * GROUP + place % GROUP
+        return order[place // GROUP] * GROUP + place % GROUP
+
+    def whereabouts(place):
+        owner, slot = owner_ref[request_of(place)], slot_ref[request_of(place)]
+        if len(sources) == 1:
+            return 0, owner * CK_DEV + slot
+        chip_x, chip_y, core = chip_and_core(owner)
+        away_x = chip_ordinal(lax.rem(here_x - chip_x + 4, 4))
+        away_y = chip_ordinal(lax.rem(here_y - chip_y + 4, 4))
+        first = jnp.where(core == 0, away_x, away_y)
+        second = jnp.where(core == 0, away_y, away_x)
+        return second + jnp.where(core == here_core, 0, 4), first * CK_DEV + slot
 
     def ready_copies(quarter):
-        at = pl.ds(order_ref[quarter] * GROUP, GROUP)
-        tokens = pl.ds(order_ref[quarter] * GROUP * ROWS, GROUP * ROWS)
+        at = pl.ds(order[quarter] * GROUP, GROUP)
+        tokens = pl.ds(order[quarter] * GROUP * ROWS, GROUP * ROWS)
         where = (at, at, at, tokens)
         sources = (ready[0], ready[1], ready[2], ready[4])
         return [
@@ -162,13 +185,9 @@
     def decay_copy():
         return pltpu.make_async_copy(ready[3], d_ref, ready_sems.at[N_TP * 4])
 
-    def copy_in(place, side, source):
-        row = row_ref[request_of(place) * 2 + side]
-        first = 0 if len(sources) > 1 else side * DK
+    def copy_in(place, source, row):
         return pltpu.make_async_copy(
-            source.at[row, pl.ds(first, DK)],
-            initial_ref.at[place, pl.ds(side * DK, DK)],
-            in_sems.at[place * 2 + side],
+            source.at[row, pl.ds(0, PAIR)], initial_ref.at[place], in_sems.at[place]
         )
 
     def copy_out(place):
@@ -178,13 +197,12 @@
 
     def start_states(quarter):
         for place in range(quarter * GROUP, (quarter + 1) * GROUP):
-            for side in range(2):
-                chosen = place_ref[request_of(place) * 2 + side]
-                for index, source in enumerate(sources):
-
-                    @pl.when(chosen == index)
-                    def _(place=place, side=side, source=source):
-                        copy_in(place, side, source).start()
+            chosen, row = whereabouts(place)
+            for index, source in enumerate(sources):
+
+                @pl.when(chosen == index)
+                def _(place=place, source=source, row=row):
+                    copy_in(place, source, row).start()
 
     def stretch(quarter, c, states, diagonals, decays):
         reads = [
@@ -223,9 +241,10 @@
 
     decay_copy().start()
     for quarter in range(N_TP):
-        start_states(quarter)
         for copy in ready_copies(quarter):
             copy.start()
+        if quarter < 2:
+            start_states(quarter)
     decay_copy().wait()
 
     for quarter in range(N_TP):
@@ -234,13 +253,12 @@
         for copy in ready_copies(quarter):
             copy.wait()
         for place in places:
-            for side in range(2):
-                copy_in(place, side, sources[0]).wait()
+            copy_in(place, sources[0], 0).wait()
         stored = [
             [initial_ref[place, pl.ds(side * DK, DK), :] for side in range(2)] for place in places
         ]
         states = [[side.astype(f32) for side in sides] for sides in stored]
-        decays = pltpu.roll(d_ref[...], DK - order_ref[quarter] * GROUP * 4, 1)
+        decays = pltpu.roll(d_ref[...], DK - order[quarter] * GROUP * 4, 1)
         outs, states = stretch(
             quarter, 0, states, [block_diagonal(*sides) for sides in stored], decays
         )
@@ -253,6 +271,8 @@
                 final_ref[place, pl.ds(side * DK, DK), :] = final.astype(bf16)
             copy_out(place).start()
         put_gated(quarter, 1, outs, lives)
+        if quarter + 2 < N_TP:
+            start_states(quarter + 2)
         pltpu.make_async_copy(
             gated_ref.at[quarter], gated_outs[quarter], gated_sems.at[quarter]
         ).start()
@@ -265,23 +285,21 @@
         copy_out(place).wait()
 
 
-def pack_kernel(core_ref, owner_ref, store_ref, keep_ref, give_ref, later_ref):
-    core = core_ref[0]
+def pack_kernel(owner_ref, store_ref, earlier_ref, later_ref):
     lane = lax.broadcasted_iota(jnp.int32, (TAG_ROWS, DV), 1)
     tag = jnp.zeros((TAG_ROWS, DV), jnp.int32)
     for r in range(R_DEV):
         tag = jnp.where(lane == r, owner_ref[r], tag)
     tag = tag.astype(f32).astype(bf16)
-    for row in range(later_ref.shape[0]):
-        keep_ref[row] = store_ref[row, core].astype(bf16)
-        give_ref[row] = store_ref[row, 1 - core].astype(bf16)
+    for row in range(CK_DEV):
         for side in range(2):
+            earlier_ref[row, pl.ds(side * DK, DK), :] = store_ref[row, side].astype(bf16)
             later_ref[row, pl.ds(side * DK, DK), :] = store_ref[row, 2 + side].astype(bf16)
         later_ref[row, pl.ds(PAIR, TAG_ROWS), :] = tag
 
 
-def locate_kernel(self_ref, tag_ref, source_ref):
-    self_owner = self_ref[0].astype(f32)
+def locate_kernel(tag_ref, source_ref):
+    self_owner = lax.axis_index("cache").astype(f32)
     source = jnp.zeros((1, DV), f32)
     for block in range(CACHE):
         named = tag_ref[block].astype(f32)[:1, :] == self_owner
@@ -289,66 +307,81 @@
     source_ref[...] = source.astype(jnp.int32)
 
 
-def project_kernel(core_ref, *refs):
-    gated, own_ref, direct, swapped = refs[:8], refs[8], refs[9:13], refs[13:17]
-    out_ref = refs[17]
-
-    def total(weights):
-        acc = None
+def project_kernel(*refs):
+    gated, own_ref, mine_ref, sibling_ref = refs[:8], refs[8], refs[9], refs[10]
+    far_mine_ref, far_sibling_ref, out_ref = refs[11:]
+    core = lax.axis_index("cache") % 2
+    rows = jnp.concatenate([ref[...] for ref in gated], axis=1)
+
+    def put(below_ref, above_ref, far_refs):
+        weights = []
         for p in range(PAIRS):
-            rows = pl.ds(p * PAIR, PAIR)
-            sides = [weights[p][...]] + [ref[rows, :] for ref in (*weights[2:], own_ref)]
-            for rows_ref, side in zip(gated[p * N_TP : (p + 1) * N_TP], sides):
-                part = jnp.dot(rows_ref[...], side, preferred_element_type=f32)
-                acc = part if acc is None else acc + part
-        return acc.astype(bf16)
-
-    @pl.when(pl.program_id(0) == 0)
+            at = pl.ds(p * PAIR, PAIR)
+            weights += [far_refs[p][...], below_ref[at, :], above_ref[at, :], own_ref[at, :]]
+        out_ref[...] = jnp.dot(
+            rows, jnp.concatenate(weights, axis=0), preferred_element_type=f32
+        ).astype(bf16)
+
+    @pl.when(core == 0)
     def _():
-        out_ref[...] = total(direct)
-
-    @pl.when(pl.program_id(0) == 1)
+        put(mine_ref, sibling_ref, (far_mine_ref, far_sibling_ref))
+
+    @pl.when(core == 1)
     def _():
-        out_ref[...] = total(swapped)
-
-
-def unpack_kernel(source_ref, *refs):
-    for place in range(UNPACKED):
-        refs[-1][place] = refs[place][0].astype(f32)
-
-
-def pack(core, owners, ckpt_store):
-    stored_here = ckpt_store.shape[0]
+        put(sibling_ref, mine_ref, (far_sibling_ref, far_mine_ref))
+
+
+def unpack_kernel(pair, source_ref, received_ref, *refs):
+    out_ref, slots_ref, states_ref, in_sems, out_sems = refs[-5:]
+
+    def copy_in(place):
+        return pltpu.make_async_copy(
+            received_ref.at[source_ref[place]], slots_ref.at[place], in_sems.at[place]
+        )
+
+    def copy_out(place):
+        return pltpu.make_async_copy(
+            states_ref.at[place],
+            out_ref.at[place, pl.ds(pair * PAIR, PAIR)],
+            out_sems.at[place],
+        )
+
+    for place in range(R_DEV):
+        copy_in(place).start()
+    for place in range(R_DEV):
+        copy_in(place).wait()
+        states_ref[place] = slots_ref[place].astype(f32)
+        copy_out(place).start()
+    for place in range(R_DEV):
+        copy_out(place).wait()
+
+
+def pack(owners, ckpt_store):
     whole = pl.BlockSpec(memory_space=pltpu.VMEM)
-    scalars = pl.BlockSpec(memory_space=pltpu.SMEM)
     return pl.pallas_call(
         pack_kernel,
-        in_specs=[scalars, scalars, whole],
+        in_specs=[pl.BlockSpec(memory_space=pltpu.SMEM), whole],
         out_shape=[
-            jax.ShapeDtypeStruct((stored_here, DK, DV), bf16),
-            jax.ShapeDtypeStruct((stored_here, DK, DV), bf16),
-            jax.ShapeDtypeStruct((stored_here, PAIR + TAG_ROWS, DV), bf16),
+            jax.ShapeDtypeStruct((CK_DEV, PAIR, DV), bf16),
+            jax.ShapeDtypeStruct((CK_DEV, PAIR + TAG_ROWS, DV), bf16),
         ],
         compiler_params=pltpu.CompilerParams(vmem_limit_bytes=VMEM_BYTES),
         cost_estimate=pl.CostEstimate(flops=0, bytes_accessed=800_000, transcendentals=0),
         name="pack",
-    )(core, owners, ckpt_store)
-
-
-def locate(self_index, gathered):
+    )(owners, ckpt_store)
+
+
+def locate(gathered):
     return pl.pallas_call(
         locate_kernel,
         grid=(1,),
-        in_specs=[
-            pl.BlockSpec(memory_space=pltpu.SMEM),
-            pl.BlockSpec((CACHE, TAG_ROWS, DV), lambda i: (0, PAIR // TAG_ROWS, 0)),
-        ],
+        in_specs=[pl.BlockSpec((CACHE, TAG_ROWS, DV), lambda i: (0, PAIR // TAG_ROWS, 0))],
         out_specs=pl.BlockSpec((1, DV), lambda i: (0, 0)),
         out_shape=jax.ShapeDtypeStruct((1, DV), jnp.int32),
         compiler_params=pltpu.CompilerParams(vmem_limit_bytes=VMEM_BYTES),
         cost_estimate=pl.CostEstimate(flops=0, bytes_accessed=200_000, transcendentals=0),
         name="locate",
-    )(self_index, gathered.reshape(CACHE, -1, DV)).reshape(DV)
+    )(gathered.reshape(CACHE, -1, DV)).reshape(DV)
 
 
 def prepare(pair, queries, key_vecs, values, log_decay, write_strength, inverses, out_gate, gain):
@@ -386,12 +419,12 @@
     )(queries, key_vecs, values, log_decay, write_strength.T, inverses, out_gate, gain)
 
 
-def advance(order, place, row, ret_owner, counts, sources, ready):
+def advance(hit_owner, hit_slot, ret_owner, counts, sources, ready):
     anywhere = pl.BlockSpec(memory_space=pl.ANY)
     return pl.pallas_call(
         advance_kernel,
         grid_spec=pltpu.PrefetchScalarGridSpec(
-            num_scalar_prefetch=5,
+            num_scalar_prefetch=4,
             grid=(1,),
             in_specs=[anywhere] * (len(sources) + len(ready)),
             out_specs=[anywhere] * (N_TP + 1),
@@ -405,7 +438,7 @@
                 pltpu.VMEM((N_TP, GROUP * ROWS, PAIR), bf16),
                 pltpu.VMEM((R_DEV, PAIR, DV), bf16),
                 pltpu.SemaphoreType.DMA((N_TP * 4 + 1,)),
-                pltpu.SemaphoreType.DMA((R_DEV * 2,)),
+                pltpu.SemaphoreType.DMA((R_DEV,)),
                 pltpu.SemaphoreType.DMA((N_TP,)),
                 pltpu.SemaphoreType.DMA((R_DEV,)),
             ],
@@ -417,70 +450,63 @@
             flops=500_000_000, bytes_accessed=10_000_000, transcendentals=100_000
         ),
         name="advance",
-    )(order, place, row, ret_owner, counts, *sources, *ready)
-
-
-def project(core, gated, own_weight, direct, swapped):
-    tiles = 3
-    tile = HALF // tiles
+    )(hit_owner, hit_slot, ret_owner, counts, *sources, *ready)
+
+
+def project(gated, own_weight, weights):
+    tile = D // TILES
     rows = gated[0].shape[0]
-    whole = pl.BlockSpec((rows, PAIR), lambda j, t, c: (0, 0))
-    chosen = lambda j, c: jnp.where(j == 0, c[0], 1 - c[0])
-    heights = [weight.shape[0] for weight in direct]
+    weights = [own_weight, *weights]
     return pl.pallas_call(
         project_kernel,
-        grid_spec=pltpu.PrefetchScalarGridSpec(
-            num_scalar_prefetch=1,
-            grid=(2, tiles),
-            in_specs=[whole] * (PAIRS * N_TP)
-            + [pl.BlockSpec((HEADS * DK, tile), lambda j, t, c: (0, chosen(j, c) * tiles + t))]
-            + [
-                pl.BlockSpec((height, tile), lambda j, t, c: (0, jnp.where(j == 0, t, tiles - 1)))
-                for height in heights
-            ]
-            + [
-                pl.BlockSpec((height, tile), lambda j, t, c: (0, jnp.where(j == 0, 0, t)))
-                for height in heights
-            ],
-            out_specs=pl.BlockSpec((rows, tile), lambda j, t, c: (0, chosen(j, c) * tiles + t)),
-        ),
+        grid=(TILES,),
+        in_specs=[pl.BlockSpec((rows, PAIR), lambda t: (0, 0))] * (PAIRS * N_TP)
+        + [pl.BlockSpec((weight.shape[0], tile), lambda t: (0, t)) for weight in weights],
+        out_specs=pl.BlockSpec((rows, tile), lambda t: (0, t)),
         out_shape=jax.ShapeDtypeStruct((rows, D), bf16),
         compiler_params=pltpu.CompilerParams(vmem_limit_bytes=VMEM_BYTES),
         cost_estimate=pl.CostEstimate(
             flops=4_800_000_000, bytes_accessed=14_000_000, transcendentals=0
         ),
         name="project",
-    )(core, *gated, own_weight, *direct, *swapped)
+    )(*gated, *weights)
 
 
 def unpack(pair, source, received, before=None):
-    def slot_of(place):
-        return pl.BlockSpec((1, PAIR, DV), lambda i, s: (s[i * UNPACKED + place], 0, 0))
-
     kept = [] if before is None else [before]
     return pl.pallas_call(
-        unpack_kernel,
+        functools.partial(unpack_kernel, pair),
         grid_spec=pltpu.PrefetchScalarGridSpec(
             num_scalar_prefetch=1,
-            grid=(R_DEV // UNPACKED,),
-            in_specs=[slot_of(place) for place in range(UNPACKED)]
-            + [pl.BlockSpec(memory_space=pl.ANY)] * len(kept),
-            out_specs=pl.BlockSpec((UNPACKED, PAIR, DV), lambda i, s: (i, pair, 0)),
+            grid=(1,),
+            in_specs=[pl.BlockSpec(memory_space=pl.ANY)] * (1 + len(kept)),
+            out_specs=pl.BlockSpec(memory_space=pl.ANY),
+            scratch_shapes=[
+                pltpu.VMEM((R_DEV, PAIR, DV), bf16),
+                pltpu.VMEM((R_DEV, PAIR, DV), f32),
+                pltpu.SemaphoreType.DMA((R_DEV,)),
+                pltpu.SemaphoreType.DMA((R_DEV,)),
+            ],
         ),
         out_shape=jax.ShapeDtypeStruct((R_DEV, HEADS * DK, DV), f32),
-        input_output_aliases={1 + UNPACKED: 0} if kept else {},
-        compiler_params=pltpu.CompilerParams(vmem_limit_bytes=VMEM_BYTES),
+        input_output_aliases={2: 0} if kept else {},
+        compiler_params=pltpu.CompilerParams(vmem_limit_bytes=UNPACK_BYTES),
         cost_estimate=pl.CostEstimate(flops=0, bytes_accessed=3_200_000, transcendentals=0),
         name="unpack",
-    )(source, *[received] * UNPACKED, *kept)
+    )(source, received, *kept)
 
 
 def along_tp(x, shift):
     return lax.ppermute(x, "tp", [(z, (z + shift) % N_TP) for z in range(N_TP)])
 
 
-def chip_and_core(index):
-    return index // 8, index // 2 % 4, index % 2
+def by_cores_along_tp(x):
+    pairs = []
+    for index in range(CACHE):
+        for z in range(N_TP):
+            to = (z + (1 if index % 2 == 0 else N_TP - 1)) % N_TP
+            pairs.append((index * N_TP + z, index * N_TP + to))
+    return lax.ppermute(x, ("cache", "tp"), pairs)
 
 
 def to_sibling(x):
@@ -499,30 +525,16 @@
     return lax.ppermute(x, "cache", pairs)
 
 
-def gather_by_chips(keep, give, beside, work):
-    mine = jnp.concatenate([keep, to_sibling(give)], axis=0)
+def gather_by_chips(mine, beside, work):
     line = jnp.concatenate(
         [mine] + [along_chips(mine, False, shift) for shift in CHIP_SHIFTS], axis=0
     )
     line, tokens = lax.optimization_barrier((line, beside[0]))
     beside = (tokens, beside[1])
-    plane = [line] + [along_chips(line, True, shift) for shift in CHIP_SHIFTS]
+    plane = [along_chips(line, True, shift) for shift in CHIP_SHIFTS]
     plane, done = lax.optimization_barrier((plane, work(beside)))
+    plane = [line, *plane]
     return plane + [to_sibling(part) for part in plane], done
-
-
-def places_by_chips(self_index, owner, slot):
-    here_x, here_y, here_core = chip_and_core(self_index)
-    chip_x, chip_y, core = chip_and_core(owner)
-    ordinal = jnp.asarray([0, 2, 1, 3], jnp.int32)
-    away_x = ordinal[lax.rem(here_x - chip_x + 4, 4)]
-    away_y = ordinal[lax.rem(here_y - chip_y + 4, 4)]
-    places, rows = [], []
-    for head in range(2):
-        first, second = (away_x, away_y) if head == 0 else (away_y, away_x)
-        places.append(second + jnp.where(here_core == head, 0, 4))
-        rows.append(first * 4 + jnp.where(core == head, 0, 2) + slot)
-    return jnp.stack(places, axis=1).reshape(-1), jnp.stack(rows, axis=1).reshape(-1)
 
 
 def body(
@@ -541,17 +553,11 @@
     norm_gain,
     out_weight,
 ):
-    self_index = lax.axis_index("cache").astype(jnp.int32)
-    z = lax.axis_index("tp").astype(jnp.int32)
-    core = lax.rem(self_index, 2)
-    stored_here = ckpt_store.shape[0]
-
-    keep, give, later = pack(core.reshape(1), ret_owner, ckpt_store)
+    earlier, later = pack(ret_owner, ckpt_store)
     later = lax.all_gather(later, "cache", axis=0, tiled=True)
 
-    half_weight = lax.dynamic_slice(out_weight, (0, core * HALF), (HEADS * DK, HALF))
+    near_weight = by_cores_along_tp(out_weight)
     shifts = QUARTER_SHIFTS[:3]
-    near_weights = [along_tp(half_weight, shift) for shift in shifts[1:]]
 
     tokens = (
         queries,
@@ -563,39 +569,34 @@
         out_gate,
         norm_gain.reshape(1, DV),
     )
-    earlier, (ready, near_weights) = gather_by_chips(
-        keep,
-        give,
-        (tokens, near_weights),
-        lambda beside: (prepare(0, *beside[0]), beside[1]),
-    )
-
-    far_weight = [
-        along_tp(weight[p * PAIR : (p + 1) * PAIR], shift)
-        for p, (weight, shift) in enumerate(zip(near_weights, shifts[1:]))
-    ]
-
-    order = lax.rem(z + jnp.asarray(QUARTER_SHIFTS, jnp.int32), N_TP)
-    place, row = places_by_chips(self_index, hit_owner, hit_slot)
-    *gated, sending = advance(order, place, row, ret_owner, suffix_stretches, earlier, ready)
+    earlier, (ready, near_weight) = gather_by_chips(
+        earlier, (tokens, near_weight), lambda beside: (prepare(0, *beside[0]), beside[1])
+    )
+    core = lax.rem(lax.axis_index("cache"), 2)
+    far_weight = by_cores_along_tp(
+        lax.dynamic_slice(near_weight, (core * PAIR, 0), (PAIR, D))
+    )
+
+    *gated, sending = advance(
+        hit_owner, hit_slot, ret_owner, suffix_stretches, earlier, ready
+    )
     received = [lax.all_to_all(sending, "cache", split_axis=0, concat_axis=0, tiled=True)]
     others = [along_tp(rows, shift) for rows, shift in zip(gated[:3], shifts)]
     gated_parts = others + [gated[3]]
 
     tokens, _ = lax.optimization_barrier((tokens, sending))
     ready = prepare(1, *tokens)
-    later, far_weight, _ = lax.optimization_barrier((later, far_weight, others))
-    place = jnp.zeros_like(place)
-    row = jnp.repeat(hit_owner * stored_here + hit_slot, 2)
-    *gated, sending = advance(order, place, row, ret_owner, suffix_stretches, [later], ready)
+    *gated, sending = advance(
+        hit_owner, hit_slot, ret_owner, suffix_stretches, [later], ready
+    )
+    sending, far_weight, _ = lax.optimization_barrier((sending, far_weight, others))
     received.append(lax.all_to_all(sending, "cache", split_axis=0, concat_axis=0, tiled=True))
     gated_parts += [along_tp(rows, shift) for rows, shift in zip(gated[:3], shifts)] + [gated[3]]
 
-    direct = [*far_weight, *near_weights]
-    swapped = [to_sibling(weight) for weight in direct]
-    mixed = project(core.reshape(1), gated_parts, out_weight, direct, swapped)
-
-    source = locate(self_index.reshape(1), later)
+    weights = [near_weight, to_sibling(near_weight), far_weight, to_sibling(far_weight)]
+    mixed = project(gated_parts, out_weight, weights)
+
+    source = locate(later)
     new_ckpts = None
     for p in range(PAIRS):
         new_ckpts = unpack(p, source, received[p], new_ckpts)

time: 152 us -> 138 us (0.908)
  Pallas kernels: 58.6 us -> 51.1 us
  local copies, waits for them, and re-layouts: 10.2 us -> 3.76 us
  starting transfers between devices: 49.5 us -> 44.9 us
  waiting for transfers between devices: 17.6 us -> 22.1 us
    ppermute x10 -> x6, starting transfers between devices: 18.4 us -> 8.1 us  [along_tp(): return lax.ppermute(x, 'tp', [(z, (z + shift) % N_TP) for z in range(N_TP)])]
    ppermute x0 -> x2, starting transfers between devices: none -> 5.89 us  [by_cores_along_tp(): return lax.ppermute(x, ('cache', 'tp'), pairs)]
    pallas_call x5, Pallas kernels: 23.4 us -> 19.4 us  [the longest x1 9.71 us: project(): pl.pallas_call(project_kernel, grid=(TILES,), in_specs=[pl.BlockSpec((row...]
    ppermute x6, waiting for transfers between devices: 2.82 us -> 6.4 us  [along_chips(): return lax.ppermute(x, 'cache', pairs)]
    pallas_call x2, Pallas kernels: 19.9 us -> 16.5 us  [prepare(): pl.pallas_call(functools.partial(prepare_kernel, pair), grid=(R_DEV // RE...]
    ppermute x9 -> x6, starting transfers between devices: 4.94 us -> 2.25 us  [to_sibling(): return lax.ppermute(x, 'cache', [(i, i ^ 1) for i in range(CACHE)])]
    all_to_all x2, starting transfers between devices: 14.9 us -> 17.5 us  [body(): lax.all_to_all(sending, 'cache', split_axis=0, concat_axis=0, tiled=True)]
    slice x2 -> x0, local copies, waits for them, and re-layouts: 2.22 us -> none  [body(): weight[p * PAIR:(p + 1) * PAIR]]
  transfers between devices with their start and end apart: 28 -> 23, of which waited for: 11 -> 10; matrix products, arithmetic and copies ran while one was open for 6% -> 2% of each run, Pallas kernels for 35% -> 34%
where the time goes in v2:
time: 138 us; the launch traced here: 137 us
  Pallas kernels  51.1 us (37%)
  starting transfers between devices  44.9 us (33%)
  waiting for transfers between devices  22.1 us (16%)
  between operations  14.2 us (10%)
  local copies, waits for them, and re-layouts  3.76 us (3%)
    all_to_all x2, starting transfers between devices, body(): lax.all_to_all(sending, 'cache', split_axis=0, concat_axis=0, tiled=True)  17.5 us
    pallas_call x2, Pallas kernels, prepare(): pl.pallas_call(functools.partial(prepare_kernel, pair), grid=(R_DEV // RE...  16.5 us
    pallas_call x2, Pallas kernels, advance(): pl.pallas_call(advance_kernel, grid_spec=pltpu.PrefetchScalarGridSpec(num...  15.3 us
    ppermute x6, waiting for transfers between devices, along_tp(): return lax.ppermute(x, 'tp', [(z, (z + shift) % N_TP) for z in range(N_TP)])  11.5 us
    ppermute x6, starting transfers between devices, along_chips(): return lax.ppermute(x, 'cache', pairs)  11.1 us
    pallas_call x1, Pallas kernels, project(): pl.pallas_call(project_kernel, grid=(TILES,), in_specs=[pl.BlockSpec((row...  9.71 us
    ppermute x6, starting transfers between devices, along_tp(): return lax.ppermute(x, 'tp', [(z, (z + shift) % N_TP) for z in range(N_TP)])  8.1 us
    pallas_call x2, Pallas kernels, unpack(): pl.pallas_call(functools.partial(unpack_kernel, pair), grid_spec=pltpu.Pr...  6.5 us
  transfers between devices with their start and end apart: 23, of which 10 were waited for; matrix products, arithmetic and copies ran while one was open for 2% of the time, Pallas kernels for 34%

profile of v2, /device:TPU:1, one launch (start us, length us, event | category | flops | bytes accessed | tf_op | source)
XLA Modules:
  0.0 137.1 jit_solution(10299272145713743646)
XLA Ops:
  7.2 1.8 %pack.1 = (bf16[2,256,128]{2,1,0:T(8,128)(2,1)}, bf16[2,272,128]{2,1,0:T(8,128)(2,1)}) custom-call(s32[16]{0:T(128)} %ret_ref.3, f32[2,4,128,128]{3,2,1,0:T(8,128)} %store_ref.1), custom_call_target="tpu_custom_call" | custom-call | bytes 800000 | tf_op jit(solution)/shard_map/pack/pallas_call | solution.py:361
  9.0 4.7 %collective-permute-start.6 = (bf16[512,2304]{1,0:T(8,128)(2,1)}, bf16[512,2304]{1,0:T(8,128)(2,1)}, u32[]{:S(2)}, u32[]{:S(2)}) collective-permute-start(bf16[512,2304]{1,0:T(8,128)(2,1)} %refs_8_.1), channel_id=1, source_target_pairs={{0,1},{1,2},{2,3},{3,0},{4,7},{5,4},{6,5},{7,6},{8,9},{9,10},{10,1... | collective-permute-start | bytes 7077896 | tf_op jit(solution)/shard_map/ppermute | solution.py:509
  13.7 2.9 %collective-permute-start = (bf16[2,256,128]{2,1,0:T(8,128)(2,1)}, bf16[2,256,128]{2,1,0:T(8,128)(2,1)S(1)}, u32[]{:S(2)}, u32[]{:S(2)}) collective-permute-start(bf16[2,256,128]{2,1,0:T(8,128)(2,1)} %get-tuple-element.52), channel_id=1, source_target_pairs={{0,64},{4,20},{8,72},{12,28},{16,80},{20,4},{24,88},{28,12},{32,96... | collective-permute-start | bytes 393224 | tf_op jit(solution)/shard_map/ppermute | solution.py:525
  17.0 2.3 %collective-permute-start.2 = (bf16[2,256,128]{2,1,0:T(8,128)(2,1)}, bf16[2,256,128]{2,1,0:T(8,128)(2,1)S(1)}, u32[]{:S(2)}, u32[]{:S(2)}) collective-permute-start(bf16[2,256,128]{2,1,0:T(8,128)(2,1)} %get-tuple-element.52), channel_id=1, source_target_pairs={{0,96},{4,28},{8,104},{12,4},{16,112},{20,12},{24,120},{28,20},{32... | collective-permute-start | bytes 393224 | tf_op jit(solution)/shard_map/ppermute | solution.py:525
  19.3 3.0 %collective-permute-done.1 = bf16[2,256,128]{2,1,0:T(8,128)(2,1)S(1)} collective-permute-done((bf16[2,256,128]{2,1,0:T(8,128)(2,1)}, bf16[2,256,128]{2,1,0:T(8,128)(2,1)S(1)}, u32[]{:S(2)}, u32[]{:S(2)}) %collective-permute-start.1) | collective-permute-done | bytes 131104 | tf_op jit(solution)/shard_map/ppermute | solution.py:525
  23.2 2.8 %collective-permute-start.3 = (bf16[8,256,128]{2,1,0:T(8,128)(2,1)S(1)}, bf16[8,256,128]{2,1,0:T(8,128)(2,1)S(1)}, u32[]{:S(2)}, u32[]{:S(2)}) collective-permute-start(bf16[8,256,128]{2,1,0:T(8,128)(2,1)S(1)} %pad_maximum_fusion.refs_0_), channel_id=1, source_target_pairs={{0,16},{4,68},{8,24},{12,76},{16,0},{20,84},{24,8},{28,92},{32,48}... | collective-permute-start | bytes 1572872 | tf_op jit(solution)/shard_map/ppermute | solution.py:525
  26.3 2.4 %collective-permute-start.5 = (bf16[8,256,128]{2,1,0:T(8,128)(2,1)S(1)}, bf16[8,256,128]{2,1,0:T(8,128)(2,1)S(1)}, u32[]{:S(2)}, u32[]{:S(2)}) collective-permute-start(bf16[8,256,128]{2,1,0:T(8,128)(2,1)S(1)} %pad_maximum_fusion.refs_0_), channel_id=1, source_target_pairs={{0,24},{4,100},{8,0},{12,108},{16,8},{20,116},{24,16},{28,124},{32... | collective-permute-start | bytes 1572872 | tf_op jit(solution)/shard_map/ppermute | solution.py:525
  29.4 8.2 %prepare.2 = (bf16[16,2,128,256]{3,2,1,0:T(8,128)(2,1)}, bf16[16,2,64,256]{3,2,1,0:T(8,128)(2,1)}, bf16[16,2,192,128]{3,2,1,0:T(8,128)(2,1)}, f32[128,128]{1,0:T(8,128)}, bf16[2048,256]{1,0:T(8,128)(2,1)}) custom-call(bf16[2048,512]{1,0:T(8,128)(2,1)} %q_ref.1, bf16[2048,512]{1,0:T(8,128)(2,1)} %k_ref.1, bf16[2048,512]{1,0:T(8,128)(2,1)} %v_ref.1, ...), custom_call_target="tpu_custom_call" | custom-call | flops 400000000 | bytes 14000000 | tf_op jit(solution)/shard_map/prepare/pallas_call | solution.py:389
  37.7 3.4 %collective-permute-done.4.refs_2_ = bf16[8,256,128]{2,1,0:T(8,128)(2,1)S(1)} collective-permute-done((bf16[8,256,128]{2,1,0:T(8,128)(2,1)S(1)}, bf16[8,256,128]{2,1,0:T(8,128)(2,1)S(1)}, u32[]{:S(2)}, u32[]{:S(2)}) %collective-permute-start.4) | collective-permute-done | bytes 524320 | tf_op jit(solution)/shard_map/ppermute | solution.py:525
  43.3 1.5 %collective-permute-done.8.refs_5_ = bf16[8,256,128]{2,1,0:T(8,128)(2,1)S(1)} collective-permute-done((bf16[8,256,128]{2,1,0:T(8,128)(2,1)S(1)}, bf16[8,256,128]{2,1,0:T(8,128)(2,1)S(1)}, u32[]{:S(2)}, u32[]{:S(2)}) %collective-permute-start.8) | collective-permute-done | bytes 524320 | tf_op jit(solution)/shard_map/ppermute | solution.py:513
  45.6 7.5 %advance.2 = (bf16[512,256]{1,0:T(8,128)(2,1)}, bf16[512,256]{1,0:T(8,128)(2,1)}, bf16[512,256]{1,0:T(8,128)(2,1)}, bf16[512,256]{1,0:T(8,128)(2,1)}, bf16[32,256,128]{2,1,0:T(8,128)(2,1)}) custom-call(s32[16]{0:T(128)} %owner_ref.5, s32[16]{0:T(128)} %slot_ref.3, s32[16]{0:T(128)} %ret_ref.3, s32[16]{0:T(128)} %counts_ref.3, ...), custom_call_target="tpu_custom_call" | custom-call | flops 500000000 | bytes 10000000 | tf_op jit(solution)/shard_map/advance/pallas_call | solution.py:424
  53.1 8.0 %all-to-all-start.1 = ((bf16[32,256,128]{2,1,0:T(8,128)(2,1)}), bf16[32,256,128]{2,1,0:T(8,128)(2,1)S(1)}, u32[]{:S(2)}, u32[]{:S(2)}) async-start(bf16[32,256,128]{2,1,0:T(8,128)(2,1)} %get-tuple-element.80), calls=%async_computation.1 | async-start | bytes 4194304 | tf_op jit(solution)/shard_map/all_to_all | solution.py:583
  63.7 1.8 %collective-permute-start.11 = (bf16[512,256]{1,0:T(8,128)(2,1)}, bf16[512,256]{1,0:T(8,128)(2,1)}, u32[]{:S(2)}, u32[]{:S(2)}) collective-permute-start(bf16[512,256]{1,0:T(8,128)(2,1)} %get-tuple-element.75), channel_id=1, source_target_pairs={{0,2},{1,3},{2,0},{3,1},{4,6},{5,7},{6,4},{7,5},{8,10},{9,11},{10,... | collective-permute-start | bytes 786440 | tf_op jit(solution)/shard_map/ppermute | solution.py:500
  66.4 1.8 %collective-permute-start.13 = (bf16[512,256]{1,0:T(8,128)(2,1)S(1)}, bf16[512,256]{1,0:T(8,128)(2,1)}, u32[]{:S(2)}, u32[]{:S(2)}) collective-permute-start(bf16[512,256]{1,0:T(8,128)(2,1)S(1)} %copy-done.10), channel_id=1, source_target_pairs={{0,3},{1,0},{2,1},{3,2},{4,7},{5,4},{6,5},{7,6},{8,11},{9,8},{10,9... | collective-permute-start | bytes 786440 | tf_op jit(solution)/shard_map/ppermute | solution.py:500
  68.2 8.2 %prepare.3 = (bf16[16,2,128,256]{3,2,1,0:T(8,128)(2,1)}, bf16[16,2,64,256]{3,2,1,0:T(8,128)(2,1)}, bf16[16,2,192,128]{3,2,1,0:T(8,128)(2,1)}, f32[128,128]{1,0:T(8,128)}, bf16[2048,256]{1,0:T(8,128)(2,1)}) custom-call(bf16[2048,512]{1,0:T(8,128)(2,1)} %q_ref.1, bf16[2048,512]{1,0:T(8,128)(2,1)} %k_ref.1, bf16[2048,512]{1,0:T(8,128)(2,1)} %v_ref.1, ...), custom_call_target="tpu_custom_call" | custom-call | flops 400000000 | bytes 14000000 | tf_op jit(solution)/shard_map/prepare/pallas_call | solution.py:389
  76.4 7.8 %advance.3 = (bf16[512,256]{1,0:T(8,128)(2,1)}, bf16[512,256]{1,0:T(8,128)(2,1)}, bf16[512,256]{1,0:T(8,128)(2,1)}, bf16[512,256]{1,0:T(8,128)(2,1)}, bf16[32,256,128]{2,1,0:T(8,128)(2,1)}) custom-call(s32[16]{0:T(128)} %owner_ref.5, s32[16]{0:T(128)} %slot_ref.3, s32[16]{0:T(128)} %ret_ref.3, s32[16]{0:T(128)} %counts_ref.3, ...), custom_call_target="tpu_custom_call" | custom-call | flops 500000000 | bytes 10000000 | tf_op jit(solution)/shard_map/advance/pallas_call | solution.py:424
  84.3 5.0 %collective-permute-done.13.refs_2_ = bf16[512,256]{1,0:T(8,128)(2,1)} collective-permute-done((bf16[512,256]{1,0:T(8,128)(2,1)S(1)}, bf16[512,256]{1,0:T(8,128)(2,1)}, u32[]{:S(2)}, u32[]{:S(2)}) %collective-permute-start.13) | collective-permute-done | bytes 262176 | tf_op jit(solution)/shard_map/ppermute | solution.py:500
  89.4 9.5 %all-to-all-start = ((bf16[32,256,128]{2,1,0:T(8,128)(2,1)}), bf16[32,256,128]{2,1,0:T(8,128)(2,1)}, u32[]{:S(2)}, u32[]{:S(2)}) async-start(bf16[32,256,128]{2,1,0:T(8,128)(2,1)} %get-tuple-element.101), calls=%async_computation | async-start | bytes 4194304 | tf_op jit(solution)/shard_map/all_to_all | solution.py:593
  100.3 2.7 %collective-permute-start.16 = (bf16[512,256]{1,0:T(8,128)(2,1)S(1)}, bf16[512,256]{1,0:T(8,128)(2,1)}, u32[]{:S(2)}, u32[]{:S(2)}) collective-permute-start(bf16[512,256]{1,0:T(8,128)(2,1)S(1)} %copy-done.11), channel_id=1, source_target_pairs={{0,3},{1,0},{2,1},{3,2},{4,7},{5,4},{6,5},{7,6},{8,11},{9,8},{10,9... | collective-permute-start | bytes 786440 | tf_op jit(solution)/shard_map/ppermute | solution.py:500
  105.0 3.5 %unpack.2.refs_0_ = f32[16,512,128]{2,1,0:T(8,128)} custom-call(s32[128]{0:T(128)S(1)} %bitcast.6, bf16[32,256,128]{2,1,0:T(8,128)(2,1)S(1)} %all-to-all-done.1.received_ref), custom_call_target="tpu_custom_call" | custom-call | bytes 3200000 | tf_op jit(solution)/shard_map/unpack/pallas_call | solution.py:477
  108.9 6.1 %collective-permute-done.15.refs_5_ = bf16[512,256]{1,0:T(8,128)(2,1)S(1)} collective-permute-done((bf16[512,256]{1,0:T(8,128)(2,1)}, bf16[512,256]{1,0:T(8,128)(2,1)S(1)}, u32[]{:S(2)}, u32[]{:S(2)}) %collective-permute-start.15) | collective-permute-done | bytes 262176 | tf_op jit(solution)/shard_map/ppermute | solution.py:500
  116.1 9.7 %project.1 = bf16[512,2304]{1,0:T(8,128)(2,1)} custom-call(bf16[512,256]{1,0:T(8,128)(2,1)} %collective-permute-done.11.refs_0_, bf16[512,256]{1,0:T(8,128)(2,1)} %collective-permute-done.12.refs_1_, bf16[512,256]{1,0:T(8,128)(2,1)} %collective-permute-done.13.refs_2_, bf16[512,256]{1,0:T(8,128)(2,1)} %get-tuple-element.78.refs_3_, ...), custom_call_target="tpu_custom_call" | custom-call | flops 4800000000 | bytes 14000000 | tf_op jit(solution)/shard_map/project/pallas_call | solution.py:460
  125.8 1.5 %all-to-all-done.received_ref = bf16[32,256,128]{2,1,0:T(8,128)(2,1)} async-done(((bf16[32,256,128]{2,1,0:T(8,128)(2,1)}), bf16[32,256,128]{2,1,0:T(8,128)(2,1)}, u32[]{:S(2)}, u32[]{:S(2)}) %all-to-all-start) | async-done | bytes 2097184 | tf_op jit(solution)/shard_map/all_to_all | solution.py:593
  127.3 3.0 %unpack.3 = f32[16,512,128]{2,1,0:T(8,128)} custom-call(s32[128]{0:T(128)S(1)} %bitcast.7, bf16[32,256,128]{2,1,0:T(8,128)(2,1)} %all-to-all-done.received_ref, f32[16,512,128]{2,1,0:T(8,128)} %unpack.2.refs_0_), custom_call_target="tpu_custom_call", output_to_operand_aliasing={{}: (2, {})} | custom-call | bytes 3200000 | tf_op jit(solution)/shard_map/unpack/pallas_call | solution.py:477
  (62 shorter events, 13.9 us)
Async XLA Ops:
  7.2 69.3 %all-gather.2.cloned.1.call-start = ((), (), s32[]{:S(2)}) async-start(), calls=%async_computation.2 | async-start | bytes 4595712 | tf_op jit(solution)/shard_map/all_gather | solution.py:557
  9.0 32.1 %collective-permute-start.6 = (bf16[512,2304]{1,0:T(8,128)(2,1)}, bf16[512,2304]{1,0:T(8,128)(2,1)}, u32[]{:S(2)}, u32[]{:S(2)}) collective-permute-start(bf16[512,2304]{1,0:T(8,128)(2,1)} %refs_8_.1), channel_id=1, source_target_pairs={{0,1},{1,2},{2,3},{3,0},{4,7},{5,4},{6,5},{7,6},{8,9},{9,10},{10,1... | collective-permute-start | bytes 7077896 | tf_op jit(solution)/shard_map/ppermute | solution.py:509
  13.7 5.6 %collective-permute-start = (bf16[2,256,128]{2,1,0:T(8,128)(2,1)}, bf16[2,256,128]{2,1,0:T(8,128)(2,1)S(1)}, u32[]{:S(2)}, u32[]{:S(2)}) collective-permute-start(bf16[2,256,128]{2,1,0:T(8,128)(2,1)} %get-tuple-element.52), channel_id=1, source_target_pairs={{0,64},{4,20},{8,72},{12,28},{16,80},{20,4},{24,88},{28,12},{32,96... | collective-permute-start | bytes 393224 | tf_op jit(solution)/shard_map/ppermute | solution.py:525
  16.6 5.6 %collective-permute-start.1 = (bf16[2,256,128]{2,1,0:T(8,128)(2,1)}, bf16[2,256,128]{2,1,0:T(8,128)(2,1)S(1)}, u32[]{:S(2)}, u32[]{:S(2)}) collective-permute-start(bf16[2,256,128]{2,1,0:T(8,128)(2,1)} %get-tuple-element.52), channel_id=1, source_target_pairs={{0,32},{4,12},{8,40},{12,20},{16,48},{20,28},{24,56},{28,4},{32,64... | collective-permute-start | bytes 393224 | tf_op jit(solution)/shard_map/ppermute | solution.py:525
  17.0 5.2 %collective-permute-start.2 = (bf16[2,256,128]{2,1,0:T(8,128)(2,1)}, bf16[2,256,128]{2,1,0:T(8,128)(2,1)S(1)}, u32[]{:S(2)}, u32[]{:S(2)}) collective-permute-start(bf16[2,256,128]{2,1,0:T(8,128)(2,1)} %get-tuple-element.52), channel_id=1, source_target_pairs={{0,96},{4,28},{8,104},{12,4},{16,112},{20,12},{24,120},{28,20},{32... | collective-permute-start | bytes 393224 | tf_op jit(solution)/shard_map/ppermute | solution.py:525
  23.2 14.4 %copy-start.2 = (bf16[8,256,128]{2,1,0:T(8,128)(2,1)}, bf16[8,256,128]{2,1,0:T(8,128)(2,1)S(1)}, u32[]{:S(2)}) copy-start(bf16[8,256,128]{2,1,0:T(8,128)(2,1)S(1)} %pad_maximum_fusion.refs_0_) | copy-start | bytes 1572868
  23.2 14.4 %collective-permute-start.3 = (bf16[8,256,128]{2,1,0:T(8,128)(2,1)S(1)}, bf16[8,256,128]{2,1,0:T(8,128)(2,1)S(1)}, u32[]{:S(2)}, u32[]{:S(2)}) collective-permute-start(bf16[8,256,128]{2,1,0:T(8,128)(2,1)S(1)} %pad_maximum_fusion.refs_0_), channel_id=1, source_target_pairs={{0,16},{4,68},{8,24},{12,76},{16,0},{20,84},{24,8},{28,92},{32,48}... | collective-permute-start | bytes 1572872 | tf_op jit(solution)/shard_map/ppermute | solution.py:525
  26.0 15.1 %collective-permute-start.4 = (bf16[8,256,128]{2,1,0:T(8,128)(2,1)S(1)}, bf16[8,256,128]{2,1,0:T(8,128)(2,1)S(1)}, u32[]{:S(2)}, u32[]{:S(2)}) collective-permute-start(bf16[8,256,128]{2,1,0:T(8,128)(2,1)S(1)} %pad_maximum_fusion.refs_0_), channel_id=1, source_target_pairs={{0,8},{4,36},{8,16},{12,44},{16,24},{20,52},{24,0},{28,60},{32,40}... | collective-permute-start | bytes 1572872 | tf_op jit(solution)/shard_map/ppermute | solution.py:525
  26.3 14.8 %collective-permute-start.5 = (bf16[8,256,128]{2,1,0:T(8,128)(2,1)S(1)}, bf16[8,256,128]{2,1,0:T(8,128)(2,1)S(1)}, u32[]{:S(2)}, u32[]{:S(2)}) collective-permute-start(bf16[8,256,128]{2,1,0:T(8,128)(2,1)S(1)} %pad_maximum_fusion.refs_0_), channel_id=1, source_target_pairs={{0,24},{4,100},{8,0},{12,108},{16,8},{20,116},{24,16},{28,124},{32... | collective-permute-start | bytes 1572872 | tf_op jit(solution)/shard_map/ppermute | solution.py:525
  28.7 13.6 %collective-permute-start.7 = (bf16[8,256,128]{2,1,0:T(8,128)(2,1)S(1)}, bf16[8,256,128]{2,1,0:T(8,128)(2,1)S(1)}, u32[]{:S(2)}, u32[]{:S(2)}) collective-permute-start(bf16[8,256,128]{2,1,0:T(8,128)(2,1)S(1)} %pad_maximum_fusion.refs_0_), channel_id=1, source_target_pairs={{0,4},{4,0},{8,12},{12,8},{16,20},{20,16},{24,28},{28,24},{32,36},... | collective-permute-start | bytes 1572872 | tf_op jit(solution)/shard_map/ppermute | solution.py:513
  41.1 2.2 %collective-permute-start.10 = (bf16[8,256,128]{2,1,0:T(8,128)(2,1)S(1)}, bf16[8,256,128]{2,1,0:T(8,128)(2,1)S(1)}, u32[]{:S(2)}, u32[]{:S(2)}) collective-permute-start(bf16[8,256,128]{2,1,0:T(8,128)(2,1)S(1)} %collective-permute-done.5.refs_3_), channel_id=1, source_target_pairs={{0,4},{4,0},{8,12},{12,8},{16,20},{20,16},{24,28},{28,24},{32,36},... | collective-permute-start | bytes 1572872 | tf_op jit(solution)/shard_map/ppermute | solution.py:513
  41.8 3.0 %collective-permute-start.8 = (bf16[8,256,128]{2,1,0:T(8,128)(2,1)S(1)}, bf16[8,256,128]{2,1,0:T(8,128)(2,1)S(1)}, u32[]{:S(2)}, u32[]{:S(2)}) collective-permute-start(bf16[8,256,128]{2,1,0:T(8,128)(2,1)S(1)} %collective-permute-done.3.refs_1_), channel_id=1, source_target_pairs={{0,4},{4,0},{8,12},{12,8},{16,20},{20,16},{24,28},{28,24},{32,36},... | collective-permute-start | bytes 1572872 | tf_op jit(solution)/shard_map/ppermute | solution.py:513
  41.8 3.2 %collective-permute-start.9 = (bf16[8,256,128]{2,1,0:T(8,128)(2,1)S(1)}, bf16[8,256,128]{2,1,0:T(8,128)(2,1)}, u32[]{:S(2)}, u32[]{:S(2)}) collective-permute-start(bf16[8,256,128]{2,1,0:T(8,128)(2,1)S(1)} %collective-permute-done.4.refs_2_), channel_id=1, source_target_pairs={{0,4},{4,0},{8,12},{12,8},{16,20},{20,16},{24,28},{28,24},{32,36},... | collective-permute-start | bytes 1572872 | tf_op jit(solution)/shard_map/ppermute | solution.py:513
  53.1 36.3 %all-to-all-start.1 = ((bf16[32,256,128]{2,1,0:T(8,128)(2,1)}), bf16[32,256,128]{2,1,0:T(8,128)(2,1)S(1)}, u32[]{:S(2)}, u32[]{:S(2)}) async-start(bf16[32,256,128]{2,1,0:T(8,128)(2,1)} %get-tuple-element.80), calls=%async_computation.1 | async-start | bytes 4194304 | tf_op jit(solution)/shard_map/all_to_all | solution.py:583
  62.5 26.8 %collective-permute-start.18 = (bf16[256,2304]{1,0:T(8,128)(2,1)S(1)}, bf16[256,2304]{1,0:T(8,128)(2,1)}, u32[]{:S(2)}, u32[]{:S(2)}) collective-permute-start(bf16[256,2304]{1,0:T(8,128)(2,1)S(1)} %constant_dynamic-slice_fusion), channel_id=1, source_target_pairs={{0,1},{1,2},{2,3},{3,0},{4,7},{5,4},{6,5},{7,6},{8,9},{9,10},{10,1... | collective-permute-start | bytes 3538952 | tf_op jit(solution)/shard_map/ppermute | solution.py:509
  63.7 44.8 %collective-permute-start.17 = (bf16[512,2304]{1,0:T(8,128)(2,1)}, bf16[512,2304]{1,0:T(8,128)(2,1)}, u32[]{:S(2)}, u32[]{:S(2)}) collective-permute-start(bf16[512,2304]{1,0:T(8,128)(2,1)} %collective-permute-done.6.refs_9_), channel_id=1, source_target_pairs={{0,4},{4,0},{8,12},{12,8},{16,20},{20,16},{24,28},{28,24},{32,36},... | collective-permute-start | bytes 7077896 | tf_op jit(solution)/shard_map/ppermute | solution.py:513
  63.7 20.5 %collective-permute-start.11 = (bf16[512,256]{1,0:T(8,128)(2,1)}, bf16[512,256]{1,0:T(8,128)(2,1)}, u32[]{:S(2)}, u32[]{:S(2)}) collective-permute-start(bf16[512,256]{1,0:T(8,128)(2,1)} %get-tuple-element.75), channel_id=1, source_target_pairs={{0,2},{1,3},{2,0},{3,1},{4,6},{5,7},{6,4},{7,5},{8,10},{9,11},{10,... | collective-permute-start | bytes 786440 | tf_op jit(solution)/shard_map/ppermute | solution.py:500
  65.5 18.8 %collective-permute-start.12 = (bf16[512,256]{1,0:T(8,128)(2,1)}, bf16[512,256]{1,0:T(8,128)(2,1)}, u32[]{:S(2)}, u32[]{:S(2)}) collective-permute-start(bf16[512,256]{1,0:T(8,128)(2,1)} %get-tuple-element.76), channel_id=1, source_target_pairs={{0,1},{1,2},{2,3},{3,0},{4,5},{5,6},{6,7},{7,4},{8,9},{9,10},{10,1... | collective-permute-start | bytes 786440 | tf_op jit(solution)/shard_map/ppermute | solution.py:500
  66.4 23.0 %collective-permute-start.13 = (bf16[512,256]{1,0:T(8,128)(2,1)S(1)}, bf16[512,256]{1,0:T(8,128)(2,1)}, u32[]{:S(2)}, u32[]{:S(2)}) collective-permute-start(bf16[512,256]{1,0:T(8,128)(2,1)S(1)} %copy-done.10), channel_id=1, source_target_pairs={{0,3},{1,0},{2,1},{3,2},{4,7},{5,4},{6,5},{7,6},{8,11},{9,8},{10,9... | collective-permute-start | bytes 786440 | tf_op jit(solution)/shard_map/ppermute | solution.py:500
  89.4 37.9 %all-to-all-start = ((bf16[32,256,128]{2,1,0:T(8,128)(2,1)}), bf16[32,256,128]{2,1,0:T(8,128)(2,1)}, u32[]{:S(2)}, u32[]{:S(2)}) async-start(bf16[32,256,128]{2,1,0:T(8,128)(2,1)} %get-tuple-element.101), calls=%async_computation | async-start | bytes 4194304 | tf_op jit(solution)/shard_map/all_to_all | solution.py:593
  98.9 16.1 %collective-permute-start.19 = (bf16[256,2304]{1,0:T(8,128)(2,1)}, bf16[256,2304]{1,0:T(8,128)(2,1)S(1)}, u32[]{:S(2)}, u32[]{:S(2)}) collective-permute-start(bf16[256,2304]{1,0:T(8,128)(2,1)} %collective-permute-done.18.refs_11_), channel_id=1, source_target_pairs={{0,4},{4,0},{8,12},{12,8},{16,20},{20,16},{24,28},{28,24},{32,36},... | collective-permute-start | bytes 3538952 | tf_op jit(solution)/shard_map/ppermute | solution.py:513
  99.3 9.6 %collective-permute-start.14 = (bf16[512,256]{1,0:T(8,128)(2,1)}, bf16[512,256]{1,0:T(8,128)(2,1)S(1)}, u32[]{:S(2)}, u32[]{:S(2)}) collective-permute-start(bf16[512,256]{1,0:T(8,128)(2,1)} %get-tuple-element.94), channel_id=1, source_target_pairs={{0,2},{1,3},{2,0},{3,1},{4,6},{5,7},{6,4},{7,5},{8,10},{9,11},{10,... | collective-permute-start | bytes 786440 | tf_op jit(solution)/shard_map/ppermute | solution.py:500
  100.3 14.7 %collective-permute-start.15 = (bf16[512,256]{1,0:T(8,128)(2,1)}, bf16[512,256]{1,0:T(8,128)(2,1)S(1)}, u32[]{:S(2)}, u32[]{:S(2)}) collective-permute-start(bf16[512,256]{1,0:T(8,128)(2,1)} %get-tuple-element.95), channel_id=1, source_target_pairs={{0,1},{1,2},{2,3},{3,0},{4,5},{5,6},{6,7},{7,4},{8,9},{9,10},{10,1... | collective-permute-start | bytes 786440 | tf_op jit(solution)/shard_map/ppermute | solution.py:500
  100.3 14.7 %collective-permute-start.16 = (bf16[512,256]{1,0:T(8,128)(2,1)S(1)}, bf16[512,256]{1,0:T(8,128)(2,1)}, u32[]{:S(2)}, u32[]{:S(2)}) collective-permute-start(bf16[512,256]{1,0:T(8,128)(2,1)S(1)} %copy-done.11), channel_id=1, source_target_pairs={{0,3},{1,0},{2,1},{3,2},{4,7},{5,4},{6,5},{7,6},{8,11},{9,8},{10,9... | collective-permute-start | bytes 786440 | tf_op jit(solution)/shard_map/ppermute | solution.py:500
  (13 other events, 56.0 us)
Sparse Core Ops, SparseCore 0:
  10.2 54.6 all-gather.1

commit v3 on v2

--- a/solution.py
+++ b/solution.py
@@ -556,7 +556,8 @@
     earlier, later = pack(ret_owner, ckpt_store)
     later = lax.all_gather(later, "cache", axis=0, tiled=True)
 
-    near_weight = by_cores_along_tp(out_weight)
+    earlier, weight = lax.optimization_barrier((earlier, out_weight))
+    near_weight = by_cores_along_tp(weight)
     shifts = QUARTER_SHIFTS[:3]
 
     tokens = (
@@ -589,7 +590,7 @@
     *gated, sending = advance(
         hit_owner, hit_slot, ret_owner, suffix_stretches, [later], ready
     )
-    sending, far_weight, _ = lax.optimization_barrier((sending, far_weight, others))
+    sending, far_weight, _ = lax.optimization_barrier((sending, far_weight, others[1:]))
     received.append(lax.all_to_all(sending, "cache", split_axis=0, concat_axis=0, tiled=True))
     gated_parts += [along_tp(rows, shift) for rows, shift in zip(gated[:3], shifts)] + [gated[3]]
 

time: 138 us -> 138 us (level)
  starting transfers between devices: 44.9 us -> 40.4 us
  waiting for transfers between devices: 22.1 us -> 25.5 us
    all_to_all x2, starting transfers between devices: 17.5 us -> 12.6 us  [body(): lax.all_to_all(sending, 'cache', split_axis=0, concat_axis=0, tiled=True)]
    all_to_all x2, waiting for transfers between devices: 1.53 us -> 5.88 us  [body(): lax.all_to_all(sending, 'cache', split_axis=0, concat_axis=0, tiled=True)]
  transfers between devices with their start and end apart: 23 -> 23, of which waited for: 10 -> 9; matrix products, arithmetic and copies ran while one was open for 2% -> 2% of each run, Pallas kernels for 34% -> 34%
where the time goes in v3:
time: 138 us; the launch traced here: 137 us
  Pallas kernels  51.5 us (37%)
  starting transfers between devices  40.4 us (29%)
  waiting for transfers between devices  25.5 us (18%)
  between operations  14.2 us (10%)
  local copies, waits for them, and re-layouts  3.84 us (3%)
    pallas_call x2, Pallas kernels, prepare(): pl.pallas_call(functools.partial(prepare_kernel, pair), grid=(R_DEV // RE...  16.5 us
    pallas_call x2, Pallas kernels, advance(): pl.pallas_call(advance_kernel, grid_spec=pltpu.PrefetchScalarGridSpec(num...  15.5 us
    all_to_all x2, starting transfers between devices, body(): lax.all_to_all(sending, 'cache', split_axis=0, concat_axis=0, tiled=True)  12.6 us
    ppermute x6, starting transfers between devices, along_chips(): return lax.ppermute(x, 'cache', pairs)  11.1 us
    ppermute x6, waiting for transfers between devices, along_tp(): return lax.ppermute(x, 'tp', [(z, (z + shift) % N_TP) for z in range(N_TP)])  10.6 us
    pallas_call x1, Pallas kernels, project(): pl.pallas_call(project_kernel, grid=(TILES,), in_specs=[pl.BlockSpec((row...  9.71 us
    ppermute x6, starting transfers between devices, along_tp(): return lax.ppermute(x, 'tp', [(z, (z + shift) % N_TP) for z in range(N_TP)])  8.05 us
    pallas_call x2, Pallas kernels, unpack(): pl.pallas_call(functools.partial(unpack_kernel, pair), grid_spec=pltpu.Pr...  6.51 us
  transfers between devices with their start and end apart: 23, of which 9 were waited for; matrix products, arithmetic and copies ran while one was open for 2% of the time, Pallas kernels for 34%

profile of v3, /device:TPU:1, one launch (start us, length us, event | category | flops | bytes accessed | tf_op | source)
XLA Modules:
  0.0 136.5 jit_solution(3352763917248818632)
XLA Ops:
  7.2 1.8 %pack.1 = (bf16[2,256,128]{2,1,0:T(8,128)(2,1)}, bf16[2,272,128]{2,1,0:T(8,128)(2,1)}) custom-call(s32[16]{0:T(128)} %ret_ref.3, f32[2,4,128,128]{3,2,1,0:T(8,128)} %store_ref.1), custom_call_target="tpu_custom_call" | custom-call | bytes 800000 | tf_op jit(solution)/shard_map/pack/pallas_call | solution.py:361
  9.0 4.7 %collective-permute-start.6 = (bf16[512,2304]{1,0:T(8,128)(2,1)}, bf16[512,2304]{1,0:T(8,128)(2,1)}, u32[]{:S(2)}, u32[]{:S(2)}) collective-permute-start(bf16[512,2304]{1,0:T(8,128)(2,1)} %refs_8_.1), channel_id=1, source_target_pairs={{0,1},{1,2},{2,3},{3,0},{4,7},{5,4},{6,5},{7,6},{8,9},{9,10},{10,1... | collective-permute-start | bytes 7077896 | tf_op jit(solution)/shard_map/ppermute | solution.py:509
  13.7 2.9 %collective-permute-start = (bf16[2,256,128]{2,1,0:T(8,128)(2,1)}, bf16[2,256,128]{2,1,0:T(8,128)(2,1)S(1)}, u32[]{:S(2)}, u32[]{:S(2)}) collective-permute-start(bf16[2,256,128]{2,1,0:T(8,128)(2,1)} %get-tuple-element.55), channel_id=1, source_target_pairs={{0,64},{4,20},{8,72},{12,28},{16,80},{20,4},{24,88},{28,12},{32,96... | collective-permute-start | bytes 393224 | tf_op jit(solution)/shard_map/ppermute | solution.py:525
  17.0 2.3 %collective-permute-start.2 = (bf16[2,256,128]{2,1,0:T(8,128)(2,1)}, bf16[2,256,128]{2,1,0:T(8,128)(2,1)S(1)}, u32[]{:S(2)}, u32[]{:S(2)}) collective-permute-start(bf16[2,256,128]{2,1,0:T(8,128)(2,1)} %get-tuple-element.55), channel_id=1, source_target_pairs={{0,96},{4,28},{8,104},{12,4},{16,112},{20,12},{24,120},{28,20},{32... | collective-permute-start | bytes 393224 | tf_op jit(solution)/shard_map/ppermute | solution.py:525
  19.3 3.0 %collective-permute-done.1 = bf16[2,256,128]{2,1,0:T(8,128)(2,1)S(1)} collective-permute-done((bf16[2,256,128]{2,1,0:T(8,128)(2,1)}, bf16[2,256,128]{2,1,0:T(8,128)(2,1)S(1)}, u32[]{:S(2)}, u32[]{:S(2)}) %collective-permute-start.1) | collective-permute-done | bytes 131104 | tf_op jit(solution)/shard_map/ppermute | solution.py:525
  23.2 2.8 %collective-permute-start.3 = (bf16[8,256,128]{2,1,0:T(8,128)(2,1)S(1)}, bf16[8,256,128]{2,1,0:T(8,128)(2,1)S(1)}, u32[]{:S(2)}, u32[]{:S(2)}) collective-permute-start(bf16[8,256,128]{2,1,0:T(8,128)(2,1)S(1)} %pad_maximum_fusion.refs_0_), channel_id=1, source_target_pairs={{0,16},{4,68},{8,24},{12,76},{16,0},{20,84},{24,8},{28,92},{32,48}... | collective-permute-start | bytes 1572872 | tf_op jit(solution)/shard_map/ppermute | solution.py:525
  26.4 2.4 %collective-permute-start.5 = (bf16[8,256,128]{2,1,0:T(8,128)(2,1)S(1)}, bf16[8,256,128]{2,1,0:T(8,128)(2,1)S(1)}, u32[]{:S(2)}, u32[]{:S(2)}) collective-permute-start(bf16[8,256,128]{2,1,0:T(8,128)(2,1)S(1)} %pad_maximum_fusion.refs_0_), channel_id=1, source_target_pairs={{0,24},{4,100},{8,0},{12,108},{16,8},{20,116},{24,16},{28,124},{32... | collective-permute-start | bytes 1572872 | tf_op jit(solution)/shard_map/ppermute | solution.py:525
  29.4 8.2 %prepare.2 = (bf16[16,2,128,256]{3,2,1,0:T(8,128)(2,1)}, bf16[16,2,64,256]{3,2,1,0:T(8,128)(2,1)}, bf16[16,2,192,128]{3,2,1,0:T(8,128)(2,1)}, f32[128,128]{1,0:T(8,128)}, bf16[2048,256]{1,0:T(8,128)(2,1)}) custom-call(bf16[2048,512]{1,0:T(8,128)(2,1)} %q_ref.1, bf16[2048,512]{1,0:T(8,128)(2,1)} %k_ref.1, bf16[2048,512]{1,0:T(8,128)(2,1)} %v_ref.1, ...), custom_call_target="tpu_custom_call" | custom-call | flops 400000000 | bytes 14000000 | tf_op jit(solution)/shard_map/prepare/pallas_call | solution.py:389
  37.7 3.4 %collective-permute-done.4.refs_2_ = bf16[8,256,128]{2,1,0:T(8,128)(2,1)S(1)} collective-permute-done((bf16[8,256,128]{2,1,0:T(8,128)(2,1)S(1)}, bf16[8,256,128]{2,1,0:T(8,128)(2,1)S(1)}, u32[]{:S(2)}, u32[]{:S(2)}) %collective-permute-start.4) | collective-permute-done | bytes 524320 | tf_op jit(solution)/shard_map/ppermute | solution.py:525
  45.6 7.7 %advance.2 = (bf16[512,256]{1,0:T(8,128)(2,1)}, bf16[512,256]{1,0:T(8,128)(2,1)}, bf16[512,256]{1,0:T(8,128)(2,1)}, bf16[512,256]{1,0:T(8,128)(2,1)}, bf16[32,256,128]{2,1,0:T(8,128)(2,1)}) custom-call(s32[16]{0:T(128)} %owner_ref.5, s32[16]{0:T(128)} %slot_ref.3, s32[16]{0:T(128)} %ret_ref.3, s32[16]{0:T(128)} %counts_ref.3, ...), custom_call_target="tpu_custom_call" | custom-call | flops 500000000 | bytes 10000000 | tf_op jit(solution)/shard_map/advance/pallas_call | solution.py:424
  53.4 7.4 %all-to-all-start.1 = ((bf16[32,256,128]{2,1,0:T(8,128)(2,1)}), bf16[32,256,128]{2,1,0:T(8,128)(2,1)S(1)}, u32[]{:S(2)}, u32[]{:S(2)}) async-start(bf16[32,256,128]{2,1,0:T(8,128)(2,1)} %get-tuple-element.84), calls=%async_computation.1 | async-start | bytes 4194304 | tf_op jit(solution)/shard_map/all_to_all | solution.py:584
  62.1 1.6 %collective-permute-start.18 = (bf16[256,2304]{1,0:T(8,128)(2,1)S(1)}, bf16[256,2304]{1,0:T(8,128)(2,1)}, u32[]{:S(2)}, u32[]{:S(2)}) collective-permute-start(bf16[256,2304]{1,0:T(8,128)(2,1)S(1)} %constant_dynamic-slice_fusion), channel_id=1, source_target_pairs={{0,1},{1,2},{2,3},{3,0},{4,7},{5,4},{6,5},{7,6},{8,9},{9,10},{10,1... | collective-permute-start | bytes 3538952 | tf_op jit(solution)/shard_map/ppermute | solution.py:509
  64.7 1.7 %collective-permute-start.13 = (bf16[512,256]{1,0:T(8,128)(2,1)}, bf16[512,256]{1,0:T(8,128)(2,1)}, u32[]{:S(2)}, u32[]{:S(2)}) collective-permute-start(bf16[512,256]{1,0:T(8,128)(2,1)} %get-tuple-element.81), channel_id=1, source_target_pairs={{0,3},{1,0},{2,1},{3,2},{4,7},{5,4},{6,5},{7,6},{8,11},{9,8},{10,9... | collective-permute-start | bytes 786440 | tf_op jit(solution)/shard_map/ppermute | solution.py:500
  66.4 8.2 %prepare.3 = (bf16[16,2,128,256]{3,2,1,0:T(8,128)(2,1)}, bf16[16,2,64,256]{3,2,1,0:T(8,128)(2,1)}, bf16[16,2,192,128]{3,2,1,0:T(8,128)(2,1)}, f32[128,128]{1,0:T(8,128)}, bf16[2048,256]{1,0:T(8,128)(2,1)}) custom-call(bf16[2048,512]{1,0:T(8,128)(2,1)} %q_ref.1, bf16[2048,512]{1,0:T(8,128)(2,1)} %k_ref.1, bf16[2048,512]{1,0:T(8,128)(2,1)} %v_ref.1, ...), custom_call_target="tpu_custom_call" | custom-call | flops 400000000 | bytes 14000000 | tf_op jit(solution)/shard_map/prepare/pallas_call | solution.py:389
  74.6 7.8 %advance.3 = (bf16[512,256]{1,0:T(8,128)(2,1)}, bf16[512,256]{1,0:T(8,128)(2,1)}, bf16[512,256]{1,0:T(8,128)(2,1)}, bf16[512,256]{1,0:T(8,128)(2,1)}, bf16[32,256,128]{2,1,0:T(8,128)(2,1)}) custom-call(s32[16]{0:T(128)} %owner_ref.5, s32[16]{0:T(128)} %slot_ref.3, s32[16]{0:T(128)} %ret_ref.3, s32[16]{0:T(128)} %counts_ref.3, ...), custom_call_target="tpu_custom_call" | custom-call | flops 500000000 | bytes 10000000 | tf_op jit(solution)/shard_map/advance/pallas_call | solution.py:424
  83.2 5.9 %all-to-all-done.1.received_ref = bf16[32,256,128]{2,1,0:T(8,128)(2,1)S(1)} async-done(((bf16[32,256,128]{2,1,0:T(8,128)(2,1)}), bf16[32,256,128]{2,1,0:T(8,128)(2,1)S(1)}, u32[]{:S(2)}, u32[]{:S(2)}) %all-to-all-start.1) | async-done | bytes 2097184 | tf_op jit(solution)/shard_map/all_to_all | solution.py:584
  89.0 5.2 %all-to-all-start = ((bf16[32,256,128]{2,1,0:T(8,128)(2,1)}), bf16[32,256,128]{2,1,0:T(8,128)(2,1)}, u32[]{:S(2)}, u32[]{:S(2)}) async-start(bf16[32,256,128]{2,1,0:T(8,128)(2,1)} %get-tuple-element.105), calls=%async_computation | async-start | bytes 4194304 | tf_op jit(solution)/shard_map/all_to_all | solution.py:594
  94.8 2.3 %collective-permute-start.11 = (bf16[512,256]{1,0:T(8,128)(2,1)S(1)}, bf16[512,256]{1,0:T(8,128)(2,1)S(1)}, u32[]{:S(2)}, u32[]{:S(2)}) collective-permute-start(bf16[512,256]{1,0:T(8,128)(2,1)S(1)} %copy-done.10), channel_id=1, source_target_pairs={{0,2},{1,3},{2,0},{3,1},{4,6},{5,7},{6,4},{7,5},{8,10},{9,11},{10,... | collective-permute-start | bytes 786440 | tf_op jit(solution)/shard_map/ppermute | solution.py:500
  98.7 5.6 %collective-permute-done.11.refs_0_ = bf16[512,256]{1,0:T(8,128)(2,1)S(1)} collective-permute-done((bf16[512,256]{1,0:T(8,128)(2,1)S(1)}, bf16[512,256]{1,0:T(8,128)(2,1)S(1)}, u32[]{:S(2)}, u32[]{:S(2)}) %collective-permute-start.11) | collective-permute-done | bytes 262176 | tf_op jit(solution)/shard_map/ppermute | solution.py:500
  105.8 1.5 %locate.1 = s32[1,128]{1,0:T(1,128)} custom-call(bf16[32,544,128]{2,1,0:T(8,128)(2,1)} %bitcast.8), custom_call_target="tpu_custom_call" | custom-call | bytes 200000 | tf_op jit(solution)/shard_map/locate/pallas_call | solution.py:375
  108.0 3.5 %unpack.2.refs_0_ = f32[16,512,128]{2,1,0:T(8,128)} custom-call(s32[128]{0:T(128)S(1)} %bitcast.6, bf16[32,256,128]{2,1,0:T(8,128)(2,1)S(1)} %all-to-all-done.1.received_ref), custom_call_target="tpu_custom_call" | custom-call | bytes 3200000 | tf_op jit(solution)/shard_map/unpack/pallas_call | solution.py:477
  111.6 4.3 %collective-permute-done.15.refs_5_ = bf16[512,256]{1,0:T(8,128)(2,1)} collective-permute-done((bf16[512,256]{1,0:T(8,128)(2,1)}, bf16[512,256]{1,0:T(8,128)(2,1)}, u32[]{:S(2)}, u32[]{:S(2)}) %collective-permute-start.15) | collective-permute-done | bytes 262176 | tf_op jit(solution)/shard_map/ppermute | solution.py:500
  117.0 9.7 %project.1 = bf16[512,2304]{1,0:T(8,128)(2,1)} custom-call(bf16[512,256]{1,0:T(8,128)(2,1)} %copy-done.12, bf16[512,256]{1,0:T(8,128)(2,1)} %copy-done.11, bf16[512,256]{1,0:T(8,128)(2,1)} %collective-permute-done.13.refs_2_, bf16[512,256]{1,0:T(8,128)(2,1)} %get-tuple-element.82.refs_3_, bf16[512,256]{1,0:T(8,128)(2,1)} %copy-done.13, ...), custom_call_target="tpu_custom_call" | custom-call | flops 4800000000 | bytes 14000000 | tf_op jit(solution)/shard_map/project/pallas_call | solution.py:460
  126.7 3.0 %unpack.3 = f32[16,512,128]{2,1,0:T(8,128)} custom-call(s32[128]{0:T(128)S(1)} %bitcast.7, bf16[32,256,128]{2,1,0:T(8,128)(2,1)} %all-to-all-done.received_ref, f32[16,512,128]{2,1,0:T(8,128)} %unpack.2.refs_0_), custom_call_target="tpu_custom_call", output_to_operand_aliasing={{}: (2, {})} | custom-call | bytes 3200000 | tf_op jit(solution)/shard_map/unpack/pallas_call | solution.py:477
  (64 shorter events, 15.3 us)
Async XLA Ops:
  7.2 67.5 %all-gather.2.cloned.1.call-start = ((), (), s32[]{:S(2)}) async-start(), calls=%async_computation.2 | async-start | bytes 4595712 | tf_op jit(solution)/shard_map/all_gather | solution.py:557
  9.0 32.1 %collective-permute-start.6 = (bf16[512,2304]{1,0:T(8,128)(2,1)}, bf16[512,2304]{1,0:T(8,128)(2,1)}, u32[]{:S(2)}, u32[]{:S(2)}) collective-permute-start(bf16[512,2304]{1,0:T(8,128)(2,1)} %refs_8_.1), channel_id=1, source_target_pairs={{0,1},{1,2},{2,3},{3,0},{4,7},{5,4},{6,5},{7,6},{8,9},{9,10},{10,1... | collective-permute-start | bytes 7077896 | tf_op jit(solution)/shard_map/ppermute | solution.py:509
  13.7 5.6 %collective-permute-start = (bf16[2,256,128]{2,1,0:T(8,128)(2,1)}, bf16[2,256,128]{2,1,0:T(8,128)(2,1)S(1)}, u32[]{:S(2)}, u32[]{:S(2)}) collective-permute-start(bf16[2,256,128]{2,1,0:T(8,128)(2,1)} %get-tuple-element.55), channel_id=1, source_target_pairs={{0,64},{4,20},{8,72},{12,28},{16,80},{20,4},{24,88},{28,12},{32,96... | collective-permute-start | bytes 393224 | tf_op jit(solution)/shard_map/ppermute | solution.py:525
  16.6 5.6 %collective-permute-start.1 = (bf16[2,256,128]{2,1,0:T(8,128)(2,1)}, bf16[2,256,128]{2,1,0:T(8,128)(2,1)S(1)}, u32[]{:S(2)}, u32[]{:S(2)}) collective-permute-start(bf16[2,256,128]{2,1,0:T(8,128)(2,1)} %get-tuple-element.55), channel_id=1, source_target_pairs={{0,32},{4,12},{8,40},{12,20},{16,48},{20,28},{24,56},{28,4},{32,64... | collective-permute-start | bytes 393224 | tf_op jit(solution)/shard_map/ppermute | solution.py:525
  17.0 5.2 %collective-permute-start.2 = (bf16[2,256,128]{2,1,0:T(8,128)(2,1)}, bf16[2,256,128]{2,1,0:T(8,128)(2,1)S(1)}, u32[]{:S(2)}, u32[]{:S(2)}) collective-permute-start(bf16[2,256,128]{2,1,0:T(8,128)(2,1)} %get-tuple-element.55), channel_id=1, source_target_pairs={{0,96},{4,28},{8,104},{12,4},{16,112},{20,12},{24,120},{28,20},{32... | collective-permute-start | bytes 393224 | tf_op jit(solution)/shard_map/ppermute | solution.py:525
  23.2 14.5 %copy-start.2 = (bf16[8,256,128]{2,1,0:T(8,128)(2,1)}, bf16[8,256,128]{2,1,0:T(8,128)(2,1)S(1)}, u32[]{:S(2)}) copy-start(bf16[8,256,128]{2,1,0:T(8,128)(2,1)S(1)} %pad_maximum_fusion.refs_0_) | copy-start | bytes 1572868
  23.2 14.5 %collective-permute-start.3 = (bf16[8,256,128]{2,1,0:T(8,128)(2,1)S(1)}, bf16[8,256,128]{2,1,0:T(8,128)(2,1)S(1)}, u32[]{:S(2)}, u32[]{:S(2)}) collective-permute-start(bf16[8,256,128]{2,1,0:T(8,128)(2,1)S(1)} %pad_maximum_fusion.refs_0_), channel_id=1, source_target_pairs={{0,16},{4,68},{8,24},{12,76},{16,0},{20,84},{24,8},{28,92},{32,48}... | collective-permute-start | bytes 1572872 | tf_op jit(solution)/shard_map/ppermute | solution.py:525
  26.1 15.1 %collective-permute-start.4 = (bf16[8,256,128]{2,1,0:T(8,128)(2,1)S(1)}, bf16[8,256,128]{2,1,0:T(8,128)(2,1)S(1)}, u32[]{:S(2)}, u32[]{:S(2)}) collective-permute-start(bf16[8,256,128]{2,1,0:T(8,128)(2,1)S(1)} %pad_maximum_fusion.refs_0_), channel_id=1, source_target_pairs={{0,8},{4,36},{8,16},{12,44},{16,24},{20,52},{24,0},{28,60},{32,40}... | collective-permute-start | bytes 1572872 | tf_op jit(solution)/shard_map/ppermute | solution.py:525
  26.4 14.8 %collective-permute-start.5 = (bf16[8,256,128]{2,1,0:T(8,128)(2,1)S(1)}, bf16[8,256,128]{2,1,0:T(8,128)(2,1)S(1)}, u32[]{:S(2)}, u32[]{:S(2)}) collective-permute-start(bf16[8,256,128]{2,1,0:T(8,128)(2,1)S(1)} %pad_maximum_fusion.refs_0_), channel_id=1, source_target_pairs={{0,24},{4,100},{8,0},{12,108},{16,8},{20,116},{24,16},{28,124},{32... | collective-permute-start | bytes 1572872 | tf_op jit(solution)/shard_map/ppermute | solution.py:525
  28.7 13.6 %collective-permute-start.7 = (bf16[8,256,128]{2,1,0:T(8,128)(2,1)S(1)}, bf16[8,256,128]{2,1,0:T(8,128)(2,1)S(1)}, u32[]{:S(2)}, u32[]{:S(2)}) collective-permute-start(bf16[8,256,128]{2,1,0:T(8,128)(2,1)S(1)} %pad_maximum_fusion.refs_0_), channel_id=1, source_target_pairs={{0,4},{4,0},{8,12},{12,8},{16,20},{20,16},{24,28},{28,24},{32,36},... | collective-permute-start | bytes 1572872 | tf_op jit(solution)/shard_map/ppermute | solution.py:513
  41.1 2.2 %collective-permute-start.10 = (bf16[8,256,128]{2,1,0:T(8,128)(2,1)S(1)}, bf16[8,256,128]{2,1,0:T(8,128)(2,1)S(1)}, u32[]{:S(2)}, u32[]{:S(2)}) collective-permute-start(bf16[8,256,128]{2,1,0:T(8,128)(2,1)S(1)} %collective-permute-done.5.refs_3_), channel_id=1, source_target_pairs={{0,4},{4,0},{8,12},{12,8},{16,20},{20,16},{24,28},{28,24},{32,36},... | collective-permute-start | bytes 1572872 | tf_op jit(solution)/shard_map/ppermute | solution.py:513
  41.8 3.0 %collective-permute-start.8 = (bf16[8,256,128]{2,1,0:T(8,128)(2,1)S(1)}, bf16[8,256,128]{2,1,0:T(8,128)(2,1)S(1)}, u32[]{:S(2)}, u32[]{:S(2)}) collective-permute-start(bf16[8,256,128]{2,1,0:T(8,128)(2,1)S(1)} %collective-permute-done.3.refs_1_), channel_id=1, source_target_pairs={{0,4},{4,0},{8,12},{12,8},{16,20},{20,16},{24,28},{28,24},{32,36},... | collective-permute-start | bytes 1572872 | tf_op jit(solution)/shard_map/ppermute | solution.py:513
  41.8 3.2 %collective-permute-start.9 = (bf16[8,256,128]{2,1,0:T(8,128)(2,1)S(1)}, bf16[8,256,128]{2,1,0:T(8,128)(2,1)}, u32[]{:S(2)}, u32[]{:S(2)}) collective-permute-start(bf16[8,256,128]{2,1,0:T(8,128)(2,1)S(1)} %collective-permute-done.4.refs_2_), channel_id=1, source_target_pairs={{0,4},{4,0},{8,12},{12,8},{16,20},{20,16},{24,28},{28,24},{32,36},... | collective-permute-start | bytes 1572872 | tf_op jit(solution)/shard_map/ppermute | solution.py:513
  53.4 35.7 %all-to-all-start.1 = ((bf16[32,256,128]{2,1,0:T(8,128)(2,1)}), bf16[32,256,128]{2,1,0:T(8,128)(2,1)S(1)}, u32[]{:S(2)}, u32[]{:S(2)}) async-start(bf16[32,256,128]{2,1,0:T(8,128)(2,1)} %get-tuple-element.84), calls=%async_computation.1 | async-start | bytes 4194304 | tf_op jit(solution)/shard_map/all_to_all | solution.py:584
  62.1 21.0 %collective-permute-start.18 = (bf16[256,2304]{1,0:T(8,128)(2,1)S(1)}, bf16[256,2304]{1,0:T(8,128)(2,1)}, u32[]{:S(2)}, u32[]{:S(2)}) collective-permute-start(bf16[256,2304]{1,0:T(8,128)(2,1)S(1)} %constant_dynamic-slice_fusion), channel_id=1, source_target_pairs={{0,1},{1,2},{2,3},{3,0},{4,7},{5,4},{6,5},{7,6},{8,9},{9,10},{10,1... | collective-permute-start | bytes 3538952 | tf_op jit(solution)/shard_map/ppermute | solution.py:509
  63.7 47.8 %collective-permute-start.17 = (bf16[512,2304]{1,0:T(8,128)(2,1)}, bf16[512,2304]{1,0:T(8,128)(2,1)}, u32[]{:S(2)}, u32[]{:S(2)}) collective-permute-start(bf16[512,2304]{1,0:T(8,128)(2,1)} %collective-permute-done.6.refs_9_), channel_id=1, source_target_pairs={{0,4},{4,0},{8,12},{12,8},{16,20},{20,16},{24,28},{28,24},{32,36},... | collective-permute-start | bytes 7077896 | tf_op jit(solution)/shard_map/ppermute | solution.py:513
  63.7 18.7 %collective-permute-start.12 = (bf16[512,256]{1,0:T(8,128)(2,1)}, bf16[512,256]{1,0:T(8,128)(2,1)S(1)}, u32[]{:S(2)}, u32[]{:S(2)}) collective-permute-start(bf16[512,256]{1,0:T(8,128)(2,1)} %get-tuple-element.80), channel_id=1, source_target_pairs={{0,1},{1,2},{2,3},{3,0},{4,5},{5,6},{6,7},{7,4},{8,9},{9,10},{10,1... | collective-permute-start | bytes 786440 | tf_op jit(solution)/shard_map/ppermute | solution.py:500
  64.7 18.5 %collective-permute-start.13 = (bf16[512,256]{1,0:T(8,128)(2,1)}, bf16[512,256]{1,0:T(8,128)(2,1)}, u32[]{:S(2)}, u32[]{:S(2)}) collective-permute-start(bf16[512,256]{1,0:T(8,128)(2,1)} %get-tuple-element.81), channel_id=1, source_target_pairs={{0,3},{1,0},{2,1},{3,2},{4,7},{5,4},{6,5},{7,6},{8,11},{9,8},{10,9... | collective-permute-start | bytes 786440 | tf_op jit(solution)/shard_map/ppermute | solution.py:500
  89.0 37.7 %all-to-all-start = ((bf16[32,256,128]{2,1,0:T(8,128)(2,1)}), bf16[32,256,128]{2,1,0:T(8,128)(2,1)}, u32[]{:S(2)}, u32[]{:S(2)}) async-start(bf16[32,256,128]{2,1,0:T(8,128)(2,1)} %get-tuple-element.105), calls=%async_computation | async-start | bytes 4194304 | tf_op jit(solution)/shard_map/all_to_all | solution.py:594
  94.3 21.6 %collective-permute-start.19 = (bf16[256,2304]{1,0:T(8,128)(2,1)}, bf16[256,2304]{1,0:T(8,128)(2,1)S(1)}, u32[]{:S(2)}, u32[]{:S(2)}) collective-permute-start(bf16[256,2304]{1,0:T(8,128)(2,1)} %collective-permute-done.18.refs_11_), channel_id=1, source_target_pairs={{0,4},{4,0},{8,12},{12,8},{16,20},{20,16},{24,28},{28,24},{32,36},... | collective-permute-start | bytes 3538952 | tf_op jit(solution)/shard_map/ppermute | solution.py:513
  94.8 9.5 %collective-permute-start.11 = (bf16[512,256]{1,0:T(8,128)(2,1)S(1)}, bf16[512,256]{1,0:T(8,128)(2,1)S(1)}, u32[]{:S(2)}, u32[]{:S(2)}) collective-permute-start(bf16[512,256]{1,0:T(8,128)(2,1)S(1)} %copy-done.10), channel_id=1, source_target_pairs={{0,2},{1,3},{2,0},{3,1},{4,6},{5,7},{6,4},{7,5},{8,10},{9,11},{10,... | collective-permute-start | bytes 786440 | tf_op jit(solution)/shard_map/ppermute | solution.py:500
  97.1 14.5 %collective-permute-start.14 = (bf16[512,256]{1,0:T(8,128)(2,1)}, bf16[512,256]{1,0:T(8,128)(2,1)S(1)}, u32[]{:S(2)}, u32[]{:S(2)}) collective-permute-start(bf16[512,256]{1,0:T(8,128)(2,1)} %get-tuple-element.98), channel_id=1, source_target_pairs={{0,2},{1,3},{2,0},{3,1},{4,6},{5,7},{6,4},{7,5},{8,10},{9,11},{10,... | collective-permute-start | bytes 786440 | tf_op jit(solution)/shard_map/ppermute | solution.py:500
  97.8 18.1 %collective-permute-start.15 = (bf16[512,256]{1,0:T(8,128)(2,1)}, bf16[512,256]{1,0:T(8,128)(2,1)}, u32[]{:S(2)}, u32[]{:S(2)}) collective-permute-start(bf16[512,256]{1,0:T(8,128)(2,1)} %get-tuple-element.99), channel_id=1, source_target_pairs={{0,1},{1,2},{2,3},{3,0},{4,5},{5,6},{6,7},{7,4},{8,9},{9,10},{10,1... | collective-permute-start | bytes 786440 | tf_op jit(solution)/shard_map/ppermute | solution.py:500
  104.3 11.6 %collective-permute-start.16 = (bf16[512,256]{1,0:T(8,128)(2,1)}, bf16[512,256]{1,0:T(8,128)(2,1)S(1)}, u32[]{:S(2)}, u32[]{:S(2)}) collective-permute-start(bf16[512,256]{1,0:T(8,128)(2,1)} %get-tuple-element.100), channel_id=1, source_target_pairs={{0,3},{1,0},{2,1},{3,2},{4,7},{5,4},{6,5},{7,6},{8,11},{9,8},{10,9... | collective-permute-start | bytes 786440 | tf_op jit(solution)/shard_map/ppermute | solution.py:500
  (14 other events, 51.9 us)
Sparse Core Ops, SparseCore 0:
  10.2 54.7 all-gather.1

commit v4 on v3

--- a/solution.py
+++ b/solution.py
@@ -26,6 +26,7 @@
 READY = 4
 GROUP = 4
 VMEM_BYTES = 60 << 20
+PROJECT_BYTES = 32 << 20
 UNPACK_BYTES = 8 << 20
 QUARTER_SHIFTS = (2, 1, 3, 0)
 
@@ -464,7 +465,7 @@
         + [pl.BlockSpec((weight.shape[0], tile), lambda t: (0, t)) for weight in weights],
         out_specs=pl.BlockSpec((rows, tile), lambda t: (0, t)),
         out_shape=jax.ShapeDtypeStruct((rows, D), bf16),
-        compiler_params=pltpu.CompilerParams(vmem_limit_bytes=VMEM_BYTES),
+        compiler_params=pltpu.CompilerParams(vmem_limit_bytes=PROJECT_BYTES),
         cost_estimate=pl.CostEstimate(
             flops=4_800_000_000, bytes_accessed=14_000_000, transcendentals=0
         ),

time: 138 us -> 136 us (0.986)
  no operation moved by 1% of the time
where the time goes in v4:
time: 136 us; the launch traced here: 134 us
  Pallas kernels  50.7 us (37%)
  starting transfers between devices  40.2 us (30%)
  waiting for transfers between devices  24.6 us (18%)
  between operations  14.2 us (10%)
  local copies, waits for them, and re-layouts  3.73 us (3%)
    pallas_call x2, Pallas kernels, prepare(): pl.pallas_call(functools.partial(prepare_kernel, pair), grid=(R_DEV // RE...  16.5 us
    pallas_call x2, Pallas kernels, advance(): pl.pallas_call(advance_kernel, grid_spec=pltpu.PrefetchScalarGridSpec(num...  15.8 us
    all_to_all x2, starting transfers between devices, body(): lax.all_to_all(sending, 'cache', split_axis=0, concat_axis=0, tiled=True)  12.2 us
    ppermute x6, starting transfers between devices, along_chips(): return lax.ppermute(x, 'cache', pairs)  11.1 us
    ppermute x6, waiting for transfers between devices, along_tp(): return lax.ppermute(x, 'tp', [(z, (z + shift) % N_TP) for z in range(N_TP)])  10.8 us
    pallas_call x1, Pallas kernels, project(): pl.pallas_call(project_kernel, grid=(TILES,), in_specs=[pl.BlockSpec((row...  8.62 us
    ppermute x6, starting transfers between devices, along_tp(): return lax.ppermute(x, 'tp', [(z, (z + shift) % N_TP) for z in range(N_TP)])  8.21 us
    pallas_call x2, Pallas kernels, unpack(): pl.pallas_call(functools.partial(unpack_kernel, pair), grid_spec=pltpu.Pr...  6.51 us
  transfers between devices with their start and end apart: 23, of which 9 were waited for; matrix products, arithmetic and copies ran while one was open for 2% of the time, Pallas kernels for 34%

profile of v4, /device:TPU:1, one launch (start us, length us, event | category | flops | bytes accessed | tf_op | source)
XLA Modules:
  0.0 134.4 jit_solution(4926669929563682150)
XLA Ops:
  7.2 1.8 %pack.1 = (bf16[2,256,128]{2,1,0:T(8,128)(2,1)}, bf16[2,272,128]{2,1,0:T(8,128)(2,1)}) custom-call(s32[16]{0:T(128)} %ret_ref.3, f32[2,4,128,128]{3,2,1,0:T(8,128)} %store_ref.1), custom_call_target="tpu_custom_call" | custom-call | bytes 800000 | tf_op jit(solution)/shard_map/pack/pallas_call | solution.py:362
  9.0 4.7 %collective-permute-start.6 = (bf16[512,2304]{1,0:T(8,128)(2,1)}, bf16[512,2304]{1,0:T(8,128)(2,1)}, u32[]{:S(2)}, u32[]{:S(2)}) collective-permute-start(bf16[512,2304]{1,0:T(8,128)(2,1)} %refs_8_.1), channel_id=1, source_target_pairs={{0,1},{1,2},{2,3},{3,0},{4,7},{5,4},{6,5},{7,6},{8,9},{9,10},{10,1... | collective-permute-start | bytes 7077896 | tf_op jit(solution)/shard_map/ppermute | solution.py:510
  13.7 2.9 %collective-permute-start = (bf16[2,256,128]{2,1,0:T(8,128)(2,1)}, bf16[2,256,128]{2,1,0:T(8,128)(2,1)S(1)}, u32[]{:S(2)}, u32[]{:S(2)}) collective-permute-start(bf16[2,256,128]{2,1,0:T(8,128)(2,1)} %get-tuple-element.55), channel_id=1, source_target_pairs={{0,64},{4,20},{8,72},{12,28},{16,80},{20,4},{24,88},{28,12},{32,96... | collective-permute-start | bytes 393224 | tf_op jit(solution)/shard_map/ppermute | solution.py:526
  17.0 2.3 %collective-permute-start.2 = (bf16[2,256,128]{2,1,0:T(8,128)(2,1)}, bf16[2,256,128]{2,1,0:T(8,128)(2,1)S(1)}, u32[]{:S(2)}, u32[]{:S(2)}) collective-permute-start(bf16[2,256,128]{2,1,0:T(8,128)(2,1)} %get-tuple-element.55), channel_id=1, source_target_pairs={{0,96},{4,28},{8,104},{12,4},{16,112},{20,12},{24,120},{28,20},{32... | collective-permute-start | bytes 393224 | tf_op jit(solution)/shard_map/ppermute | solution.py:526
  19.3 3.0 %collective-permute-done.1 = bf16[2,256,128]{2,1,0:T(8,128)(2,1)S(1)} collective-permute-done((bf16[2,256,128]{2,1,0:T(8,128)(2,1)}, bf16[2,256,128]{2,1,0:T(8,128)(2,1)S(1)}, u32[]{:S(2)}, u32[]{:S(2)}) %collective-permute-start.1) | collective-permute-done | bytes 131104 | tf_op jit(solution)/shard_map/ppermute | solution.py:526
  23.2 2.8 %collective-permute-start.3 = (bf16[8,256,128]{2,1,0:T(8,128)(2,1)S(1)}, bf16[8,256,128]{2,1,0:T(8,128)(2,1)S(1)}, u32[]{:S(2)}, u32[]{:S(2)}) collective-permute-start(bf16[8,256,128]{2,1,0:T(8,128)(2,1)S(1)} %pad_maximum_fusion.refs_0_), channel_id=1, source_target_pairs={{0,16},{4,68},{8,24},{12,76},{16,0},{20,84},{24,8},{28,92},{32,48}... | collective-permute-start | bytes 1572872 | tf_op jit(solution)/shard_map/ppermute | solution.py:526
  26.3 2.4 %collective-permute-start.5 = (bf16[8,256,128]{2,1,0:T(8,128)(2,1)S(1)}, bf16[8,256,128]{2,1,0:T(8,128)(2,1)S(1)}, u32[]{:S(2)}, u32[]{:S(2)}) collective-permute-start(bf16[8,256,128]{2,1,0:T(8,128)(2,1)S(1)} %pad_maximum_fusion.refs_0_), channel_id=1, source_target_pairs={{0,24},{4,100},{8,0},{12,108},{16,8},{20,116},{24,16},{28,124},{32... | collective-permute-start | bytes 1572872 | tf_op jit(solution)/shard_map/ppermute | solution.py:526
  29.4 8.2 %prepare.2 = (bf16[16,2,128,256]{3,2,1,0:T(8,128)(2,1)}, bf16[16,2,64,256]{3,2,1,0:T(8,128)(2,1)}, bf16[16,2,192,128]{3,2,1,0:T(8,128)(2,1)}, f32[128,128]{1,0:T(8,128)}, bf16[2048,256]{1,0:T(8,128)(2,1)}) custom-call(bf16[2048,512]{1,0:T(8,128)(2,1)} %q_ref.1, bf16[2048,512]{1,0:T(8,128)(2,1)} %k_ref.1, bf16[2048,512]{1,0:T(8,128)(2,1)} %v_ref.1, ...), custom_call_target="tpu_custom_call" | custom-call | flops 400000000 | bytes 14000000 | tf_op jit(solution)/shard_map/prepare/pallas_call | solution.py:390
  37.7 3.4 %collective-permute-done.4.refs_2_ = bf16[8,256,128]{2,1,0:T(8,128)(2,1)S(1)} collective-permute-done((bf16[8,256,128]{2,1,0:T(8,128)(2,1)S(1)}, bf16[8,256,128]{2,1,0:T(8,128)(2,1)S(1)}, u32[]{:S(2)}, u32[]{:S(2)}) %collective-permute-start.4) | collective-permute-done | bytes 524320 | tf_op jit(solution)/shard_map/ppermute | solution.py:526
  45.6 8.0 %advance.2 = (bf16[512,256]{1,0:T(8,128)(2,1)}, bf16[512,256]{1,0:T(8,128)(2,1)}, bf16[512,256]{1,0:T(8,128)(2,1)}, bf16[512,256]{1,0:T(8,128)(2,1)}, bf16[32,256,128]{2,1,0:T(8,128)(2,1)}) custom-call(s32[16]{0:T(128)} %owner_ref.5, s32[16]{0:T(128)} %slot_ref.3, s32[16]{0:T(128)} %ret_ref.3, s32[16]{0:T(128)} %counts_ref.3, ...), custom_call_target="tpu_custom_call" | custom-call | flops 500000000 | bytes 10000000 | tf_op jit(solution)/shard_map/advance/pallas_call | solution.py:425
  53.6 7.0 %all-to-all-start.1 = ((bf16[32,256,128]{2,1,0:T(8,128)(2,1)}), bf16[32,256,128]{2,1,0:T(8,128)(2,1)S(1)}, u32[]{:S(2)}, u32[]{:S(2)}) async-start(bf16[32,256,128]{2,1,0:T(8,128)(2,1)} %get-tuple-element.84), calls=%async_computation.1 | async-start | bytes 4194304 | tf_op jit(solution)/shard_map/all_to_all | solution.py:585
  60.6 2.4 %constant_dynamic-slice_fusion = bf16[256,2304]{1,0:T(8,128)(2,1)} fusion(bf16[512,2304]{1,0:T(8,128)(2,1)} %collective-permute-done.6.refs_9_, s32[]{:T(128)S(6)} %select_n.3), kind=kLoop, calls=%fused_computation.1 | loop fusion | bytes 2359300 | tf_op jit(solution)/shard_map/dynamic_slice | solution.py:579
  63.0 1.6 %collective-permute-start.18 = (bf16[256,2304]{1,0:T(8,128)(2,1)}, bf16[256,2304]{1,0:T(8,128)(2,1)S(1)}, u32[]{:S(2)}, u32[]{:S(2)}) collective-permute-start(bf16[256,2304]{1,0:T(8,128)(2,1)} %constant_dynamic-slice_fusion), channel_id=1, source_target_pairs={{0,1},{1,2},{2,3},{3,0},{4,7},{5,4},{6,5},{7,6},{8,9},{9,10},{10,1... | collective-permute-start | bytes 3538952 | tf_op jit(solution)/shard_map/ppermute | solution.py:510
  67.3 8.3 %prepare.3 = (bf16[16,2,128,256]{3,2,1,0:T(8,128)(2,1)}, bf16[16,2,64,256]{3,2,1,0:T(8,128)(2,1)}, bf16[16,2,192,128]{3,2,1,0:T(8,128)(2,1)}, f32[128,128]{1,0:T(8,128)}, bf16[2048,256]{1,0:T(8,128)(2,1)}) custom-call(bf16[2048,512]{1,0:T(8,128)(2,1)} %q_ref.1, bf16[2048,512]{1,0:T(8,128)(2,1)} %k_ref.1, bf16[2048,512]{1,0:T(8,128)(2,1)} %v_ref.1, ...), custom_call_target="tpu_custom_call" | custom-call | flops 400000000 | bytes 14000000 | tf_op jit(solution)/shard_map/prepare/pallas_call | solution.py:390
  75.6 7.8 %advance.3 = (bf16[512,256]{1,0:T(8,128)(2,1)}, bf16[512,256]{1,0:T(8,128)(2,1)}, bf16[512,256]{1,0:T(8,128)(2,1)}, bf16[512,256]{1,0:T(8,128)(2,1)}, bf16[32,256,128]{2,1,0:T(8,128)(2,1)}) custom-call(s32[16]{0:T(128)} %owner_ref.5, s32[16]{0:T(128)} %slot_ref.3, s32[16]{0:T(128)} %ret_ref.3, s32[16]{0:T(128)} %counts_ref.3, ...), custom_call_target="tpu_custom_call" | custom-call | flops 500000000 | bytes 10000000 | tf_op jit(solution)/shard_map/advance/pallas_call | solution.py:425
  84.2 4.7 %all-to-all-done.1.received_ref = bf16[32,256,128]{2,1,0:T(8,128)(2,1)S(1)} async-done(((bf16[32,256,128]{2,1,0:T(8,128)(2,1)}), bf16[32,256,128]{2,1,0:T(8,128)(2,1)S(1)}, u32[]{:S(2)}, u32[]{:S(2)}) %all-to-all-start.1) | async-done | bytes 2097184 | tf_op jit(solution)/shard_map/all_to_all | solution.py:585
  88.9 5.2 %all-to-all-start = ((bf16[32,256,128]{2,1,0:T(8,128)(2,1)}), bf16[32,256,128]{2,1,0:T(8,128)(2,1)}, u32[]{:S(2)}, u32[]{:S(2)}) async-start(bf16[32,256,128]{2,1,0:T(8,128)(2,1)} %get-tuple-element.105), calls=%async_computation | async-start | bytes 4194304 | tf_op jit(solution)/shard_map/all_to_all | solution.py:595
  94.6 2.8 %collective-permute-start.11 = (bf16[512,256]{1,0:T(8,128)(2,1)}, bf16[512,256]{1,0:T(8,128)(2,1)S(1)}, u32[]{:S(2)}, u32[]{:S(2)}) collective-permute-start(bf16[512,256]{1,0:T(8,128)(2,1)} %get-tuple-element.79), channel_id=1, source_target_pairs={{0,2},{1,3},{2,0},{3,1},{4,6},{5,7},{6,4},{7,5},{8,10},{9,11},{10,... | collective-permute-start | bytes 786440 | tf_op jit(solution)/shard_map/ppermute | solution.py:501
  98.6 5.8 %collective-permute-done.11.refs_0_ = bf16[512,256]{1,0:T(8,128)(2,1)S(1)} collective-permute-done((bf16[512,256]{1,0:T(8,128)(2,1)}, bf16[512,256]{1,0:T(8,128)(2,1)S(1)}, u32[]{:S(2)}, u32[]{:S(2)}) %collective-permute-start.11) | collective-permute-done | bytes 262176 | tf_op jit(solution)/shard_map/ppermute | solution.py:501
  104.3 1.6 %collective-permute-start.16 = (bf16[512,256]{1,0:T(8,128)(2,1)}, bf16[512,256]{1,0:T(8,128)(2,1)}, u32[]{:S(2)}, u32[]{:S(2)}) collective-permute-start(bf16[512,256]{1,0:T(8,128)(2,1)} %get-tuple-element.100), channel_id=1, source_target_pairs={{0,3},{1,0},{2,1},{3,2},{4,7},{5,4},{6,5},{7,6},{8,11},{9,8},{10,9... | collective-permute-start | bytes 786440 | tf_op jit(solution)/shard_map/ppermute | solution.py:501
  108.1 3.5 %unpack.2.refs_0_ = f32[16,512,128]{2,1,0:T(8,128)} custom-call(s32[128]{0:T(128)S(1)} %bitcast.6, bf16[32,256,128]{2,1,0:T(8,128)(2,1)S(1)} %all-to-all-done.1.received_ref), custom_call_target="tpu_custom_call" | custom-call | bytes 3200000 | tf_op jit(solution)/shard_map/unpack/pallas_call | solution.py:478
  111.6 4.3 %collective-permute-done.15.refs_5_ = bf16[512,256]{1,0:T(8,128)(2,1)} collective-permute-done((bf16[512,256]{1,0:T(8,128)(2,1)}, bf16[512,256]{1,0:T(8,128)(2,1)}, u32[]{:S(2)}, u32[]{:S(2)}) %collective-permute-start.15) | collective-permute-done | bytes 262176 | tf_op jit(solution)/shard_map/ppermute | solution.py:501
  115.9 8.6 %project.1 = bf16[512,2304]{1,0:T(8,128)(2,1)} custom-call(bf16[512,256]{1,0:T(8,128)(2,1)S(1)} %collective-permute-done.11.refs_0_, bf16[512,256]{1,0:T(8,128)(2,1)S(1)} %collective-permute-done.12.refs_1_, bf16[512,256]{1,0:T(8,128)(2,1)} %collective-permute-done.13.refs_2_, bf16[512,256]{1,0:T(8,128)(2,1)S(1)} %copy-done.3, ...), custom_call_target="tpu_custom_call" | custom-call | flops 4800000000 | bytes 14000000 | tf_op jit(solution)/shard_map/project/pallas_call | solution.py:461
  124.6 3.0 %unpack.3 = f32[16,512,128]{2,1,0:T(8,128)} custom-call(s32[128]{0:T(128)S(1)} %bitcast.7, bf16[32,256,128]{2,1,0:T(8,128)(2,1)} %all-to-all-done.received_ref, f32[16,512,128]{2,1,0:T(8,128)} %unpack.2.refs_0_), custom_call_target="tpu_custom_call", output_to_operand_aliasing={{}: (2, {})} | custom-call | bytes 3200000 | tf_op jit(solution)/shard_map/unpack/pallas_call | solution.py:478
  (58 shorter events, 14.2 us)
Async XLA Ops:
  7.2 68.4 %all-gather.2.cloned.1.call-start = ((), (), s32[]{:S(2)}) async-start(), calls=%async_computation.2 | async-start | bytes 4595712 | tf_op jit(solution)/shard_map/all_gather | solution.py:558
  9.0 32.1 %collective-permute-start.6 = (bf16[512,2304]{1,0:T(8,128)(2,1)}, bf16[512,2304]{1,0:T(8,128)(2,1)}, u32[]{:S(2)}, u32[]{:S(2)}) collective-permute-start(bf16[512,2304]{1,0:T(8,128)(2,1)} %refs_8_.1), channel_id=1, source_target_pairs={{0,1},{1,2},{2,3},{3,0},{4,7},{5,4},{6,5},{7,6},{8,9},{9,10},{10,1... | collective-permute-start | bytes 7077896 | tf_op jit(solution)/shard_map/ppermute | solution.py:510
  13.7 5.6 %collective-permute-start = (bf16[2,256,128]{2,1,0:T(8,128)(2,1)}, bf16[2,256,128]{2,1,0:T(8,128)(2,1)S(1)}, u32[]{:S(2)}, u32[]{:S(2)}) collective-permute-start(bf16[2,256,128]{2,1,0:T(8,128)(2,1)} %get-tuple-element.55), channel_id=1, source_target_pairs={{0,64},{4,20},{8,72},{12,28},{16,80},{20,4},{24,88},{28,12},{32,96... | collective-permute-start | bytes 393224 | tf_op jit(solution)/shard_map/ppermute | solution.py:526
  16.6 5.6 %collective-permute-start.1 = (bf16[2,256,128]{2,1,0:T(8,128)(2,1)}, bf16[2,256,128]{2,1,0:T(8,128)(2,1)S(1)}, u32[]{:S(2)}, u32[]{:S(2)}) collective-permute-start(bf16[2,256,128]{2,1,0:T(8,128)(2,1)} %get-tuple-element.55), channel_id=1, source_target_pairs={{0,32},{4,12},{8,40},{12,20},{16,48},{20,28},{24,56},{28,4},{32,64... | collective-permute-start | bytes 393224 | tf_op jit(solution)/shard_map/ppermute | solution.py:526
  17.0 5.2 %collective-permute-start.2 = (bf16[2,256,128]{2,1,0:T(8,128)(2,1)}, bf16[2,256,128]{2,1,0:T(8,128)(2,1)S(1)}, u32[]{:S(2)}, u32[]{:S(2)}) collective-permute-start(bf16[2,256,128]{2,1,0:T(8,128)(2,1)} %get-tuple-element.55), channel_id=1, source_target_pairs={{0,96},{4,28},{8,104},{12,4},{16,112},{20,12},{24,120},{28,20},{32... | collective-permute-start | bytes 393224 | tf_op jit(solution)/shard_map/ppermute | solution.py:526
  23.2 14.5 %copy-start.5 = (bf16[8,256,128]{2,1,0:T(8,128)(2,1)}, bf16[8,256,128]{2,1,0:T(8,128)(2,1)S(1)}, u32[]{:S(2)}) copy-start(bf16[8,256,128]{2,1,0:T(8,128)(2,1)S(1)} %pad_maximum_fusion.refs_0_) | copy-start | bytes 1572868
  23.2 14.5 %collective-permute-start.3 = (bf16[8,256,128]{2,1,0:T(8,128)(2,1)S(1)}, bf16[8,256,128]{2,1,0:T(8,128)(2,1)S(1)}, u32[]{:S(2)}, u32[]{:S(2)}) collective-permute-start(bf16[8,256,128]{2,1,0:T(8,128)(2,1)S(1)} %pad_maximum_fusion.refs_0_), channel_id=1, source_target_pairs={{0,16},{4,68},{8,24},{12,76},{16,0},{20,84},{24,8},{28,92},{32,48}... | collective-permute-start | bytes 1572872 | tf_op jit(solution)/shard_map/ppermute | solution.py:526
  26.0 15.1 %collective-permute-start.4 = (bf16[8,256,128]{2,1,0:T(8,128)(2,1)S(1)}, bf16[8,256,128]{2,1,0:T(8,128)(2,1)S(1)}, u32[]{:S(2)}, u32[]{:S(2)}) collective-permute-start(bf16[8,256,128]{2,1,0:T(8,128)(2,1)S(1)} %pad_maximum_fusion.refs_0_), channel_id=1, source_target_pairs={{0,8},{4,36},{8,16},{12,44},{16,24},{20,52},{24,0},{28,60},{32,40}... | collective-permute-start | bytes 1572872 | tf_op jit(solution)/shard_map/ppermute | solution.py:526
  26.3 14.8 %collective-permute-start.5 = (bf16[8,256,128]{2,1,0:T(8,128)(2,1)S(1)}, bf16[8,256,128]{2,1,0:T(8,128)(2,1)S(1)}, u32[]{:S(2)}, u32[]{:S(2)}) collective-permute-start(bf16[8,256,128]{2,1,0:T(8,128)(2,1)S(1)} %pad_maximum_fusion.refs_0_), channel_id=1, source_target_pairs={{0,24},{4,100},{8,0},{12,108},{16,8},{20,116},{24,16},{28,124},{32... | collective-permute-start | bytes 1572872 | tf_op jit(solution)/shard_map/ppermute | solution.py:526
  28.7 13.6 %collective-permute-start.7 = (bf16[8,256,128]{2,1,0:T(8,128)(2,1)S(1)}, bf16[8,256,128]{2,1,0:T(8,128)(2,1)S(1)}, u32[]{:S(2)}, u32[]{:S(2)}) collective-permute-start(bf16[8,256,128]{2,1,0:T(8,128)(2,1)S(1)} %pad_maximum_fusion.refs_0_), channel_id=1, source_target_pairs={{0,4},{4,0},{8,12},{12,8},{16,20},{20,16},{24,28},{28,24},{32,36},... | collective-permute-start | bytes 1572872 | tf_op jit(solution)/shard_map/ppermute | solution.py:514
  41.1 2.2 %collective-permute-start.10 = (bf16[8,256,128]{2,1,0:T(8,128)(2,1)S(1)}, bf16[8,256,128]{2,1,0:T(8,128)(2,1)S(1)}, u32[]{:S(2)}, u32[]{:S(2)}) collective-permute-start(bf16[8,256,128]{2,1,0:T(8,128)(2,1)S(1)} %collective-permute-done.5.refs_3_), channel_id=1, source_target_pairs={{0,4},{4,0},{8,12},{12,8},{16,20},{20,16},{24,28},{28,24},{32,36},... | collective-permute-start | bytes 1572872 | tf_op jit(solution)/shard_map/ppermute | solution.py:514
  41.8 3.0 %collective-permute-start.8 = (bf16[8,256,128]{2,1,0:T(8,128)(2,1)S(1)}, bf16[8,256,128]{2,1,0:T(8,128)(2,1)S(1)}, u32[]{:S(2)}, u32[]{:S(2)}) collective-permute-start(bf16[8,256,128]{2,1,0:T(8,128)(2,1)S(1)} %collective-permute-done.3.refs_1_), channel_id=1, source_target_pairs={{0,4},{4,0},{8,12},{12,8},{16,20},{20,16},{24,28},{28,24},{32,36},... | collective-permute-start | bytes 1572872 | tf_op jit(solution)/shard_map/ppermute | solution.py:514
  41.8 3.2 %collective-permute-start.9 = (bf16[8,256,128]{2,1,0:T(8,128)(2,1)S(1)}, bf16[8,256,128]{2,1,0:T(8,128)(2,1)}, u32[]{:S(2)}, u32[]{:S(2)}) collective-permute-start(bf16[8,256,128]{2,1,0:T(8,128)(2,1)S(1)} %collective-permute-done.4.refs_2_), channel_id=1, source_target_pairs={{0,4},{4,0},{8,12},{12,8},{16,20},{20,16},{24,28},{28,24},{32,36},... | collective-permute-start | bytes 1572872 | tf_op jit(solution)/shard_map/ppermute | solution.py:514
  53.6 35.3 %all-to-all-start.1 = ((bf16[32,256,128]{2,1,0:T(8,128)(2,1)}), bf16[32,256,128]{2,1,0:T(8,128)(2,1)S(1)}, u32[]{:S(2)}, u32[]{:S(2)}) async-start(bf16[32,256,128]{2,1,0:T(8,128)(2,1)} %get-tuple-element.84), calls=%async_computation.1 | async-start | bytes 4194304 | tf_op jit(solution)/shard_map/all_to_all | solution.py:585
  63.0 21.2 %collective-permute-start.18 = (bf16[256,2304]{1,0:T(8,128)(2,1)}, bf16[256,2304]{1,0:T(8,128)(2,1)S(1)}, u32[]{:S(2)}, u32[]{:S(2)}) collective-permute-start(bf16[256,2304]{1,0:T(8,128)(2,1)} %constant_dynamic-slice_fusion), channel_id=1, source_target_pairs={{0,1},{1,2},{2,3},{3,0},{4,7},{5,4},{6,5},{7,6},{8,9},{9,10},{10,1... | collective-permute-start | bytes 3538952 | tf_op jit(solution)/shard_map/ppermute | solution.py:510
  64.6 47.0 %collective-permute-start.17 = (bf16[512,2304]{1,0:T(8,128)(2,1)}, bf16[512,2304]{1,0:T(8,128)(2,1)}, u32[]{:S(2)}, u32[]{:S(2)}) collective-permute-start(bf16[512,2304]{1,0:T(8,128)(2,1)} %collective-permute-done.6.refs_9_), channel_id=1, source_target_pairs={{0,4},{4,0},{8,12},{12,8},{16,20},{20,16},{24,28},{28,24},{32,36},... | collective-permute-start | bytes 7077896 | tf_op jit(solution)/shard_map/ppermute | solution.py:514
  64.6 18.8 %collective-permute-start.12 = (bf16[512,256]{1,0:T(8,128)(2,1)}, bf16[512,256]{1,0:T(8,128)(2,1)S(1)}, u32[]{:S(2)}, u32[]{:S(2)}) collective-permute-start(bf16[512,256]{1,0:T(8,128)(2,1)} %get-tuple-element.80), channel_id=1, source_target_pairs={{0,1},{1,2},{2,3},{3,0},{4,5},{5,6},{6,7},{7,4},{8,9},{9,10},{10,1... | collective-permute-start | bytes 786440 | tf_op jit(solution)/shard_map/ppermute | solution.py:501
  66.1 18.1 %collective-permute-start.13 = (bf16[512,256]{1,0:T(8,128)(2,1)}, bf16[512,256]{1,0:T(8,128)(2,1)}, u32[]{:S(2)}, u32[]{:S(2)}) collective-permute-start(bf16[512,256]{1,0:T(8,128)(2,1)} %get-tuple-element.81), channel_id=1, source_target_pairs={{0,3},{1,0},{2,1},{3,2},{4,7},{5,4},{6,5},{7,6},{8,11},{9,8},{10,9... | collective-permute-start | bytes 786440 | tf_op jit(solution)/shard_map/ppermute | solution.py:501
  88.9 35.7 %all-to-all-start = ((bf16[32,256,128]{2,1,0:T(8,128)(2,1)}), bf16[32,256,128]{2,1,0:T(8,128)(2,1)}, u32[]{:S(2)}, u32[]{:S(2)}) async-start(bf16[32,256,128]{2,1,0:T(8,128)(2,1)} %get-tuple-element.105), calls=%async_computation | async-start | bytes 4194304 | tf_op jit(solution)/shard_map/all_to_all | solution.py:595
  94.1 21.8 %collective-permute-start.19 = (bf16[256,2304]{1,0:T(8,128)(2,1)S(1)}, bf16[256,2304]{1,0:T(8,128)(2,1)}, u32[]{:S(2)}, u32[]{:S(2)}) collective-permute-start(bf16[256,2304]{1,0:T(8,128)(2,1)S(1)} %collective-permute-done.18.refs_11_), channel_id=1, source_target_pairs={{0,4},{4,0},{8,12},{12,8},{16,20},{20,16},{24,28},{28,24},{32,36},... | collective-permute-start | bytes 3538952 | tf_op jit(solution)/shard_map/ppermute | solution.py:514
  94.6 9.7 %collective-permute-start.11 = (bf16[512,256]{1,0:T(8,128)(2,1)}, bf16[512,256]{1,0:T(8,128)(2,1)S(1)}, u32[]{:S(2)}, u32[]{:S(2)}) collective-permute-start(bf16[512,256]{1,0:T(8,128)(2,1)} %get-tuple-element.79), channel_id=1, source_target_pairs={{0,2},{1,3},{2,0},{3,1},{4,6},{5,7},{6,4},{7,5},{8,10},{9,11},{10,... | collective-permute-start | bytes 786440 | tf_op jit(solution)/shard_map/ppermute | solution.py:501
  97.4 14.2 %collective-permute-start.14 = (bf16[512,256]{1,0:T(8,128)(2,1)}, bf16[512,256]{1,0:T(8,128)(2,1)S(1)}, u32[]{:S(2)}, u32[]{:S(2)}) collective-permute-start(bf16[512,256]{1,0:T(8,128)(2,1)} %get-tuple-element.98), channel_id=1, source_target_pairs={{0,2},{1,3},{2,0},{3,1},{4,6},{5,7},{6,4},{7,5},{8,10},{9,11},{10,... | collective-permute-start | bytes 786440 | tf_op jit(solution)/shard_map/ppermute | solution.py:501
  97.6 18.3 %collective-permute-start.15 = (bf16[512,256]{1,0:T(8,128)(2,1)}, bf16[512,256]{1,0:T(8,128)(2,1)}, u32[]{:S(2)}, u32[]{:S(2)}) collective-permute-start(bf16[512,256]{1,0:T(8,128)(2,1)} %get-tuple-element.99), channel_id=1, source_target_pairs={{0,1},{1,2},{2,3},{3,0},{4,5},{5,6},{6,7},{7,4},{8,9},{9,10},{10,1... | collective-permute-start | bytes 786440 | tf_op jit(solution)/shard_map/ppermute | solution.py:501
  104.3 11.6 %collective-permute-start.16 = (bf16[512,256]{1,0:T(8,128)(2,1)}, bf16[512,256]{1,0:T(8,128)(2,1)}, u32[]{:S(2)}, u32[]{:S(2)}) collective-permute-start(bf16[512,256]{1,0:T(8,128)(2,1)} %get-tuple-element.100), channel_id=1, source_target_pairs={{0,3},{1,0},{2,1},{3,2},{4,7},{5,4},{6,5},{7,6},{8,11},{9,8},{10,9... | collective-permute-start | bytes 786440 | tf_op jit(solution)/shard_map/ppermute | solution.py:501
  (11 other events, 52.9 us)
Sparse Core Ops, SparseCore 0:
  10.2 54.7 all-gather.1
